TPU v7x, 512 devices: a whole 4x8x8 slice. The times are simulated.
512 devices in a mesh: seq: 64 (over x, z, core), tp: 8 (over y).
Axes of the slice: x: 4, y: 8, z: 8, core: 2. Of those that a mesh axis runs over, the one named last changes fastest.
Arguments:
- query: bfloat16 [65536, 4096], P(('seq', 'tp')), may hold values from -40 to 40, as said below
- keys: bfloat16 [65536, 1024], P(('seq', 'tp')), may hold values from -8 to 8
- values: bfloat16 [65536, 1024], P(('seq', 'tp')), may hold values from -12 to 12
- cotangent: bfloat16 [65536, 4096], P(('seq', 'tp')), may hold values from -158.39192 to 158.39192
- rate: float32 [128, 32], P('seq', 'tp'), may hold values from 0.0001171875 to 7, as said below
- gate_logit: float32 [32], P('tp'), may hold values from -2 to 2
Outputs:
- grad_query: bfloat16 [65536, 4096], P(('seq', 'tp'))
- grad_keys: bfloat16 [65536, 1024], P(('seq', 'tp'))
- grad_values: bfloat16 [65536, 1024], P(('seq', 'tp'))
Inputs may be any that keep to these rules, and one draw needn't show every extreme that they name: `query`: in some draws a few queries are large multiples of earlier keys. `rate`: Positive.
All inputs are finite; a program needn't handle non-finite values.
Results may differ from a plain program's by a relative error of at most 0.0055.
Values may be sent and summed in bfloat16 or wider, within the bound.
No kernel may reach another device: no remote copies, remote signals or barrier semaphores. Data moves between devices by JAX's collectives and lax.ppermute only.
A program may use at most 128 MiB of HBM per device.

v0:
```python
import math

import jax
import jax.numpy as jnp
from jax import lax
from jax.sharding import PartitionSpec as P

HD = 128
SEG = 512


PRECISE = lax.Precision.HIGH


def entering(shard, axis, combine, identity):
    size, here = (lax.axis_size(axis), lax.axis_index(axis))
    everything = jax.tree.map(
        lambda part, kind: lax.all_gather(part.astype(kind), axis),
        shard,
        (jnp.bfloat16, jnp.bfloat16, jnp.bfloat16),
    )
    start = jax.tree.map(
        lambda part, zero: jnp.broadcast_to(jnp.asarray(zero, part.dtype), part.shape),
        shard,
        identity,
    )

    def step(k, before):
        reached = k < here
        new = combine(
            before, jax.tree.map(lambda part, own: part[k].astype(own.dtype), everything, shard)
        )
        return jax.tree.map(lambda a, b: jnp.where(reached, a, b), new, before)

    return lax.fori_loop(0, size, step, start)


def entering_2(part, axis, combine, identity):
    count = lax.axis_size(axis)
    place = lax.axis_index(axis)
    ahead = count - 1 - place
    gathered = jax.tree.map(lambda a: lax.all_gather(a, axis), part)
    state = jax.tree.map(lambda a, e: jnp.zeros_like(a) + jnp.asarray(e, a.dtype), part, identity)

    def one(step, state):
        source = count - 1 - step
        return combine(
            state, jax.tree.map(lambda a: lax.dynamic_index_in_dim(a, source, 0, False), gathered)
        )

    return lax.fori_loop(0, ahead, one, state)


def feature_map(arg_value):
    return jnp.where(arg_value > 0, arg_value + 1.0, jnp.exp(jnp.minimum(arg_value, 0.0)))


def feature_slope(arg_value):
    return jnp.where(arg_value > 0, 1.0, jnp.exp(jnp.minimum(arg_value, 0.0)))


def local_grads(q_seg, k_seg, v_seg, d_seg):
    length, group_size, head_width = q_seg.shape
    row_count = group_size * length
    q_rows = jnp.transpose(q_seg, (1, 0, 2)).reshape(row_count, head_width)
    d_rows = jnp.transpose(d_seg, (1, 0, 2)).reshape(row_count, head_width)
    block_rows = min(512, row_count)
    score_scale = 1.0 / math.sqrt(head_width)
    key_pos = jnp.arange(length, dtype=jnp.int32)

    def local_advance(running, position):
        grad_k, grad_v = running
        offset = position * block_rows
        q_blk = lax.dynamic_slice_in_dim(q_rows, offset, block_rows, 0)
        d_blk = lax.dynamic_slice_in_dim(d_rows, offset, block_rows, 0)
        query_pos = (offset + jnp.arange(block_rows, dtype=jnp.int32)) % length
        visible = key_pos[None, :] <= query_pos[:, None]
        scores = jnp.dot(q_blk, k_seg.T, preferred_element_type=jnp.float32) * score_scale
        scores = jnp.where(visible, scores, -1e30)
        row_max = jnp.max(scores, axis=1, keepdims=True)
        weights = jnp.where(visible, jnp.exp(scores - row_max), 0.0)
        probs = weights / jnp.sum(weights, axis=1, keepdims=True)
        probs_low = probs.astype(jnp.bfloat16)
        grad_p = jnp.dot(d_blk, v_seg.T, preferred_element_type=jnp.float32)
        row_inner = jnp.sum(probs * grad_p, axis=1, keepdims=True)
        grad_s = (probs * (grad_p - row_inner) * score_scale).astype(jnp.bfloat16)
        grad_q = jnp.dot(grad_s, k_seg, preferred_element_type=jnp.float32)
        grad_k = grad_k + jnp.dot(grad_s.T, q_blk, preferred_element_type=jnp.float32)
        grad_v = grad_v + jnp.dot(probs_low.T, d_blk, preferred_element_type=jnp.float32)
        return ((grad_k, grad_v), grad_q)

    empty_grad = jnp.zeros((length, head_width), jnp.float32)
    (grad_k, grad_v), grad_q = lax.scan(
        local_advance,
        (empty_grad, empty_grad),
        jnp.arange(row_count // block_rows, dtype=jnp.int32),
    )
    grad_q = jnp.transpose(grad_q, (1, 0, 2))
    return (grad_q, grad_k, grad_v)


def local_pack(head_inputs):
    return local_grads(head_inputs[0], head_inputs[1], head_inputs[2], head_inputs[3])


def memory_grads(q_seg, d_seg, memory, norm_sum, gates):
    queries32 = q_seg.astype(jnp.float32)
    features = feature_map(queries32)
    numer = jnp.einsum("thc,hcd->thd", features, memory, precision=PRECISE)
    denom = jnp.einsum("thc,hc->th", features, norm_sum, precision=PRECISE) + 1.0
    retrieved = numer / denom[:, :, None]
    mem_cot = gates[None, :, None] * d_seg.astype(jnp.float32)
    num_cot = mem_cot / denom[:, :, None]
    den_cot = -jnp.sum(mem_cot * retrieved, axis=2) / denom
    feat_cot = (
        jnp.einsum("thd,hcd->thc", num_cot, memory, precision=PRECISE)
        + den_cot[:, :, None] * norm_sum[None]
    )
    state_cot = jnp.einsum("thc,thd->hcd", features, num_cot, precision=PRECISE)
    norm_cot = jnp.einsum("thc,th->hc", features, den_cot, precision=PRECISE)
    return (feat_cot * feature_slope(queries32), state_cot, norm_cot)


def lookup_aggregate(seg_pair):
    features = feature_map(seg_pair[0].astype(jnp.float32))
    moments = jnp.einsum(
        "tgc,tgd->gcd", features, seg_pair[1].astype(jnp.float32), precision=PRECISE
    )
    return (moments, jnp.sum(features, axis=0))


def key_grads(k_seg, v_seg, moment_grad, total_grad):
    keys32 = k_seg.astype(jnp.float32)
    features = feature_map(keys32)
    feat_cot = (
        jnp.einsum("tgd,gcd->tgc", v_seg.astype(jnp.float32), moment_grad, precision=PRECISE)
        + total_grad[None]
    )
    extra_v = jnp.einsum("tgc,gcd->tgd", features, moment_grad, precision=PRECISE)
    return (feat_cot * feature_slope(keys32), extra_v)


def finish_keys(seg_inputs):
    k_seg, v_seg, moment_grad, total_grad, grad_k, grad_v = seg_inputs
    extra_k, extra_v = key_grads(k_seg, v_seg, moment_grad, total_grad)
    return ((grad_k + extra_k).astype(jnp.bfloat16), (grad_v + extra_v).astype(jnp.bfloat16))


def segment_grads(q_seg, k_seg, v_seg, d_seg, memory, norm_sum, gates):
    seg_len, head_count, head_width = q_seg.shape
    kv_count = k_seg.shape[1]
    group_size = head_count // kv_count
    local_cot = ((1.0 - gates)[None, :, None] * d_seg.astype(jnp.float32)).astype(jnp.bfloat16)
    grad_q_mem, state_cot, norm_cot = memory_grads(q_seg, d_seg, memory, norm_sum, gates)
    q_groups = jnp.moveaxis(q_seg.reshape(seg_len, kv_count, group_size, head_width), 1, 0)
    c_groups = jnp.moveaxis(local_cot.reshape(seg_len, kv_count, group_size, head_width), 1, 0)
    grad_q, grad_k, grad_v = lax.map(
        local_pack, (q_groups, jnp.moveaxis(k_seg, 1, 0), jnp.moveaxis(v_seg, 1, 0), c_groups)
    )
    grad_q = jnp.moveaxis(grad_q, 0, 1).reshape(seg_len, head_count, head_width) + grad_q_mem
    return (
        grad_q.astype(jnp.bfloat16),
        jnp.moveaxis(grad_k, 0, 1),
        jnp.moveaxis(grad_v, 0, 1),
        state_cot,
        norm_cot,
    )


def chain_forward(start_state, moments, totals, decay, group_size):

    def chain_advance(carried, seg_inputs):
        memory, norm_sum = carried
        moment, total_sum, fading_multiplier = seg_inputs
        next_memory = fading_multiplier[:, None, None] * memory + jnp.repeat(
            moment, group_size, axis=0
        )
        next_norm = fading_multiplier[:, None] * norm_sum + jnp.repeat(
            total_sum, group_size, axis=0
        )
        return ((next_memory, next_norm), (memory, norm_sum))

    return lax.scan(chain_advance, start_state, (moments, totals, decay))


def chain_backward(start_state, state_cots, norm_cots, decay, kv_count):

    def retreat(carried, seg_inputs):
        state_next, norm_next = carried
        state_cot, norm_cot, fading_multiplier = seg_inputs
        head_count, head_width = norm_next.shape
        moment_grad = state_next.reshape(
            kv_count, head_count // kv_count, head_width, head_width
        ).sum(axis=1)
        total_grad = norm_next.reshape(kv_count, head_count // kv_count, head_width).sum(axis=1)
        new_state = (
            state_cot + fading_multiplier[:, None, None] * state_next,
            norm_cot + fading_multiplier[:, None] * norm_next,
        )
        return (new_state, (moment_grad, total_grad))

    return lax.scan(retreat, start_state, (state_cots, norm_cots, decay), reverse=True)


def link_states(earlier, later):
    return (
        earlier[0] * later[0],
        later[0][:, None, None] * earlier[1] + later[1],
        later[0][:, None] * earlier[2] + later[2],
    )


def local(query, keys, values, cotangent, rate, gate_logit):
    q_loc, k_loc, v_loc, d_loc = (
        lax.all_to_all(query, "tp", split_axis=1, concat_axis=0, tiled=True),
        lax.all_to_all(keys, "tp", split_axis=1, concat_axis=0, tiled=True),
        lax.all_to_all(values, "tp", split_axis=1, concat_axis=0, tiled=True),
        lax.all_to_all(cotangent, "tp", split_axis=1, concat_axis=0, tiled=True),
    )
    seg_count, head_count = rate.shape
    tok_count = q_loc.shape[0]
    kv_count = k_loc.shape[1] // HD
    group_size = head_count // kv_count
    q_all = q_loc.reshape(seg_count, SEG, head_count, HD)
    k_all = k_loc.reshape(seg_count, SEG, kv_count, HD)
    v_all = v_loc.reshape(seg_count, SEG, kv_count, HD)
    decay = jnp.exp(-rate)
    moments, totals = lax.map(lookup_aggregate, (k_all, v_all))
    empty_memory = jnp.zeros((head_count, HD, HD), jnp.float32)
    empty_norm = jnp.zeros((head_count, HD), jnp.float32)
    (segment_memory, own_norm), unused_states = chain_forward(
        (empty_memory, empty_norm), moments, totals, decay, group_size
    )
    span_decay = jnp.prod(decay, axis=0)
    identity = (jnp.ones_like(span_decay), empty_memory, empty_norm)
    unused_decay, start_memory, start_norm = entering(
        (span_decay, segment_memory, own_norm), "seq", link_states, identity
    )
    last_state, (states, norms) = chain_forward(
        (start_memory, start_norm), moments, totals, decay, group_size
    )
    d_all = d_loc.reshape(seg_count, SEG, head_count, HD)
    gates = jax.nn.sigmoid(gate_logit)

    def per_segment(seg_inputs):
        return segment_grads(
            seg_inputs[0],
            seg_inputs[1],
            seg_inputs[2],
            seg_inputs[3],
            seg_inputs[4],
            seg_inputs[5],
            gates,
        )

    grad_query, resident_lookup_vectors, local_v, state_cots, norm_cots = lax.map(
        per_segment, (q_all, k_all, v_all, d_all, states, norms)
    )
    (own_state_cot, own_norm_cot), unused_grads = chain_backward(
        (empty_memory, empty_norm), state_cots, norm_cots, decay, kv_count
    )
    unused_span, later_state, later_norm = entering_2(
        (span_decay, own_state_cot, own_norm_cot), "seq", link_states, identity
    )
    first_state, (moment_grads, total_grads) = chain_backward(
        (later_state, later_norm), state_cots, norm_cots, decay, kv_count
    )
    grad_keys, grad_values = lax.map(
        finish_keys, (k_all, v_all, moment_grads, total_grads, resident_lookup_vectors, local_v)
    )
    return (
        lax.all_to_all(
            grad_query.reshape(tok_count, head_count * HD),
            "tp",
            split_axis=0,
            concat_axis=1,
            tiled=True,
        ),
        lax.all_to_all(
            grad_keys.reshape(tok_count, kv_count * HD),
            "tp",
            split_axis=0,
            concat_axis=1,
            tiled=True,
        ),
        lax.all_to_all(
            grad_values.reshape(tok_count, kv_count * HD),
            "tp",
            split_axis=0,
            concat_axis=1,
            tiled=True,
        ),
    )


def solution(mesh):
    in_specs = (
        P(("seq", "tp"), None),
        P(("seq", "tp"), None),
        P(("seq", "tp"), None),
        P(("seq", "tp"), None),
        P("seq", "tp"),
        P("tp"),
    )
    out_specs = (P(("seq", "tp"), None), P(("seq", "tp"), None), P(("seq", "tp"), None))
    return jax.shard_map(local, mesh=mesh, in_specs=in_specs, out_specs=out_specs, check_vma=False)
```

profile of v0, /device:TPU:1, one launch (start us, length us, event | category | flops | bytes accessed | tf_op | source)
XLA Modules:
  0.0 752.2 jit_solution(2883080311310516691)
XLA Ops:
  7.2 1.9 copy.83
  9.1 7.7 %all-to-all-start.2 = ((bf16[128,8,128]{0,2,1:T(8,128)(2,1)}), bf16[128,8,128]{0,2,1:T(8,128)(2,1)S(1)}, u32[]{:S(2)}, u32[]{:S(2)}) async-start(bf16[128,8,128]{0,2,1:T(8,128)(2,1)} %bitcast.58), calls=%async_computation.2 | async-start | bytes 524288 | tf_op jit(solution)/shard_map/all_to_all | solution.py:216
  16.7 1.8 copy.85
  18.5 7.6 %all-to-all-done.2 = bf16[128,8,128]{0,2,1:T(8,128)(2,1)S(1)} async-done(((bf16[128,8,128]{0,2,1:T(8,128)(2,1)}), bf16[128,8,128]{0,2,1:T(8,128)(2,1)S(1)}, u32[]{:S(2)}, u32[]{:S(2)}) %all-to-all-start.2) | async-done | bytes 262176 | tf_op jit(solution)/shard_map/all_to_all | solution.py:216
  26.1 3.4 all-to-all-start.3
  31.2 7.8 %all-to-all-done.3 = bf16[128,8,128]{0,2,1:T(8,128)(2,1)S(1)} async-done(((bf16[128,8,128]{0,2,1:T(8,128)(2,1)}), bf16[128,8,128]{0,2,1:T(8,128)(2,1)S(1)}, u32[]{:S(2)}, u32[]{:S(2)}) %all-to-all-start.3) | async-done | bytes 262176 | tf_op jit(solution)/shard_map/all_to_all | solution.py:217
  39.8 5.6 while.183
  46.6 2.3 copy.144
  48.9 3.6 all-to-all-start
  53.6 24.1 %all-to-all-done = bf16[128,8,512]{2,0,1:T(8,128)(2,1)S(1)} async-done(((bf16[128,8,512]{2,0,1:T(8,128)(2,1)}), bf16[128,8,512]{2,0,1:T(8,128)(2,1)S(1)}, u32[]{:S(2)}, u32[]{:S(2)}) %all-to-all-start) | async-done | bytes 1048608 | tf_op jit(solution)/shard_map/all_to_all | solution.py:215
  77.7 3.6 all-to-all-start.1
  83.7 135.8 %all-reduce = bf16[256]{0:T(256)(128)(2,1)S(1)} all-reduce(bf16[256]{0:T(256)(128)(2,1)S(1)} %dynamic-update-slice), channel_id=7, replica_groups=mesh['seq'=64,'tp'=8] {'seq'}, use_global_device_ids=true, to_apply=%add | all-reduce | flops 256 | bytes 1024
  220.2 42.4 %all-gather.6 = bf16[64,4,128]{2,1,0:T(4,128)(2,1)S(1)} all-gather(bf16[1,4,128]{2,1,0:T(4,128)(2,1)S(1)} %convert_bitcast_fusion), channel_id=3, replica_groups=mesh['seq'=64,'tp'=8] {'seq'}, dimensions={0}, use_global_device_ids=true | all-gather | bytes 66560 | tf_op jit(solution)/shard_map/all_gather | solution.py:18
  264.8 70.6 %while.191 = (s32[]{:T(128)}, f32[4,128,128]{2,1,0:T(8,128)S(1)}, f32[4,128]{1,0:T(4,128)S(1)}, s32[]{:T(128)}, bf16[64,4]{1,0:T(8,128)(2,1)S(1)}, /*index=5*/bf...) while((s32[]{:T(128)}, f32[4,128,128]{2,1,0:T(8,128)S(1)}, ...), condition=%wide.region_7.8_spmd.clone, body=%wide.region_6.7_spmd.clone.sunk | while | flops 330248 | bytes 660663 | solution.py:35
  336.3 2.0 while.184
  339.7 98.7 %while.186 = (s32[]{:T(128)}, bf16[2,512,4,128]{3,2,1,0:T(4,128)(2,1)}, f32[2,512,1,128]{3,1,2,0:T(8,128)}, f32[2,512,1,128]{3,1,2,0:T(8,128)}, f32[2,4,128,128]...) while((s32[]{:T(128)}, ...), condition=%wide.region_17.18_spmd, body=%wide.region_10.17_spmd.sunk | while | flops 961292800 | bytes 33087700 | solution.py:256
  344.4 1.6 dynamic-slice_bitcast_fusion.10
  347.5 30.2 %while.193 = (s32[]{:T(128)}, f32[512,128]{1,0:T(8,128)S(1)}, f32[512,128]{1,0:T(8,128)}, f32[4,512,128]{1,2,0:T(8,128)}, s32[4]{0:T(128)}, /*index=5*/bf16[2048...) while((s32[]{:T(128)}, f32[512,128]{1,0:T(8,128)S(1)}, ...), condition=%wide.region_15.15_spmd.clone, body=%wide.region_11.14_spmd.clone.sunk | while | flops 342888960 | bytes 11176662 | solution.py:93
  352.6 2.0 convolution_add_fusion.5
  360.1 2.1 convolution_add_fusion.5
  367.7 2.1 convolution_add_fusion.5
  375.2 2.1 convolution_add_fusion.5
  377.7 1.9 bitcast_dynamic-update-slice_fusion.11
  380.5 1.8 fusion.208
  382.4 2.3 fusion.209
  386.7 1.5 fusion.210
  393.8 1.6 dynamic-slice_bitcast_fusion.10
  396.9 30.2 %while.193 = (s32[]{:T(128)}, f32[512,128]{1,0:T(8,128)S(1)}, f32[512,128]{1,0:T(8,128)}, f32[4,512,128]{1,2,0:T(8,128)}, s32[4]{0:T(128)}, /*index=5*/bf16[2048...) while((s32[]{:T(128)}, f32[512,128]{1,0:T(8,128)S(1)}, ...), condition=%wide.region_15.15_spmd.clone, body=%wide.region_11.14_spmd.clone.sunk | while | flops 342888960 | bytes 11176662 | solution.py:93
  402.0 2.0 convolution_add_fusion.5
  409.5 2.1 convolution_add_fusion.5
  417.0 2.1 convolution_add_fusion.5
  424.6 2.1 convolution_add_fusion.5
  427.1 1.9 bitcast_dynamic-update-slice_fusion.11
  429.9 1.8 fusion.208
  431.7 2.3 fusion.209
  438.5 7.8 %while.192 = (s32[]{:T(128)}, f32[4,128,128]{2,1,0:T(8,128)}, f32[4,128]{1,0:T(4,128)}, f32[2,4,128,128]{3,2,1,0:T(8,128)}, f32[2,4]{1,0:T(2,128)}, /*index=5*/f32[2,4,128]{2,1,0:T(4,128)}, s32[]{:T(128)}, s32[]{:T(128)}) while((s32[]{:T(128)}, f32[4,128,128]{2,1,0:T(8,128)}, f32[4,128]{1,0:T(4,128)}, ...), condition=%wide.region_19.20_spmd.clone, body=%wide.region_18.19_spmd.clone.sunk | while | flops 198148 | bytes 792760 | solution.py:202
  439.3 1.8 bitcast_add_fusion.13
  443.1 1.9 bitcast_add_fusion.13
  447.2 124.6 %all-reduce.1 = f32[256]{0:T(256)S(1)} all-reduce(f32[256]{0:T(256)S(1)} %dynamic-update-slice.1), channel_id=4, replica_groups=mesh['seq'=64,'tp'=8] {'seq'}, use_global_device_ids=true, to_apply=%add.1 | all-reduce | flops 256 | bytes 2048
  571.9 2.3 all_to_all.102
  574.2 6.5 all-to-all-start.4
  580.7 50.3 %all-gather.7 = f32[64,4,128]{2,1,0:T(4,128)S(1)} all-gather(f32[1,4,128]{2,1,0:T(4,128)} %bitcast.434), channel_id=6, replica_groups=mesh['seq'=64,'tp'=8] {'seq'}, dimensions={0}, use_global_device_ids=true | all-gather | bytes 133120 | tf_op jit(solution)/shard_map/all_gather | solution.py:42
  631.1 71.2 %while.187 = (s32[]{:T(128)}, f32[4,128,128]{2,1,0:T(8,128)S(1)}, f32[4,128]{1,0:T(4,128)S(1)}, s32[]{:T(128)}, f32[64,4]{1,0:T(8,128)S(1)}, /*index=5*/f32[64,4...) while((s32[]{:T(128)}, f32[4,128,128]{2,1,0:T(8,128)S(1)}, ...), condition=%wide.region_21.22_spmd, body=%wide.region_20.21_spmd.sunk | while | flops 132102 | bytes 792807 | solution.py:51
  702.3 5.1 while.188
  707.4 7.6 %while.189 = (s32[]{:T(128)}, bf16[2,512,1,128]{3,1,0,2:T(8,128)(2,1)S(1)}, bf16[2,512,1,128]{3,1,0,2:T(8,128)(2,1)}, f32[2,512,1,128]{3,1,2,0:T(8,128)S(1)}, f3...) while((s32[]{:T(128)}, ...), condition=%wide.region_27.28_spmd, body=%wide.region_26.27_spmd.sunk | while | flops 101646336 | bytes 4983929 | solution.py:268
  715.0 16.5 %all_to_all.121 = bf16[8,128,128]{2,1,0:T(8,128)(2,1)S(1)} all-to-all(bf16[8,128,128]{2,1,0:T(8,128)(2,1)S(1)} %bitcast.431), channel_id=1, replica_groups=mesh['seq'=64,'tp'=8] {'tp'}, dimensions={0} | all-to-all | bytes 524288 | tf_op jit(solution)/shard_map/all_to_all | solution.py:279
  731.5 3.4 all-to-all-start.6
  738.0 6.3 all-to-all-done.6
  (638 shorter events, 242.7 us)
Async XLA Ops:
  7.2 45.3 %copy-start.4 = (bf16[128,4096]{1,0:T(8,128)(2,1)S(1)}, bf16[128,4096]{1,0:T(8,128)(2,1)}, u32[]{:S(2)}) copy-start(bf16[128,4096]{1,0:T(8,128)(2,1)} %param.29) | copy-start | bytes 3145732
  7.2 212.4 %copy-start.9 = (f32[4]{0:T(128)S(1)}, f32[4]{0:T(128)}, u32[]{:S(2)}) copy-start(f32[4]{0:T(128)} %param.31) | copy-start | bytes 52
  9.1 17.1 %all-to-all-start.2 = ((bf16[128,8,128]{0,2,1:T(8,128)(2,1)}), bf16[128,8,128]{0,2,1:T(8,128)(2,1)S(1)}, u32[]{:S(2)}, u32[]{:S(2)}) async-start(bf16[128,8,128]{0,2,1:T(8,128)(2,1)} %bitcast.58), calls=%async_computation.2 | async-start | bytes 524288 | tf_op jit(solution)/shard_map/all_to_all | solution.py:216
  26.1 12.8 %all-to-all-start.3 = ((bf16[128,8,128]{0,2,1:T(8,128)(2,1)}), bf16[128,8,128]{0,2,1:T(8,128)(2,1)S(1)}, u32[]{:S(2)}, u32[]{:S(2)}) async-start(bf16[128,8,128]{0,2,1:T(8,128)(2,1)} %bitcast.62), calls=%async_computation.3 | async-start | bytes 524288 | tf_op jit(solution)/shard_map/all_to_all | solution.py:217
  29.5 235.3 %all-gather.11.cloned.1.call-start = ((), (), s32[]{:S(2)}) async-start(), calls=%async_computation.7 | async-start | bytes 8519680 | tf_op jit(solution)/shard_map/all_gather | solution.py:18
  30.3 189.8 %copy-start.8 = (f32[4]{0:T(128)}, f32[4]{0:T(128)S(1)}, u32[]{:S(2)}) copy-start(f32[4]{0:T(128)S(1)} %get-tuple-element.1419) | copy-start | bytes 52
  48.9 28.8 %all-to-all-start = ((bf16[128,8,512]{2,0,1:T(8,128)(2,1)}), bf16[128,8,512]{2,0,1:T(8,128)(2,1)S(1)}, u32[]{:S(2)}, u32[]{:S(2)}) async-start(bf16[128,8,512]{2,0,1:T(8,128)(2,1)} %bitcast.264), calls=%async_computation | async-start | bytes 2097152 | tf_op jit(solution)/shard_map/all_to_all | solution.py:215
  77.7 186.0 %all-to-all-start.1 = ((bf16[128,8,512]{2,0,1:T(8,128)(2,1)}), bf16[128,8,512]{2,0,1:T(8,128)(2,1)S(1)}, u32[]{:S(2)}, u32[]{:S(2)}) async-start(bf16[128,8,512]{2,0,1:T(8,128)(2,1)} %bitcast.263), calls=%async_computation.1 | async-start | bytes 2097152 | tf_op jit(solution)/shard_map/all_to_all | solution.py:218
  81.3 549.8 %all-gather.13.cloned.1.call-start = ((), (), s32[]{:S(2)}) async-start(), calls=%async_computation.8 | async-start | bytes 17039360 | tf_op jit(solution)/shard_map/all_gather | solution.py:42
  338.3 1.5 copy-start.7
  377.7 9.0 %copy-start.5 = (f32[2,4,128]{2,1,0:T(4,128)S(1)}, f32[2,4,128]{2,1,0:T(4,128)}, u32[]{:S(2)}) copy-start(f32[2,4,128]{2,1,0:T(4,128)} %get-tuple-element.2111) | copy-start | bytes 12292 | tf_op jit(solution)/shard_map/while
  377.7 9.0 %copy-start = (f32[2,4,128,128]{3,2,1,0:T(8,128)S(1)}, f32[2,4,128,128]{3,2,1,0:T(8,128)}, u32[]{:S(2)}) copy-start(f32[2,4,128,128]{3,2,1,0:T(8,128)} %get-tuple-element.2110) | copy-start | bytes 1572868 | tf_op jit(solution)/shard_map/while
  386.7 1.6 copy-start.6
  388.3 0.8 copy-start.1
  427.1 9.0 %copy-start.5 = (f32[2,4,128]{2,1,0:T(4,128)S(1)}, f32[2,4,128]{2,1,0:T(4,128)}, u32[]{:S(2)}) copy-start(f32[2,4,128]{2,1,0:T(4,128)} %get-tuple-element.2111) | copy-start | bytes 12292 | tf_op jit(solution)/shard_map/while
  427.1 9.0 %copy-start = (f32[2,4,128,128]{3,2,1,0:T(8,128)S(1)}, f32[2,4,128,128]{3,2,1,0:T(8,128)}, u32[]{:S(2)}) copy-start(f32[2,4,128,128]{3,2,1,0:T(8,128)} %get-tuple-element.2110) | copy-start | bytes 1572868 | tf_op jit(solution)/shard_map/while
  436.1 1.6 copy-start.6
  437.6 0.8 copy-start.1
  438.5 268.9 %copy-start.2 = (f32[2,512,1,128]{3,1,2,0:T(8,128)S(1)}, f32[2,512,1,128]{3,1,2,0:T(8,128)}, u32[]{:S(2)}) copy-start(f32[2,512,1,128]{3,1,2,0:T(8,128)} %get-tuple-element.2231) | copy-start | bytes 1572868
  438.5 268.9 %copy-start.3 = (f32[2,512,1,128]{3,1,2,0:T(8,128)S(1)}, f32[2,512,1,128]{3,1,2,0:T(8,128)}, u32[]{:S(2)}) copy-start(f32[2,512,1,128]{3,1,2,0:T(8,128)} %get-tuple-element.2236) | copy-start | bytes 1572868
  574.2 140.8 %all-to-all-start.4 = ((bf16[8,128,512]{2,1,0:T(8,128)(2,1)}), bf16[8,128,512]{2,1,0:T(8,128)(2,1)S(1)}, u32[]{:S(2)}, u32[]{:S(2)}) async-start(bf16[8,128,512]{2,1,0:T(8,128)(2,1)} %all_to_all.102), calls=%async_computation.4 | async-start | bytes 2097152 | tf_op jit(solution)/shard_map/all_to_all | solution.py:272
  731.5 12.8 %all-to-all-start.6 = ((bf16[8,128,128]{2,1,0:T(8,128)(2,1)}), bf16[8,128,128]{2,1,0:T(8,128)(2,1)S(1)}, u32[]{:S(2)}, u32[]{:S(2)}) async-start(bf16[8,128,128]{2,1,0:T(8,128)(2,1)} %bitcast.78), calls=%async_computation.6 | async-start | bytes 524288 | tf_op jit(solution)/shard_map/all_to_all | solution.py:286
Sparse Core Ops, SparseCore 0:
  46.7 93.4 all-gather.10
  446.4 103.4 all-gather.12
where the time goes:
time: 759 us; the launch traced here: 752 us
  blocking collectives  370 us (49%)
  other arithmetic  162 us (21%)
  local copies, waits for them, and re-layouts  65.8 us (9%)
  matrix products  60 us (8%)
  waiting for transfers between devices  45.9 us (6%)
  starting transfers between devices  28.2 us (4%)
  between operations  15 us (2%)
    unnamed x2, blocking collectives  260 us
    select_n x128, other arithmetic, step(): return jax.tree.map(lambda a, b: jnp.where(reached, a, b), new, before)  69.9 us
    add x62, other arithmetic, link_states(): later[0][:, None, None] * earlier[1] + later[1]  65.4 us
    all_gather x1, blocking collectives, entering_2(): gathered = jax.tree.map(lambda a: lax.all_gather(a, axis), part)  50.3 us
    all_gather x1, blocking collectives, entering(): lax.all_gather(part.astype(kind), axis)  42.4 us
    all_to_all x1, waiting for transfers between devices, local(): lax.all_to_all(query, 'tp', split_axis=1, concat_axis=0, tiled=True)  24.1 us
    dot_general x8, matrix products, local_advance(): jnp.dot(probs_low.T, d_blk, preferred_element_type=jnp.float32)  16.8 us
    all_to_all x1, blocking collectives, local(): lax.all_to_all(grad_keys.reshape(tok_count, kv_count * HD), 'tp', split_a...  16.5 us
  transfers between devices with their start and end apart: 8, of which 4 were waited for; matrix products, arithmetic and copies ran while one was open for 13% of the time, Pallas kernels for 0%

commit v1 on v0

v1 whole, which is shorter than its diff:
```python
import functools
import math

import jax
import jax.numpy as jnp
from jax import lax
from jax.experimental import pallas as pl
from jax.experimental.pallas import tpu as pltpu
from jax.sharding import PartitionSpec as P

HD = 128
SEG = 512
HALF = 64
BLK = 256
F32 = jnp.float32
BF16 = jnp.bfloat16
SCALE = 1.0 / math.sqrt(HD)
LOG2E = 1.4426950408889634
EXACT = lax.Precision.HIGHEST
VMEM = pltpu.VMEM
SMEM = pltpu.SMEM
NN = (((1,), (0,)), ((), ()))
NT = (((1,), (1,)), ((), ()))
TN = (((0,), (0,)), ((), ()))


def mm(a, b, dims, precision=None):
    return lax.dot_general(a, b, dims, precision=precision, preferred_element_type=F32)


def split(a):
    hi = a.astype(BF16)
    return hi, (a - hi.astype(F32)).astype(BF16)


def mm3(a, b, dims):
    ah, al = a if isinstance(a, tuple) else split(a)
    bh, bl = b if isinstance(b, tuple) else split(b)
    return mm(ah, bh, dims) + (mm(al, bh, dims) + mm(ah, bl, dims))


def mm2(a, b, dims):
    ah, al = split(a)
    return mm(ah, b, dims) + mm(al, b, dims)


def features_of(x):
    slope = jnp.exp(jnp.minimum(x, 0.0))
    return slope + jnp.maximum(x, 0.0), slope


def params(mib):
    return pltpu.CompilerParams(vmem_limit_bytes=mib << 20)


def cost(flops, size, exps=0):
    return pl.CostEstimate(flops=flops, bytes_accessed=size, transcendentals=exps)


def moments_kernel(kv_ref, rate_ref, out_ref, moment_ref, total_ref):
    for e in range(2):
        rows = pl.ds(e * SEG, SEG)
        sk, _ = features_of(kv_ref[rows, :HD].astype(F32))
        moment = mm2(sk, kv_ref[rows, HD:], TN)
        total = jnp.sum(sk, axis=0, keepdims=True)
        out_ref[:, 2 * e, :] = moment[:HALF]
        out_ref[:, 2 * e + 1, :] = moment[HALF:]
        out_ref[:, 4 + e, :] = jnp.broadcast_to(total, (HALF, HD))
        if e == 0:
            moment_ref[...] = moment
            total_ref[...] = jnp.broadcast_to(total, (8, HD))
    out_ref[:, 6, :] = jnp.broadcast_to(rate_ref[...], (HALF, HD))
    out_ref[:, 7, :] = jnp.zeros((HALF, HD), F32)


def moments_call(kv, rate_row):
    return pl.pallas_call(
        moments_kernel,
        out_shape=(
            jax.ShapeDtypeStruct((HALF, 8, HD), F32),
            jax.ShapeDtypeStruct((HD, HD), F32),
            jax.ShapeDtypeStruct((8, HD), F32),
        ),
        compiler_params=params(16),
        cost_estimate=cost(2 * 2 * SEG * HD * HD * 2, 1 << 20, 2 * SEG * HD),
        name="moments",
    )(kv, rate_row)


def cumulative(rates):
    rows = lax.broadcasted_iota(jnp.int32, (HALF, HALF), 0)
    cols = lax.broadcasted_iota(jnp.int32, (HALF, HALF), 1)
    upto = (cols <= rows).astype(F32)
    before = (cols < rows).astype(F32)
    same = (cols == rows).astype(F32)
    upto_t = (rows <= cols).astype(F32)
    before_t = (rows < cols).astype(F32)
    return dict(
        inc_col=mm(upto, rates, NN, EXACT),
        exc_col=mm(before, rates, NN, EXACT),
        inc_row=mm(rates, upto_t, TN, EXACT),
        exc_row=mm(rates, before_t, TN, EXACT),
        row=mm(rates, same, TN, EXACT),
        rows=rows,
        cols=cols,
    )


def pair_col(a, h):
    return a[:, h : h + 1] + a[:, 4 + h : 5 + h]


def pair_row(a, h):
    return a[h : h + 1, :] + a[4 + h : 5 + h, :]


def forward_kernel(me_ref, in_ref, out_ref, norm_ref):
    c = cumulative(in_ref[:, 6, :])
    earlier = c["cols"] < c["rows"]
    x0 = jnp.concatenate([in_ref[:, 0, :], in_ref[:, 1, :], in_ref[:, 4, :]], axis=1)
    x1 = jnp.concatenate([in_ref[:, 2, :], in_ref[:, 3, :], in_ref[:, 5, :]], axis=1)
    mine = lax.broadcasted_iota(jnp.int32, (HALF, HD), 0) == me_ref[0]
    for h in range(4):
        gap = pair_col(c["exc_col"], h) - pair_row(c["inc_row"], h)
        second = jnp.exp(jnp.where(earlier, -gap, -1e30))
        first = second * jnp.exp(-c["row"][4 + h : 5 + h, :])
        state = mm(first, x0, NN, EXACT) + mm(second, x1, NN, EXACT)
        out_ref[:, 2 * h, :] = state[:, :HD]
        out_ref[:, 2 * h + 1, :] = state[:, HD : 2 * HD]
        own = jnp.sum(jnp.where(mine, state[:, 2 * HD :], 0.0), axis=0, keepdims=True)
        norm_ref[2 * h : 2 * h + 2, :] = jnp.broadcast_to(own, (2, HD))


def forward_call(me, recv):
    return pl.pallas_call(
        forward_kernel,
        in_specs=[pl.BlockSpec(memory_space=SMEM), pl.BlockSpec(memory_space=VMEM)],
        out_shape=(
            jax.ShapeDtypeStruct((HALF, 8, HD), F32),
            jax.ShapeDtypeStruct((8, HD), F32),
        ),
        compiler_params=params(16),
        cost_estimate=cost(4 * 2 * 64 * 128 * 384 * 6, 1 << 20, 4 * 8192),
        name="forward_scan",
    )(me, recv)


def attention_kernel(gate_ref, q_ref, d_ref, k_ref, v_ref, gq_ref, gk_ref, gv_ref):
    h = pl.program_id(1)
    rest = 1.0 - gate_ref[h]
    local_cot = (rest * d_ref[...].astype(F32)).astype(BF16)
    u_pos = lax.broadcasted_iota(jnp.int32, (BLK, BLK), 0)
    t_pos = lax.broadcasted_iota(jnp.int32, (BLK, BLK), 1)
    visible = u_pos <= t_pos
    nb = SEG // BLK
    ks = [k_ref[pl.ds(i * BLK, BLK), :] for i in range(nb)]
    vs = [v_ref[pl.ds(i * BLK, BLK), :] for i in range(nb)]
    grad_k = [None] * nb
    grad_v = [None] * nb

    def plus(a, b):
        return b if a is None else a + b

    for tb in range(nb):
        q = q_ref[pl.ds(tb * BLK, BLK), :]
        lc = local_cot[tb * BLK : (tb + 1) * BLK]
        s = [mm(ks[u], q, NT) for u in range(tb + 1)]
        s[tb] = jnp.where(visible, s[tb], -1e30)
        top = functools.reduce(jnp.maximum, [jnp.max(a, axis=0, keepdims=True) for a in s])
        w = [jnp.exp2((a - top) * (SCALE * LOG2E)) for a in s]
        total = sum(jnp.sum(a, axis=0, keepdims=True) for a in w)
        inv = 1.0 / total
        p = [a * inv for a in w]
        gp = [mm(vs[u], lc, NT) for u in range(tb + 1)]
        inner = sum(jnp.sum(a * b, axis=0, keepdims=True) for a, b in zip(p, gp))
        gs = [(a * (b - inner) * SCALE).astype(BF16) for a, b in zip(p, gp)]
        gq_t = None
        for u in range(tb + 1):
            gq_t = plus(gq_t, mm(ks[u], gs[u], TN))
            grad_k[u] = plus(grad_k[u], mm(gs[u], q, NN))
            grad_v[u] = plus(grad_v[u], mm(p[u].astype(BF16), lc, NN))
        gq_ref[pl.ds(tb * BLK, BLK), :] = gq_t.T

    @pl.when(h == 0)
    def _():
        for u in range(nb):
            gk_ref[pl.ds(u * BLK, BLK), :] = grad_k[u]
            gv_ref[pl.ds(u * BLK, BLK), :] = grad_v[u]

    @pl.when(h > 0)
    def _():
        for u in range(nb):
            gk_ref[pl.ds(u * BLK, BLK), :] += grad_k[u]
            gv_ref[pl.ds(u * BLK, BLK), :] += grad_v[u]


def attention_call(gates, q, d, kv):
    head = pl.BlockSpec((SEG, HD), lambda s, h: (s, h))
    return pl.pallas_call(
        attention_kernel,
        grid=(2, 4),
        in_specs=[
            pl.BlockSpec(memory_space=SMEM),
            head,
            head,
            pl.BlockSpec((SEG, HD), lambda s, h: (s, 0)),
            pl.BlockSpec((SEG, HD), lambda s, h: (s, 1)),
        ],
        out_specs=[
            head,
            pl.BlockSpec((SEG, HD), lambda s, h: (s, 0)),
            pl.BlockSpec((SEG, HD), lambda s, h: (s, 0)),
        ],
        out_shape=(
            jax.ShapeDtypeStruct((2 * SEG, 4 * HD), F32),
            jax.ShapeDtypeStruct((2 * SEG, HD), F32),
            jax.ShapeDtypeStruct((2 * SEG, HD), F32),
        ),
        compiler_params=params(32),
        cost_estimate=cost(8 * 5 * 2 * SEG * SEG * HD, 6 << 20, 8 * SEG * SEG),
        name="attention",
    )(gates, q, d, kv, kv)


def memory_kernel(
    gate_ref, rate_ref, q_ref, d_ref, local_ref, state_ref, norm_ref, moment_ref, total_ref,
    gq_ref, send_ref, later_ref, later_norm_ref, rows_ref,
):
    later = None
    later_norm = None
    for h in range(4):
        cols = pl.ds(h * HD, HD)
        gate = gate_ref[h]
        decay = jnp.exp(jnp.full((1, HD), -rate_ref[0, h], F32))
        memory = jnp.concatenate([state_ref[:, 2 * h, :], state_ref[:, 2 * h + 1, :]], axis=0)
        norm = norm_ref[2 * h : 2 * h + 1, :]
        cots = []
        for e in range(2):
            if e == 1:
                memory = decay * memory + moment_ref[...]
                norm = decay * norm + total_ref[0:1, :]
            rows = pl.ds(e * SEG, SEG)
            sq, slope = features_of(q_ref[rows, cols].astype(F32))
            sq_low = sq.astype(BF16)
            memory_low = memory.astype(BF16)
            numer = mm(sq_low, memory_low, NN)
            denom = jnp.sum(sq * norm, axis=1, keepdims=True) + 1.0
            inv = 1.0 / denom
            num_cot = (gate * d_ref[rows, cols].astype(F32)) * inv
            den_cot = -jnp.sum(num_cot * numer, axis=1, keepdims=True) * inv
            num_low = num_cot.astype(BF16)
            feat_cot = mm(num_low, memory_low, NT) + den_cot * norm
            gq_ref[rows, cols] = (local_ref[rows, cols] + feat_cot * slope).astype(BF16)
            cots.append((mm(sq_low, num_low, TN), jnp.sum(sq * den_cot, axis=0, keepdims=True)))
        own = cots[0][0] + decay * cots[1][0]
        own_norm = cots[0][1] + decay * cots[1][1]
        rows_ref[:, 2 * h, :] = own[:HALF]
        rows_ref[:, 2 * h + 1, :] = own[HALF:]
        upper = own_norm.astype(BF16).astype(F32)
        rows_ref[:, 8 + h, :] = jnp.broadcast_to(upper, (HALF, HD))
        rows_ref[:, 12 + h, :] = jnp.broadcast_to(own_norm - upper, (HALF, HD))
        later = cots[1][0] if later is None else later + cots[1][0]
        later_norm = cots[1][1] if later_norm is None else later_norm + cots[1][1]
    send_ref[...] = rows_ref[...].astype(BF16)
    later_ref[...] = later
    later_norm_ref[...] = jnp.broadcast_to(later_norm, (8, HD))


def memory_call(gates, rate, q, d, local, state, norm, moment, total):
    return pl.pallas_call(
        memory_kernel,
        in_specs=[pl.BlockSpec(memory_space=SMEM)] * 2 + [pl.BlockSpec(memory_space=VMEM)] * 7,
        out_shape=(
            jax.ShapeDtypeStruct((2 * SEG, 4 * HD), BF16),
            jax.ShapeDtypeStruct((HALF, 16, HD), BF16),
            jax.ShapeDtypeStruct((HD, HD), F32),
            jax.ShapeDtypeStruct((8, HD), F32),
        ),
        scratch_shapes=[pltpu.VMEM((HALF, 16, HD), F32)],
        compiler_params=params(32),
        cost_estimate=cost(8 * 3 * 2 * SEG * HD * HD, 6 << 20, 8 * SEG * HD),
        name="memory",
    )(gates, rate, q, d, local, state, norm, moment, total)


def backward_kernel(me_ref, first_ref, in_ref, out_ref, norm_ref, rows_ref):
    c = cumulative(first_ref[:, 6, :])
    rows_ref[...] = in_ref[...].astype(F32)
    after = c["cols"] > c["rows"]
    mine = lax.broadcasted_iota(jnp.int32, (HALF, HD), 0) == me_ref[0]
    one = zero = None
    for h in range(4):
        gap = pair_row(c["exc_row"], h) - pair_col(c["inc_col"], h)
        weight = jnp.exp(jnp.where(after, -gap, -1e30))
        own = jnp.concatenate(
            [
                rows_ref[:, 2 * h, :],
                rows_ref[:, 2 * h + 1, :],
                rows_ref[:, 8 + h, :] + rows_ref[:, 12 + h, :],
            ],
            axis=1,
        )
        carried = mm(weight, own, NN, EXACT)
        earlier = jnp.exp(-first_ref[:, 6, 4 + h : 5 + h]) * carried
        one = carried if one is None else one + carried
        zero = earlier if zero is None else zero + earlier
    for e, value in ((0, zero), (1, one)):
        out_ref[:, 2 * e, :] = value[:, :HD]
        out_ref[:, 2 * e + 1, :] = value[:, HD : 2 * HD]
        own = jnp.sum(jnp.where(mine, value[:, 2 * HD :], 0.0), axis=0, keepdims=True)
        norm_ref[4 * e : 4 * e + 4, :] = jnp.broadcast_to(own, (4, HD))


def backward_call(me, first, recv):
    return pl.pallas_call(
        backward_kernel,
        in_specs=[pl.BlockSpec(memory_space=SMEM)] + [pl.BlockSpec(memory_space=VMEM)] * 2,
        out_shape=(
            jax.ShapeDtypeStruct((HALF, 4, HD), F32),
            jax.ShapeDtypeStruct((8, HD), F32),
        ),
        scratch_shapes=[pltpu.VMEM((HALF, 16, HD), F32)],
        compiler_params=params(16),
        cost_estimate=cost(4 * 2 * 64 * 64 * 384 * 6, 1 << 20, 4 * 4096),
        name="backward_scan",
    )(me, first, recv)


def finish_kernel(kv_ref, cot_ref, norm_ref, later_ref, later_norm_ref, gk_ref, gv_ref, out_ref):
    for e in range(2):
        rows = pl.ds(e * SEG, SEG)
        moment_cot = jnp.concatenate([cot_ref[:, 2 * e, :], cot_ref[:, 2 * e + 1, :]], axis=0)
        total_cot = norm_ref[4 * e : 4 * e + 1, :]
        if e == 0:
            moment_cot = moment_cot + later_ref[...]
            total_cot = total_cot + later_norm_ref[0:1, :]
        sk, slope = features_of(kv_ref[rows, :HD].astype(F32))
        high, low = split(moment_cot)
        values = kv_ref[rows, HD:]
        feat_cot = mm(values, high, NT) + mm(values, low, NT) + total_cot
        extra_v = mm3(sk, (high, low), NN)
        out_ref[rows, :HD] = (gk_ref[rows, :] + feat_cot * slope).astype(BF16)
        out_ref[rows, HD:] = (gv_ref[rows, :] + extra_v).astype(BF16)


def finish_call(kv, cot, norm, later, later_norm, gk, gv):
    return pl.pallas_call(
        finish_kernel,
        out_shape=jax.ShapeDtypeStruct((2 * SEG, 2 * HD), BF16),
        compiler_params=params(16),
        cost_estimate=cost(2 * 5 * 2 * SEG * HD * HD, 3 << 20, 2 * SEG * HD),
        name="finish",
    )(kv, cot, norm, later, later_norm, gk, gv)


def to_heads(x, parts):
    tokens = x[0].shape[0]
    width = x[0].shape[1] // 8
    blocks = jnp.concatenate([a.reshape(tokens, 8, width) for a in x], axis=2)
    blocks = jnp.transpose(blocks, (1, 0, 2))
    moved = lax.all_to_all(blocks, "tp", split_axis=0, concat_axis=0, tiled=True)
    return moved.reshape(8 * tokens, parts * width)


def to_tokens(x):
    blocks = x.reshape(8, x.shape[0] // 8, x.shape[1])
    return lax.all_to_all(blocks, "tp", split_axis=0, concat_axis=0, tiled=True)


def over_seq(x):
    return lax.all_to_all(x, "seq", split_axis=0, concat_axis=0, tiled=True)


def local(query, keys, values, cotangent, rate, gate_logit):
    me = lax.axis_index("seq").astype(jnp.int32).reshape(1)
    gates = jax.nn.sigmoid(gate_logit)
    rate_row = jnp.pad(rate.reshape(1, 8), ((0, 0), (0, HD - 8)))
    kv = to_heads((keys, values), 2)
    q = to_heads((query,), 1)
    send, moment, total = moments_call(kv, rate_row)
    first = over_seq(send)
    d = to_heads((cotangent,), 1)
    states, norm = forward_call(me, first)
    state = over_seq(states)
    gq_local, gk, gv = attention_call(gates, q, d, kv)
    gq, cots, later, later_norm = memory_call(
        gates, rate, q, d, gq_local, state, norm, moment, total
    )
    third = over_seq(cots)
    gq_moved = to_tokens(gq)
    carried, carried_norm = backward_call(me, first, third)
    cot = over_seq(carried)
    gkv = finish_call(kv, cot, carried_norm, later, later_norm, gk, gv)
    gkv_moved = to_tokens(gkv)
    tokens = query.shape[0]
    grad_query = jnp.transpose(gq_moved, (1, 0, 2)).reshape(tokens, -1)
    grad_keys = jnp.transpose(gkv_moved[:, :, :HD], (1, 0, 2)).reshape(tokens, -1)
    grad_values = jnp.transpose(gkv_moved[:, :, HD:], (1, 0, 2)).reshape(tokens, -1)
    return grad_query, grad_keys, grad_values


def solution(mesh):
    rows = P(("seq", "tp"), None)
    in_specs = (rows, rows, rows, rows, P("seq", "tp"), P("tp"))
    return jax.shard_map(
        local, mesh=mesh, in_specs=in_specs, out_specs=(rows, rows, rows), check_vma=False
    )
```

time: 759 us -> 241 us (0.32)
  blocking collectives: 370 us -> 58.7 us
  other arithmetic: 162 us -> 0.87 us
  waiting for transfers between devices: 45.9 us -> 108 us
  matrix products: 60 us -> 0 us
  local copies, waits for them, and re-layouts: 65.8 us -> 12.2 us
  Pallas kernels: 0 us -> 18.5 us
  between operations: 15 us -> 0.83 us
  starting transfers between devices: 28.2 us -> 41.3 us
    unnamed x2 -> x0, blocking collectives: 260 us -> none
    all_gather x2 -> x0, blocking collectives: 92.7 us -> none  [the longest x1 50.3 us: entering_2(): gathered = jax.tree.map(lambda a: lax.all_gather(a, axis), part)]
    add x138 -> x0, other arithmetic: 77.6 us -> none  [the longest x62 65.4 us: link_states(): later[0][:, None, None] * earlier[1] + later[1]]
    select_n x136 -> x0, other arithmetic: 70 us -> none  [the longest x128 69.9 us: step(): return jax.tree.map(lambda a, b: jnp.where(reached, a, b), new, before)]
    all_to_all x6, waiting for transfers between devices: 45.9 us -> 108 us  [the longest x3 70 us: to_heads(): lax.all_to_all(blocks, 'tp', split_axis=0, concat_axis=0, tiled=True)]
    dot_general x56 -> x0, matrix products: 60 us -> none  [the longest x8 16.8 us: local_advance(): jnp.dot(probs_low.T, d_blk, preferred_element_type=jnp.float32)]
    all_to_all x1 -> x3, blocking collectives: 16.5 us -> 58.7 us  [the longest x2 38.3 us: over_seq(): return lax.all_to_all(x, 'seq', split_axis=0, concat_axis=0, tiled=True)]
    dynamic_slice x32 -> x0, local copies, waits for them, and re-layouts: 20.4 us -> none  [the longest x8 9.74 us: local_grads(): lax.scan(local_advance, (empty_grad, empty_grad), jnp.arange(row_count //...]
  transfers between devices with their start and end apart: 8 -> 6, of which waited for: 4 -> 5; matrix products, arithmetic and copies ran while one was open for 13% -> 2% of each run, Pallas kernels for 0% -> 5%
where the time goes in v1:
time: 241 us
  waiting for transfers between devices  108 us (45%)
  blocking collectives  58.7 us (24%)
  starting transfers between devices  41.3 us (17%)
  Pallas kernels  18.5 us (8%)
  local copies, waits for them, and re-layouts  12.2 us (5%)
    all_to_all x3, waiting for transfers between devices, to_heads(): lax.all_to_all(blocks, 'tp', split_axis=0, concat_axis=0, tiled=True)  70 us
    all_to_all x2, blocking collectives, over_seq(): return lax.all_to_all(x, 'seq', split_axis=0, concat_axis=0, tiled=True)  38.3 us
    all_to_all x1, waiting for transfers between devices, to_tokens(): return lax.all_to_all(blocks, 'tp', split_axis=0, concat_axis=0, tiled=True)  27.5 us
    all_to_all x2, starting transfers between devices, over_seq(): return lax.all_to_all(x, 'seq', split_axis=0, concat_axis=0, tiled=True)  23 us
    all_to_all x1, blocking collectives, to_tokens(): return lax.all_to_all(blocks, 'tp', split_axis=0, concat_axis=0, tiled=True)  20.4 us
    all_to_all x3, starting transfers between devices, to_heads(): lax.all_to_all(blocks, 'tp', split_axis=0, concat_axis=0, tiled=True)  14.8 us
    pallas_call x1, Pallas kernels, attention_call(): pl.pallas_call(attention_kernel, grid=(2, 4), in_specs=[pl.BlockSpec(memo...  11.3 us
    all_to_all x2, waiting for transfers between devices, over_seq(): return lax.all_to_all(x, 'seq', split_axis=0, concat_axis=0, tiled=True)  10.9 us
  transfers between devices with their start and end apart: 6, of which 5 were waited for; matrix products, arithmetic and copies ran while one was open for 2% of the time, Pallas kernels for 5%

profile of v1, /device:TPU:1, one launch (start us, length us, event | category | flops | bytes accessed | tf_op | source)
XLA Modules:
  0.0 240.8 jit_solution(13606382663644792784)
XLA Ops:
  0.6 0.0 copy-start
  0.6 0.0 copy-start.9
  0.7 0.0 copy-start.10
  0.7 0.9 copy-done
  1.6 1.1 copy_bitcast_fusion.2
  2.7 0.9 maximum_bitcast_fusion
  3.5 7.7 %all-to-all-start.2 = ((bf16[8,128,256]{2,1,0:T(8,128)(2,1)}), bf16[8,128,256]{2,1,0:T(8,128)(2,1)S(1)}, u32[]{:S(2)}, u32[]{:S(2)}) async-start(bf16[8,128,256]{2,1,0:T(8,128)(2,1)} %maximum_bitcast_fusion), calls=%async_computation.2 | async-start | bytes 1048576 | tf_op jit(solution)/shard_map/all_to_all | solution.py:361
  11.2 0.0 copy-done.9
  11.2 0.1 reshape.56
  11.3 14.7 %all-to-all-done.2 = bf16[8,128,256]{2,1,0:T(8,128)(2,1)S(1)} async-done(((bf16[8,128,256]{2,1,0:T(8,128)(2,1)}), bf16[8,128,256]{2,1,0:T(8,128)(2,1)S(1)}, u32[]{:S(2)}, u32[]{:S(2)}) %all-to-all-start.2) | async-done | bytes 524320 | tf_op jit(solution)/shard_map/all_to_all | solution.py:361
  25.9 1.1 moments.1
  27.1 17.0 %all-to-all-start.3 = ((f32[64,8,128]{2,1,0:T(8,128)}), f32[64,8,128]{2,1,0:T(8,128)S(1)}, u32[]{:S(2)}, u32[]{:S(2)}) async-start(f32[64,8,128]{2,1,0:T(8,128)} %get-tuple-element.18), calls=%async_computation.3 | async-start | bytes 524288 | tf_op jit(solution)/shard_map/all_to_all | solution.py:371
  44.1 0.0 copy-done.10
  44.1 0.0 copy-start.11
  44.1 1.1 copy.30
  45.2 10.9 %all-to-all-done.3.in_ref.first_ref = f32[64,8,128]{2,1,0:T(8,128)S(1)} async-done(((f32[64,8,128]{2,1,0:T(8,128)}), f32[64,8,128]{2,1,0:T(8,128)S(1)}, u32[]{:S(2)}, u32[]{:S(2)}) %all-to-all-start.3) | async-done | bytes 262176 | tf_op jit(solution)/shard_map/all_to_all | solution.py:371
  56.1 3.6 %all-to-all-start = ((bf16[8,128,512]{2,1,0:T(8,128)(2,1)}), bf16[8,128,512]{2,1,0:T(8,128)(2,1)S(1)}, u32[]{:S(2)}, u32[]{:S(2)}) async-start(bf16[8,128,512]{2,1,0:T(8,128)(2,1)} %bitcast.44), calls=%async_computation | async-start | bytes 2097152 | tf_op jit(solution)/shard_map/all_to_all | solution.py:361
  59.7 0.0 copy-done.11
  59.7 1.1 copy.29
  60.8 28.1 %all-to-all-done = bf16[8,128,512]{2,1,0:T(8,128)(2,1)S(1)} async-done(((bf16[8,128,512]{2,1,0:T(8,128)(2,1)}), bf16[8,128,512]{2,1,0:T(8,128)(2,1)S(1)}, u32[]{:S(2)}, u32[]{:S(2)}) %all-to-all-start) | async-done | bytes 1048608 | tf_op jit(solution)/shard_map/all_to_all | solution.py:361
  88.9 3.6 %all-to-all-start.1 = ((bf16[8,128,512]{2,1,0:T(8,128)(2,1)}), bf16[8,128,512]{2,1,0:T(8,128)(2,1)S(1)}, u32[]{:S(2)}, u32[]{:S(2)}) async-start(bf16[8,128,512]{2,1,0:T(8,128)(2,1)} %bitcast.57), calls=%async_computation.1 | async-start | bytes 2097152 | tf_op jit(solution)/shard_map/all_to_all | solution.py:361
  92.4 1.2 forward_scan.1
  93.6 0.0 copy-start.8
  93.7 0.7 copy-done.8
  94.4 27.2 %all-to-all-done.1 = bf16[8,128,512]{2,1,0:T(8,128)(2,1)S(1)} async-done(((bf16[8,128,512]{2,1,0:T(8,128)(2,1)}), bf16[8,128,512]{2,1,0:T(8,128)(2,1)S(1)}, u32[]{:S(2)}, u32[]{:S(2)}) %all-to-all-start.1) | async-done | bytes 1048608 | tf_op jit(solution)/shard_map/all_to_all | solution.py:361
  121.6 6.0 %all-to-all-start.4 = ((f32[64,8,128]{2,1,0:T(8,128)}), f32[64,8,128]{2,1,0:T(8,128)S(1)}, u32[]{:S(2)}, u32[]{:S(2)}) async-start(f32[64,8,128]{2,1,0:T(8,128)} %copy-done.8), calls=%async_computation.4 | async-start | bytes 524288 | tf_op jit(solution)/shard_map/all_to_all | solution.py:371
  127.6 0.0 copy-done.12
  127.6 11.3 %attention.1 = (f32[1024,512]{1,0:T(8,128)S(1)}, f32[1024,128]{1,0:T(8,128)S(1)}, f32[1024,128]{1,0:T(8,128)S(1)}) custom-call(f32[4]{0:T(128)S(1)} %add_divide_fusion.gate_ref, bf16[1024,512]{1,0:T(8,128)(2,1)S(1)} %bitcast.51, bf16[1024,512]{1,0:T(8,128)(2,1)S(1)} %bitcast.53, bf16[1024,256]{1,0:T(8,128)(2,1)S(1)} %bitcast.48, bf16[1024,256]{1,0:T(8,128)(2,1)S(1)} %bitcast.49), custom_call_target="tpu_custom_call" | custom-call | flops 2684354560 | bytes 6291456 | tf_op jit(solution)/shard_map/attention/pallas_call | solution.py:199
  138.9 0.0 copy-start.1
  138.9 1.3 copy-done.1
  140.3 0.8 copy-done.4
  141.1 0.8 copy-done.6
  141.9 0.0 all-to-all-done.4.state_ref
  141.9 1.6 copy-done.2
  143.5 3.2 %memory.1 = (bf16[1024,512]{1,0:T(8,128)(2,1)S(1)}, bf16[64,16,128]{2,1,0:T(8,128)(2,1)S(1)}, f32[128,128]{1,0:T(8,128)S(1)}, f32[8,128]{1,0:T(8,128)S(1)}) custom-call(f32[4]{0:T(128)S(1)} %add_divide_fusion.gate_ref, f32[2,4]{1,0:T(2,128)S(1)} %copy-done.9, bf16[1024,512]{1,0:T(8,128)(2,1)S(1)} %bitcast.52, bf16[1024,512]{1,0:T(8,128)(2,1)S(1)} %bitcast.54, ...), custom_call_target="tpu_custom_call" | custom-call | flops 402653184 | bytes 6291456 | tf_op jit(solution)/shard_map/memory/pallas_call | solution.py:270
  146.7 0.0 copy-start.3
  146.7 22.1 %all_to_all.45.in_ref = bf16[64,16,128]{2,1,0:T(8,128)(2,1)S(1)} all-to-all(bf16[64,16,128]{2,1,0:T(8,128)(2,1)S(1)} %get-tuple-element.24), channel_id=1, replica_groups=mesh['seq'=64,'tp'=8] {'seq'}, dimensions={0} | all-to-all | bytes 524288 | tf_op jit(solution)/shard_map/all_to_all | solution.py:371
  168.8 1.0 backward_scan.1
  169.9 16.2 %all_to_all.46.cot_ref = f32[64,4,128]{2,1,0:T(4,128)S(1)} all-to-all(f32[64,4,128]{2,1,0:T(4,128)S(1)} %get-tuple-element.25), channel_id=1, replica_groups=mesh['seq'=64,'tp'=8] {'seq'}, dimensions={0} | all-to-all | bytes 262144 | tf_op jit(solution)/shard_map/all_to_all | solution.py:371
  186.1 0.0 copy-done.7
  186.1 0.6 finish.1
  186.6 20.4 %all_to_all.47 = bf16[8,128,256]{2,1,0:T(8,128)(2,1)S(1)} all-to-all(bf16[8,128,256]{2,1,0:T(8,128)(2,1)S(1)} %bitcast.55), channel_id=1, replica_groups=mesh['seq'=64,'tp'=8] {'tp'}, dimensions={0} | all-to-all | bytes 1048576 | tf_op jit(solution)/shard_map/all_to_all | solution.py:367
  207.0 3.6 %all-to-all-start.5 = ((bf16[8,128,512]{2,1,0:T(8,128)(2,1)}), bf16[8,128,512]{2,1,0:T(8,128)(2,1)S(1)}, u32[]{:S(2)}, u32[]{:S(2)}) async-start(bf16[8,128,512]{2,1,0:T(8,128)(2,1)} %bitcast.56), calls=%async_computation.5 | async-start | bytes 2097152 | tf_op jit(solution)/shard_map/all_to_all | solution.py:367
  210.6 0.1 slice_bitcast_fusion
  210.7 0.8 copy.31
  211.5 0.8 copy.32
  212.2 27.5 %all-to-all-done.5 = bf16[8,128,512]{2,1,0:T(8,128)(2,1)S(1)} async-done(((bf16[8,128,512]{2,1,0:T(8,128)(2,1)}), bf16[8,128,512]{2,1,0:T(8,128)(2,1)S(1)}, u32[]{:S(2)}, u32[]{:S(2)}) %all-to-all-start.5) | async-done | bytes 1048608 | tf_op jit(solution)/shard_map/all_to_all | solution.py:367
  239.7 1.1 copy.20
  (10 shorter events, 0.0 us)
Async XLA Ops:
  0.6 1.0 copy-start
  0.6 10.5 %copy-start.9 = (f32[2,4]{1,0:T(2,128)S(1)}, f32[2,4]{1,0:T(2,128)}, u32[]{:S(2)}) copy-start(f32[2,4]{1,0:T(2,128)} %rate_ref.1) | copy-start | bytes 100
  0.7 43.5 %copy-start.10 = (bf16[128,4096]{1,0:T(8,128)(2,1)S(1)}, bf16[128,4096]{1,0:T(8,128)(2,1)}, u32[]{:S(2)}) copy-start(bf16[128,4096]{1,0:T(8,128)(2,1)} %param.6) | copy-start | bytes 3145732
  3.5 22.4 %all-to-all-start.2 = ((bf16[8,128,256]{2,1,0:T(8,128)(2,1)}), bf16[8,128,256]{2,1,0:T(8,128)(2,1)S(1)}, u32[]{:S(2)}, u32[]{:S(2)}) async-start(bf16[8,128,256]{2,1,0:T(8,128)(2,1)} %maximum_bitcast_fusion), calls=%async_computation.2 | async-start | bytes 1048576 | tf_op jit(solution)/shard_map/all_to_all | solution.py:361
  27.1 29.0 %all-to-all-start.3 = ((f32[64,8,128]{2,1,0:T(8,128)}), f32[64,8,128]{2,1,0:T(8,128)S(1)}, u32[]{:S(2)}, u32[]{:S(2)}) async-start(f32[64,8,128]{2,1,0:T(8,128)} %get-tuple-element.18), calls=%async_computation.3 | async-start | bytes 524288 | tf_op jit(solution)/shard_map/all_to_all | solution.py:371
  44.1 15.6 %copy-start.11 = (bf16[128,4096]{1,0:T(8,128)(2,1)S(1)}, bf16[128,4096]{1,0:T(8,128)(2,1)}, u32[]{:S(2)}) copy-start(bf16[128,4096]{1,0:T(8,128)(2,1)} %param.9) | copy-start | bytes 3145732
  56.1 32.8 %all-to-all-start = ((bf16[8,128,512]{2,1,0:T(8,128)(2,1)}), bf16[8,128,512]{2,1,0:T(8,128)(2,1)S(1)}, u32[]{:S(2)}, u32[]{:S(2)}) async-start(bf16[8,128,512]{2,1,0:T(8,128)(2,1)} %bitcast.44), calls=%async_computation | async-start | bytes 2097152 | tf_op jit(solution)/shard_map/all_to_all | solution.py:361
  60.8 66.8 %copy-start.12 = (f32[4]{0:T(128)S(1)}, f32[4]{0:T(128)}, u32[]{:S(2)}) copy-start(f32[4]{0:T(128)} %param.11) | copy-start | bytes 52
  88.9 32.7 %all-to-all-start.1 = ((bf16[8,128,512]{2,1,0:T(8,128)(2,1)}), bf16[8,128,512]{2,1,0:T(8,128)(2,1)S(1)}, u32[]{:S(2)}, u32[]{:S(2)}) async-start(bf16[8,128,512]{2,1,0:T(8,128)(2,1)} %bitcast.57), calls=%async_computation.1 | async-start | bytes 2097152 | tf_op jit(solution)/shard_map/all_to_all | solution.py:361
  93.6 0.7 copy-start.8
  121.6 20.3 %all-to-all-start.4 = ((f32[64,8,128]{2,1,0:T(8,128)}), f32[64,8,128]{2,1,0:T(8,128)S(1)}, u32[]{:S(2)}, u32[]{:S(2)}) async-start(f32[64,8,128]{2,1,0:T(8,128)} %copy-done.8), calls=%async_computation.4 | async-start | bytes 524288 | tf_op jit(solution)/shard_map/all_to_all | solution.py:371
  138.9 1.3 copy-start.1
  140.3 0.8 copy-start.4
  141.1 0.8 copy-start.6
  141.9 1.6 copy-start.2
  143.5 42.6 %copy-start.5 = (f32[1024,128]{1,0:T(8,128)S(1)}, f32[1024,128]{1,0:T(8,128)}, u32[]{:S(2)}) copy-start(f32[1024,128]{1,0:T(8,128)} %copy-done.4) | copy-start | bytes 1572868
  143.5 42.6 %copy-start.7 = (f32[1024,128]{1,0:T(8,128)S(1)}, f32[1024,128]{1,0:T(8,128)}, u32[]{:S(2)}) copy-start(f32[1024,128]{1,0:T(8,128)} %copy-done.6) | copy-start | bytes 1572868
  146.7 60.3 %copy-start.3 = (bf16[1024,512]{1,0:T(8,128)(2,1)}, bf16[1024,512]{1,0:T(8,128)(2,1)S(1)}, u32[]{:S(2)}) copy-start(bf16[1024,512]{1,0:T(8,128)(2,1)S(1)} %get-tuple-element.23) | copy-start | bytes 3145732
  207.0 32.7 %all-to-all-start.5 = ((bf16[8,128,512]{2,1,0:T(8,128)(2,1)}), bf16[8,128,512]{2,1,0:T(8,128)(2,1)S(1)}, u32[]{:S(2)}, u32[]{:S(2)}) async-start(bf16[8,128,512]{2,1,0:T(8,128)(2,1)} %bitcast.56), calls=%async_computation.5 | async-start | bytes 2097152 | tf_op jit(solution)/shard_map/all_to_all | solution.py:367

commit v2 on v1

v2 whole, which is shorter than its diff:
```python
import functools
import math

import jax
import jax.numpy as jnp
from jax import lax
from jax.experimental import pallas as pl
from jax.experimental.pallas import tpu as pltpu
from jax.sharding import PartitionSpec as P

HD = 128
SEG = 512
HALF = 64
BLK = 256
F32 = jnp.float32
BF16 = jnp.bfloat16
SCALE = 1.0 / math.sqrt(HD)
LOG2E = 1.4426950408889634
EXACT = lax.Precision.HIGHEST
VMEM = pltpu.VMEM
SMEM = pltpu.SMEM
NN = (((1,), (0,)), ((), ()))
NT = (((1,), (1,)), ((), ()))
TN = (((0,), (0,)), ((), ()))


def mm(a, b, dims, precision=None):
    return lax.dot_general(a, b, dims, precision=precision, preferred_element_type=F32)


def split(a):
    hi = a.astype(BF16)
    return hi, (a - hi.astype(F32)).astype(BF16)


def mm3(a, b, dims):
    ah, al = a if isinstance(a, tuple) else split(a)
    bh, bl = b if isinstance(b, tuple) else split(b)
    return mm(ah, bh, dims) + (mm(al, bh, dims) + mm(ah, bl, dims))


def mm2(a, b, dims):
    ah, al = split(a)
    return mm(ah, b, dims) + mm(al, b, dims)


def features_of(x):
    slope = jnp.exp(jnp.minimum(x, 0.0))
    return slope + jnp.maximum(x, 0.0), slope


def params(mib):
    return pltpu.CompilerParams(vmem_limit_bytes=mib << 20)


def cost(flops, size, exps=0):
    return pl.CostEstimate(flops=flops, bytes_accessed=size, transcendentals=exps)


ROWS = 2 * HD + 16


def moments_kernel(kv_ref, rate_ref, out_ref):
    for e in range(2):
        rows = pl.ds(e * SEG, SEG)
        sk, _ = features_of(kv_ref[rows, :HD].astype(F32))
        out_ref[pl.ds(e * HD, HD), :] = mm2(sk, kv_ref[rows, HD:], TN)
        total = jnp.sum(sk, axis=0, keepdims=True)
        out_ref[pl.ds(2 * HD + 4 * e, 4), :] = jnp.broadcast_to(total, (4, HD))
    out_ref[pl.ds(2 * HD + 8, 8), :] = rate_ref[...]


def moments_call(kv, rate_rows):
    return pl.pallas_call(
        moments_kernel,
        out_shape=jax.ShapeDtypeStruct((ROWS, HD), F32),
        compiler_params=params(16),
        cost_estimate=cost(2 * 2 * SEG * HD * HD * 2, 1 << 20, 2 * SEG * HD),
        name="moments",
    )(kv, rate_rows)


def rate_row(ref, e, h):
    row = 2 * HD + 8 + 4 * e + h
    return ref[row : row + 1, :]


def term(ref, e):
    total = 2 * HD + 4 * e
    return ref[pl.ds(e * HD, HD), :], ref[total : total + 1, :]


def pack(send_ref, i, state, norm, decay):
    send_ref[pl.ds(i * HD, HD), :] = state.astype(BF16)
    return split_rows(norm), split_rows(decay)


def split_rows(a):
    upper = a.astype(BF16).astype(F32)
    return upper, a - upper


def pack_tail(send_ref, tails):
    (n0, d0), (n1, d1) = tails
    rows = [n0[0], n1[0], n0[1], n1[1], d0[0], d1[0], d0[1], d1[1]]
    tail = jnp.concatenate(rows + [jnp.zeros((8, HD), F32)], axis=0)
    send_ref[pl.ds(2 * HD, 16), :] = tail.astype(BF16)


def store_state(ref, i, state, norm, decay):
    ref[pl.ds(i * HD, HD), :] = state
    ref[2 * HD + i : 2 * HD + i + 1, :] = norm
    ref[2 * HD + 2 + i : 2 * HD + 3 + i, :] = decay


def load_state(ref, i):
    return (
        ref[pl.ds(i * HD, HD), :],
        ref[2 * HD + i : 2 * HD + i + 1, :],
        ref[2 * HD + 2 + i : 2 * HD + 3 + i, :],
    )


def chip_kernel(core_ref, own_ref, other_ref, base_ref, send_ref):
    is_first = core_ref[0] == 0

    def rate(ref, e, i):
        return jnp.where(is_first, rate_row(ref, e, i), rate_row(ref, e, 2 + i))

    tails = []
    for i in range(2):
        side = []
        for ref in (own_ref, other_ref):
            (m0, t0), (m1, t1) = term(ref, 0), term(ref, 1)
            fade = jnp.exp(-rate(ref, 1, i))
            both = jnp.exp(-(rate(ref, 0, i) + rate(ref, 1, i)))
            side.append((fade * m0 + m1, fade * t0 + t1, both))
        (m_own, t_own, a_own), (m_other, t_other, a_other) = side
        w_own = jnp.where(is_first, a_other, 1.0)
        w_other = jnp.where(is_first, 1.0, a_own)
        state = w_own * m_own + w_other * m_other
        norm = w_own * t_own + w_other * t_other
        decay = a_own * a_other
        store_state(base_ref, i, state, norm, decay)
        tails.append(pack(send_ref, i, state, norm, decay))
    base_ref[pl.ds(2 * HD + 4, 12), :] = jnp.zeros((12, HD), F32)
    pack_tail(send_ref, tails)


def chip_call(core, own, other):
    return pl.pallas_call(
        chip_kernel,
        in_specs=[pl.BlockSpec(memory_space=SMEM)] + [pl.BlockSpec(memory_space=VMEM)] * 2,
        out_shape=(
            jax.ShapeDtypeStruct((ROWS, HD), F32),
            jax.ShapeDtypeStruct((ROWS, HD), BF16),
        ),
        compiler_params=params(16),
        cost_estimate=cost(1 << 20, 1 << 19),
        name="chip_terms",
    )(core, own, other)


def round_kernel(start, recv_ref, base_ref, *refs):
    held_ref, out_ref, send_ref = (None,) * start + refs if start else refs
    tail = recv_ref[pl.ds(2 * HD, 16), :].astype(F32)
    tails = []
    for i in range(2):
        state = recv_ref[pl.ds(i * HD, HD), :].astype(F32)
        norm = tail[i : i + 1] + tail[2 + i : 3 + i]
        decay = tail[4 + i : 5 + i] + tail[6 + i : 7 + i]
        if not start:
            state0, norm0, decay0 = load_state(held_ref, i)
            state = state0 + decay0 * state
            norm = norm0 + decay0 * norm
            decay = decay0 * decay
        store_state(out_ref, i, state, norm, decay)
        state1, norm1, decay1 = load_state(base_ref, i)
        tails.append(
            pack(send_ref, i, state1 + decay1 * state, norm1 + decay1 * norm, decay1 * decay)
        )
    out_ref[pl.ds(2 * HD + 4, 12), :] = jnp.zeros((12, HD), F32)
    pack_tail(send_ref, tails)


def round_call(recv, base, held):
    start = held is None
    operands = (recv, base) if start else (recv, base, held)
    return pl.pallas_call(
        functools.partial(round_kernel, start),
        out_shape=(
            jax.ShapeDtypeStruct((ROWS, HD), F32),
            jax.ShapeDtypeStruct((ROWS, HD), BF16),
        ),
        compiler_params=params(16),
        cost_estimate=cost(1 << 20, 1 << 19),
        name="round",
    )(*operands)


def swap_cores(x):
    return lax.ppermute(x, "seq", [(i, i ^ 1) for i in range(lax.axis_size("seq"))])


def exclusive_scan(base, send, ahead):
    size = lax.axis_size("seq")
    held = None
    hop = 2
    while hop < size:
        moves = [(i, i + hop) if ahead else (i + hop, i) for i in range(size - hop)]
        held, send = round_call(lax.ppermute(send, "seq", moves), base, held)
        hop *= 2
    return held


def cumulative(rates):
    rows = lax.broadcasted_iota(jnp.int32, (HALF, HALF), 0)
    cols = lax.broadcasted_iota(jnp.int32, (HALF, HALF), 1)
    upto = (cols <= rows).astype(F32)
    before = (cols < rows).astype(F32)
    same = (cols == rows).astype(F32)
    upto_t = (rows <= cols).astype(F32)
    before_t = (rows < cols).astype(F32)
    return dict(
        inc_col=mm(upto, rates, NN, EXACT),
        exc_col=mm(before, rates, NN, EXACT),
        inc_row=mm(rates, upto_t, TN, EXACT),
        exc_row=mm(rates, before_t, TN, EXACT),
        row=mm(rates, same, TN, EXACT),
        rows=rows,
        cols=cols,
    )


def pair_col(a, h):
    return a[:, h : h + 1] + a[:, 4 + h : 5 + h]


def pair_row(a, h):
    return a[h : h + 1, :] + a[4 + h : 5 + h, :]


def attention_kernel(gate_ref, q_ref, d_ref, k_ref, v_ref, extra_ref, gq_ref, gk_ref, gv_ref):
    h = pl.program_id(1)
    rest = 1.0 - gate_ref[h]
    local_cot = (rest * d_ref[...].astype(F32)).astype(BF16)
    u_pos = lax.broadcasted_iota(jnp.int32, (BLK, BLK), 0)
    t_pos = lax.broadcasted_iota(jnp.int32, (BLK, BLK), 1)
    visible = u_pos <= t_pos
    nb = SEG // BLK
    ks = [k_ref[pl.ds(i * BLK, BLK), :] for i in range(nb)]
    vs = [v_ref[pl.ds(i * BLK, BLK), :] for i in range(nb)]
    grad_k = [None] * nb
    grad_v = [None] * nb

    def plus(a, b):
        return b if a is None else a + b

    for tb in range(nb):
        q = q_ref[pl.ds(tb * BLK, BLK), :]
        lc = local_cot[tb * BLK : (tb + 1) * BLK]
        s = [mm(ks[u], q, NT) for u in range(tb + 1)]
        s[tb] = jnp.where(visible, s[tb], -1e30)
        top = functools.reduce(jnp.maximum, [jnp.max(a, axis=0, keepdims=True) for a in s])
        w = [jnp.exp2((a - top) * (SCALE * LOG2E)) for a in s]
        total = sum(jnp.sum(a, axis=0, keepdims=True) for a in w)
        inv = 1.0 / total
        p = [a * inv for a in w]
        gp = [mm(vs[u], lc, NT) for u in range(tb + 1)]
        inner = sum(jnp.sum(a * b, axis=0, keepdims=True) for a, b in zip(p, gp))
        gs = [(a * (b - inner) * SCALE).astype(BF16) for a, b in zip(p, gp)]
        gq_t = None
        for u in range(tb + 1):
            gq_t = plus(gq_t, mm(ks[u], gs[u], TN))
            grad_k[u] = plus(grad_k[u], mm(gs[u], q, NN))
            grad_v[u] = plus(grad_v[u], mm(p[u].astype(BF16), lc, NN))
        rows = pl.ds(tb * BLK, BLK)
        gq_ref[rows, :] = (gq_t.T + extra_ref[rows, :]).astype(BF16)

    @pl.when(h == 0)
    def _():
        for u in range(nb):
            gk_ref[pl.ds(u * BLK, BLK), :] = grad_k[u]
            gv_ref[pl.ds(u * BLK, BLK), :] = grad_v[u]

    @pl.when(h > 0)
    def _():
        for u in range(nb):
            gk_ref[pl.ds(u * BLK, BLK), :] += grad_k[u]
            gv_ref[pl.ds(u * BLK, BLK), :] += grad_v[u]


def attention_call(gates, qd, kv, extra):
    head = pl.BlockSpec((SEG, HD), lambda s, h: (s, h))
    return pl.pallas_call(
        attention_kernel,
        grid=(2, 4),
        in_specs=[
            pl.BlockSpec(memory_space=SMEM),
            head,
            pl.BlockSpec((SEG, HD), lambda s, h: (s, 4 + h)),
            pl.BlockSpec((SEG, HD), lambda s, h: (s, 0)),
            pl.BlockSpec((SEG, HD), lambda s, h: (s, 1)),
            head,
        ],
        out_specs=[
            head,
            pl.BlockSpec((SEG, HD), lambda s, h: (s, 0)),
            pl.BlockSpec((SEG, HD), lambda s, h: (s, 0)),
        ],
        out_shape=(
            jax.ShapeDtypeStruct((2 * SEG, 6 * HD), BF16),
            jax.ShapeDtypeStruct((2 * SEG, HD), F32),
            jax.ShapeDtypeStruct((2 * SEG, HD), F32),
        ),
        compiler_params=params(32),
        cost_estimate=cost(8 * 5 * 2 * SEG * SEG * HD, 6 << 20, 8 * SEG * SEG),
        name="attention",
    )(gates, qd, qd, kv, kv, extra)


def memory_kernel(
    core_ref, gate_ref, qd_ref, own_ref, other_ref, held_ref, held_other_ref,
    extra_ref, send_ref, later_ref, later_norm_ref, rows_ref,
):
    later = None
    later_norm = None
    is_first = core_ref[0] == 0
    m0, t0 = term(other_ref, 0)
    m1, t1 = term(other_ref, 1)
    for h in range(4):
        cols = pl.ds(h * HD, HD)
        dcols = pl.ds((4 + h) * HD, HD)
        gate = gate_ref[h]
        here = is_first if h < 2 else jnp.logical_not(is_first)
        memory, norm, _ = (
            jnp.where(here, a, b)
            for a, b in zip(load_state(held_ref, h % 2), load_state(held_other_ref, h % 2))
        )
        fade = jnp.exp(-rate_row(other_ref, 1, h))
        both = jnp.exp(-(rate_row(other_ref, 0, h) + rate_row(other_ref, 1, h)))
        memory = jnp.where(is_first, memory, both * memory + (fade * m0 + m1))
        norm = jnp.where(is_first, norm, both * norm + (fade * t0 + t1))
        decay = jnp.exp(-rate_row(own_ref, 0, h))
        cots = []
        for e in range(2):
            if e == 1:
                moment, total = term(own_ref, 0)
                memory = decay * memory + moment
                norm = decay * norm + total
            rows = pl.ds(e * SEG, SEG)
            sq, slope = features_of(qd_ref[rows, cols].astype(F32))
            sq_low = sq.astype(BF16)
            memory_low = memory.astype(BF16)
            numer = mm(sq_low, memory_low, NN)
            denom = jnp.sum(sq * norm, axis=1, keepdims=True) + 1.0
            inv = 1.0 / denom
            num_cot = (gate * qd_ref[rows, dcols].astype(F32)) * inv
            den_cot = -jnp.sum(num_cot * numer, axis=1, keepdims=True) * inv
            num_low = num_cot.astype(BF16)
            feat_cot = mm(num_low, memory_low, NT) + den_cot * norm
            extra_ref[rows, cols] = feat_cot * slope
            cots.append((mm(sq_low, num_low, TN), jnp.sum(sq * den_cot, axis=0, keepdims=True)))
        own = cots[0][0] + decay * cots[1][0]
        own_norm = cots[0][1] + decay * cots[1][1]
        rows_ref[:, 2 * h, :] = own[:HALF]
        rows_ref[:, 2 * h + 1, :] = own[HALF:]
        rows_ref[:, 8 + h, :] = jnp.broadcast_to(own_norm, (HALF, HD))
        later = cots[1][0] if later is None else later + cots[1][0]
        later_norm = cots[1][1] if later_norm is None else later_norm + cots[1][1]
    lane = lax.broadcasted_iota(jnp.int32, (1, HD), 1)
    rest = jnp.zeros((1, HD), F32)
    for e in range(2):
        for h in range(4):
            rest = jnp.where(lane == 4 * e + h, rate_row(own_ref, e, h), rest)
    for part in range(4):
        upper, rest = split_rows(rest)
        rows_ref[:, 12 + part, :] = jnp.broadcast_to(upper, (HALF, HD))
    send_ref[...] = rows_ref[...].astype(BF16)
    later_ref[...] = later
    later_norm_ref[...] = jnp.broadcast_to(later_norm, (8, HD))


def memory_call(core, gates, qd, own, other, held, held_other):
    return pl.pallas_call(
        memory_kernel,
        in_specs=[pl.BlockSpec(memory_space=SMEM)] * 2 + [pl.BlockSpec(memory_space=VMEM)] * 5,
        out_shape=(
            jax.ShapeDtypeStruct((2 * SEG, 4 * HD), F32),
            jax.ShapeDtypeStruct((HALF, 16, HD), BF16),
            jax.ShapeDtypeStruct((HD, HD), F32),
            jax.ShapeDtypeStruct((8, HD), F32),
        ),
        scratch_shapes=[pltpu.VMEM((HALF, 16, HD), F32)],
        compiler_params=params(32),
        cost_estimate=cost(8 * 3 * 2 * SEG * HD * HD, 6 << 20, 8 * SEG * HD),
        name="memory",
    )(core, gates, qd, own, other, held, held_other)


def backward_kernel(me_ref, in_ref, out_ref, norm_ref, rows_ref):
    rows_ref[...] = in_ref[...].astype(F32)
    rates = sum(rows_ref[:, 12 + part, :] for part in range(3))
    c = cumulative(rates)
    after = c["cols"] > c["rows"]
    mine = lax.broadcasted_iota(jnp.int32, (HALF, HD), 0) == me_ref[0]
    one = zero = None
    for h in range(4):
        gap = pair_row(c["exc_row"], h) - pair_col(c["inc_col"], h)
        weight = jnp.exp(jnp.where(after, -gap, -1e30))
        own = jnp.concatenate(
            [rows_ref[:, 2 * h, :], rows_ref[:, 2 * h + 1, :], rows_ref[:, 8 + h, :]], axis=1
        )
        carried = mm(weight, own, NN, EXACT)
        earlier = jnp.exp(-rates[:, 4 + h : 5 + h]) * carried
        one = carried if one is None else one + carried
        zero = earlier if zero is None else zero + earlier
    for e, value in ((0, zero), (1, one)):
        out_ref[:, 2 * e, :] = value[:, :HD]
        out_ref[:, 2 * e + 1, :] = value[:, HD : 2 * HD]
        own = jnp.sum(jnp.where(mine, value[:, 2 * HD :], 0.0), axis=0, keepdims=True)
        norm_ref[4 * e : 4 * e + 4, :] = jnp.broadcast_to(own, (4, HD))


def backward_call(me, recv):
    return pl.pallas_call(
        backward_kernel,
        in_specs=[pl.BlockSpec(memory_space=SMEM)] + [pl.BlockSpec(memory_space=VMEM)],
        out_shape=(
            jax.ShapeDtypeStruct((HALF, 4, HD), F32),
            jax.ShapeDtypeStruct((8, HD), F32),
        ),
        scratch_shapes=[pltpu.VMEM((HALF, 16, HD), F32)],
        compiler_params=params(16),
        cost_estimate=cost(4 * 2 * 64 * 64 * 384 * 6, 1 << 20, 4 * 4096),
        name="backward_scan",
    )(me, recv)


def finish_kernel(
    grads_ref, kv_ref, cot_ref, norm_ref, later_ref, later_norm_ref, gk_ref, gv_ref, out_ref
):
    del grads_ref
    for e in range(2):
        rows = pl.ds(e * SEG, SEG)
        moment_cot = jnp.concatenate([cot_ref[:, 2 * e, :], cot_ref[:, 2 * e + 1, :]], axis=0)
        total_cot = norm_ref[4 * e : 4 * e + 1, :]
        if e == 0:
            moment_cot = moment_cot + later_ref[...]
            total_cot = total_cot + later_norm_ref[0:1, :]
        sk, slope = features_of(kv_ref[rows, :HD].astype(F32))
        high, low = split(moment_cot)
        values = kv_ref[rows, HD:]
        feat_cot = mm(values, high, NT) + mm(values, low, NT) + total_cot
        extra_v = mm3(sk, (high, low), NN)
        out_ref[rows, :HD] = (gk_ref[rows, :] + feat_cot * slope).astype(BF16)
        out_ref[rows, HD:] = (gv_ref[rows, :] + extra_v).astype(BF16)


def finish_call(grads, kv, cot, norm, later, later_norm, gk, gv):
    return pl.pallas_call(
        finish_kernel,
        grid=(1,),
        in_specs=[pl.BlockSpec(memory_space=pl.ANY)] + [pl.BlockSpec(memory_space=VMEM)] * 7,
        out_specs=pl.BlockSpec((2 * SEG, 2 * HD), lambda i: (0, 2)),
        out_shape=jax.ShapeDtypeStruct((2 * SEG, 6 * HD), BF16),
        input_output_aliases={0: 0},
        compiler_params=params(16),
        cost_estimate=cost(2 * 5 * 2 * SEG * HD * HD, 3 << 20, 2 * SEG * HD),
        name="finish",
    )(grads, kv, cot, norm, later, later_norm, gk, gv)


def to_heads(x, y):
    tokens, width = x.shape[0], x.shape[1] // 8
    blocks = jnp.concatenate([a.reshape(tokens, 8, width) for a in (x, y)], axis=2)
    blocks = jnp.transpose(blocks, (1, 0, 2))
    moved = lax.all_to_all(blocks, "tp", split_axis=0, concat_axis=0, tiled=True)
    return moved.reshape(8 * tokens, 2 * width)


def to_tokens(x):
    blocks = x.reshape(8, x.shape[0] // 8, x.shape[1])
    return lax.all_to_all(blocks, "tp", split_axis=0, concat_axis=0, tiled=True)


def columns(x, start, width):
    part = jnp.transpose(x[:, :, start : start + width], (1, 0, 2))
    return part.reshape(x.shape[1], -1)


def over_seq(x):
    return lax.all_to_all(x, "seq", split_axis=0, concat_axis=0, tiled=True)


def local(query, keys, values, cotangent, rate, gate_logit):
    me = lax.axis_index("seq").astype(jnp.int32).reshape(1)
    core = me % 2
    gates = jax.nn.sigmoid(gate_logit)
    rate_rows = jnp.broadcast_to(rate.reshape(8, 1), (8, HD))
    kv = to_heads(keys, values)
    qd = to_heads(query, cotangent)
    own = moments_call(kv, rate_rows)
    other = swap_cores(own)
    base, send = chip_call(core, own, other)
    held = exclusive_scan(base, send, True)
    held_other = swap_cores(held)
    extra, cots, later, later_norm = memory_call(core, gates, qd, own, other, held, held_other)
    third = over_seq(cots)
    grads, gk, gv = attention_call(gates, qd, kv, extra)
    carried, carried_norm = backward_call(me, third)
    cot = over_seq(carried)
    grads = finish_call(grads, kv, cot, carried_norm, later, later_norm, gk, gv)
    moved = to_tokens(grads)
    width = 4 * HD
    return (
        columns(moved, 0, width),
        columns(moved, width, HD),
        columns(moved, width + HD, HD),
    )


def solution(mesh):
    rows = P(("seq", "tp"), None)
    in_specs = (rows, rows, rows, rows, P("seq", "tp"), P("tp"))
    return jax.shard_map(
        local, mesh=mesh, in_specs=in_specs, out_specs=(rows, rows, rows), check_vma=False
    )
```

time: 241 us -> 188 us (0.78)
  waiting for transfers between devices: 108 us -> 20.6 us
  starting transfers between devices: 41.3 us -> 64.9 us
  blocking collectives: 58.7 us -> 64 us
  local copies, waits for them, and re-layouts: 12.2 us -> 15 us
    all_to_all x3 -> x2, waiting for transfers between devices: 70 us -> 11.3 us  [to_heads(): lax.all_to_all(blocks, 'tp', split_axis=0, concat_axis=0, tiled=True)]
    ppermute x0 -> x7, starting transfers between devices: none -> 47.6 us  [the longest x5 36.1 us: exclusive_scan(): held, send = round_call(lax.ppermute(send, 'seq', moves), base, held)]
    all_to_all x1 -> x0, waiting for transfers between devices: 27.5 us -> none  [to_tokens(): return lax.all_to_all(blocks, 'tp', split_axis=0, concat_axis=0, tiled=True)]
    all_to_all x1, blocking collectives: 20.4 us -> 45.5 us  [to_tokens(): return lax.all_to_all(blocks, 'tp', split_axis=0, concat_axis=0, tiled=True)]
    all_to_all x2 -> x1, blocking collectives: 38.3 us -> 18.6 us  [over_seq(): return lax.all_to_all(x, 'seq', split_axis=0, concat_axis=0, tiled=True)]
    all_to_all x2 -> x1, starting transfers between devices: 23 us -> 6.02 us  [over_seq(): return lax.all_to_all(x, 'seq', split_axis=0, concat_axis=0, tiled=True)]
    all_to_all x2 -> x1, waiting for transfers between devices: 10.9 us -> 0.01 us  [over_seq(): return lax.all_to_all(x, 'seq', split_axis=0, concat_axis=0, tiled=True)]
    ppermute x0 -> x7, waiting for transfers between devices: none -> 9.29 us  [the longest x5 7.37 us: exclusive_scan(): held, send = round_call(lax.ppermute(send, 'seq', moves), base, held)]
  transfers between devices with their start and end apart: 6 -> 10, of which waited for: 5 -> 8; matrix products, arithmetic and copies ran while one was open for 2% -> 2% of each run, Pallas kernels for 5% -> 7%
where the time goes in v2:
time: 188 us; the launch traced here: 186 us
  starting transfers between devices  64.9 us (35%)
  blocking collectives  64 us (34%)
  waiting for transfers between devices  20.6 us (11%)
  Pallas kernels  18.1 us (10%)
  local copies, waits for them, and re-layouts  15 us (8%)
  other arithmetic  2.5 us (1%)
    all_to_all x1, blocking collectives, to_tokens(): return lax.all_to_all(blocks, 'tp', split_axis=0, concat_axis=0, tiled=True)  45.5 us
    ppermute x5, starting transfers between devices, exclusive_scan(): held, send = round_call(lax.ppermute(send, 'seq', moves), base, held)  36.1 us
    all_to_all x1, blocking collectives, over_seq(): return lax.all_to_all(x, 'seq', split_axis=0, concat_axis=0, tiled=True)  18.6 us
    pallas_call x1, Pallas kernels, attention_call(): pl.pallas_call(attention_kernel, grid=(2, 4), in_specs=[pl.BlockSpec(memo...  11.7 us
    ppermute x2, starting transfers between devices, swap_cores(): lax.ppermute(x, 'seq', [(i, i ^ 1) for i in range(lax.axis_size('seq'))])  11.4 us
    all_to_all x2, waiting for transfers between devices, to_heads(): lax.all_to_all(blocks, 'tp', split_axis=0, concat_axis=0, tiled=True)  11.3 us
    all_to_all x2, starting transfers between devices, to_heads(): lax.all_to_all(blocks, 'tp', split_axis=0, concat_axis=0, tiled=True)  11.3 us
    unnamed x24, local copies, waits for them, and re-layouts  9.34 us
  transfers between devices with their start and end apart: 10, of which 8 were waited for; matrix products, arithmetic and copies ran while one was open for 2% of the time, Pallas kernels for 7%

profile of v2, /device:TPU:1, one launch (start us, length us, event | category | flops | bytes accessed | tf_op | source)
XLA Modules:
  0.0 186.0 jit_solution(16316552416182266233)
XLA Ops:
  0.6 0.0 copy-start
  0.6 0.9 copy-done
  1.6 1.1 copy_bitcast_fusion.4
  2.7 0.9 maximum_bitcast_fusion.1
  3.5 7.7 %all-to-all-start.1 = ((bf16[8,128,256]{2,1,0:T(8,128)(2,1)}), bf16[8,128,256]{2,1,0:T(8,128)(2,1)S(1)}, u32[]{:S(2)}, u32[]{:S(2)}) async-start(bf16[8,128,256]{2,1,0:T(8,128)(2,1)} %maximum_bitcast_fusion.1), calls=%async_computation.1 | async-start | bytes 1048576 | tf_op jit(solution)/shard_map/all_to_all | solution.py:478
  11.2 1.8 copy_bitcast_fusion
  12.9 1.6 maximum_bitcast_fusion
  14.6 11.3 %all-to-all-done.1 = bf16[8,128,256]{2,1,0:T(8,128)(2,1)S(1)} async-done(((bf16[8,128,256]{2,1,0:T(8,128)(2,1)}), bf16[8,128,256]{2,1,0:T(8,128)(2,1)S(1)}, u32[]{:S(2)}, u32[]{:S(2)}) %all-to-all-start.1) | async-done | bytes 524320 | tf_op jit(solution)/shard_map/all_to_all | solution.py:478
  25.9 3.6 %all-to-all-start = ((bf16[8,128,1024]{2,1,0:T(8,128)(2,1)}), bf16[8,128,1024]{2,1,0:T(8,128)(2,1)S(1)}, u32[]{:S(2)}, u32[]{:S(2)}) async-start(bf16[8,128,1024]{2,1,0:T(8,128)(2,1)} %maximum_bitcast_fusion), calls=%async_computation | async-start | bytes 4194304 | tf_op jit(solution)/shard_map/all_to_all | solution.py:478
  29.5 0.0 copy-start.10
  29.6 0.1 broadcast_in_dim.7
  29.6 0.1 broadcast_in_dim.8.rate_ref
  29.7 0.4 moments.1.own_ref
  30.1 5.6 %collective-permute-start = (f32[272,128]{1,0:T(8,128)S(1)}, f32[272,128]{1,0:T(8,128)S(1)}, u32[]{:S(2)}, u32[]{:S(2)}) collective-permute-start(f32[272,128]{1,0:T(8,128)S(1)} %moments.1.own_ref), channel_id=1, source_target_pairs={{0,8},{8,0},{16,24},{24,16},{32,40},{40,32},{48,56},{56,48},{64,72... | collective-permute-start | bytes 417800 | tf_op jit(solution)/shard_map/ppermute | solution.py:202
  35.8 1.0 collective-permute-done.other_ref
  36.7 0.1 chip_terms.1
  36.8 4.0 %collective-permute-start.1 = (bf16[272,128]{1,0:T(8,128)(2,1)S(1)}, bf16[272,128]{1,0:T(8,128)(2,1)S(1)}, u32[]{:S(2)}, u32[]{:S(2)}) collective-permute-start(bf16[272,128]{1,0:T(8,128)(2,1)S(1)} %get-tuple-element.23), channel_id=1, source_target_pairs={{0,16},{8,24},{16,32},{24,40},{32,48},{40,56},{48,64},{56,72},{64,... | collective-permute-start | bytes 208904 | tf_op jit(solution)/shard_map/ppermute | solution.py:211
  40.8 1.3 collective-permute-done.1.recv_ref
  42.2 5.8 %collective-permute-start.2 = (bf16[272,128]{1,0:T(8,128)(2,1)S(1)}, bf16[272,128]{1,0:T(8,128)(2,1)S(1)}, u32[]{:S(2)}, u32[]{:S(2)}) collective-permute-start(bf16[272,128]{1,0:T(8,128)(2,1)S(1)} %get-tuple-element.25), channel_id=1, source_target_pairs={{0,32},{8,40},{16,48},{24,56},{32,64},{40,72},{48,80},{56,88},{64,... | collective-permute-start | bytes 208904 | tf_op jit(solution)/shard_map/ppermute | solution.py:211
  48.0 1.3 collective-permute-done.2.recv_ref
  49.4 12.4 %collective-permute-start.3 = (bf16[272,128]{1,0:T(8,128)(2,1)S(1)}, bf16[272,128]{1,0:T(8,128)(2,1)S(1)}, u32[]{:S(2)}, u32[]{:S(2)}) collective-permute-start(bf16[272,128]{1,0:T(8,128)(2,1)S(1)} %get-tuple-element.27), channel_id=1, source_target_pairs={{0,64},{8,72},{16,80},{24,88},{32,96},{40,104},{48,112},{56,120},{... | collective-permute-start | bytes 208904 | tf_op jit(solution)/shard_map/ppermute | solution.py:211
  61.8 2.0 %collective-permute-done.3.recv_ref = bf16[272,128]{1,0:T(8,128)(2,1)S(1)} collective-permute-done((bf16[272,128]{1,0:T(8,128)(2,1)S(1)}, bf16[272,128]{1,0:T(8,128)(2,1)S(1)}, u32[]{:S(2)}, u32[]{:S(2)}) %collective-permute-start.3) | collective-permute-done | bytes 69664 | tf_op jit(solution)/shard_map/ppermute | solution.py:211
  63.9 7.6 %collective-permute-start.4 = (bf16[272,128]{1,0:T(8,128)(2,1)S(1)}, bf16[272,128]{1,0:T(8,128)(2,1)S(1)}, u32[]{:S(2)}, u32[]{:S(2)}) collective-permute-start(bf16[272,128]{1,0:T(8,128)(2,1)S(1)} %get-tuple-element.29), channel_id=1, source_target_pairs={{0,128},{8,136},{16,144},{24,152},{32,160},{40,168},{48,176},{56,1... | collective-permute-start | bytes 208904 | tf_op jit(solution)/shard_map/ppermute | solution.py:211
  71.5 1.3 collective-permute-done.4.recv_ref
  72.9 6.2 %collective-permute-start.5 = (bf16[272,128]{1,0:T(8,128)(2,1)S(1)}, bf16[272,128]{1,0:T(8,128)(2,1)S(1)}, u32[]{:S(2)}, u32[]{:S(2)}) collective-permute-start(bf16[272,128]{1,0:T(8,128)(2,1)S(1)} %get-tuple-element.31), channel_id=1, source_target_pairs={{0,256},{8,264},{16,272},{24,280},{32,288},{40,296},{48,304},{56,3... | collective-permute-start | bytes 208904 | tf_op jit(solution)/shard_map/ppermute | solution.py:211
  79.2 1.3 collective-permute-done.5.recv_ref
  80.5 0.7 round.9
  81.2 5.8 %collective-permute-start.6 = (f32[272,128]{1,0:T(8,128)S(1)}, f32[272,128]{1,0:T(8,128)S(1)}, u32[]{:S(2)}, u32[]{:S(2)}) collective-permute-start(f32[272,128]{1,0:T(8,128)S(1)} %get-tuple-element.33.held_ref), channel_id=1, source_target_pairs={{0,8},{8,0},{16,24},{24,16},{32,40},{40,32},{48,56},{56,48},{64,72... | collective-permute-start | bytes 417800 | tf_op jit(solution)/shard_map/ppermute | solution.py:202
  87.0 1.0 collective-permute-done.6.held_other_ref
  88.0 2.9 %memory.1 = (f32[1024,512]{1,0:T(8,128)S(1)}, bf16[64,16,128]{2,1,0:T(8,128)(2,1)S(1)}, f32[128,128]{1,0:T(8,128)S(1)}, f32[8,128]{1,0:T(8,128)S(1)}) custom-call(s32[1]{0:T(128)S(6)} %select_n.7.core_ref, f32[4]{0:T(128)S(1)} %add_divide_fusion.gate_ref, bf16[1024,1024]{1,0:T(8,128)(2,1)S(1)} %bitcast.40, f32[272,128]{1,0:T(8,128)S(1)} %moments.1.own_ref, ...), custom_call_target="tpu_custom_call" | custom-call | flops 402653184 | bytes 6291456 | tf_op jit(solution)/shard_map/memory/pallas_call | solution.py:385
  90.9 1.3 copy-done.7
  92.2 18.6 %all_to_all.25.in_ref = bf16[64,16,128]{2,1,0:T(8,128)(2,1)S(1)} all-to-all(bf16[64,16,128]{2,1,0:T(8,128)(2,1)S(1)} %get-tuple-element.36), channel_id=1, replica_groups=mesh['seq'=64,'tp'=8] {'seq'}, dimensions={0} | all-to-all | bytes 524288 | tf_op jit(solution)/shard_map/all_to_all | solution.py:493
  110.8 1.7 backward_scan.1
  112.5 6.0 %all-to-all-start.3 = ((f32[64,4,128]{2,1,0:T(4,128)}), f32[64,4,128]{2,1,0:T(4,128)S(1)}, u32[]{:S(2)}, u32[]{:S(2)}) async-start(f32[64,4,128]{2,1,0:T(4,128)} %get-tuple-element.37), calls=%async_computation.3 | async-start | bytes 262144 | tf_op jit(solution)/shard_map/all_to_all | solution.py:493
  118.5 1.6 copy-done.8
  120.1 11.7 %attention.1 = (bf16[1024,768]{1,0:T(8,128)(2,1)S(1)}, f32[1024,128]{1,0:T(8,128)S(1)}, f32[1024,128]{1,0:T(8,128)S(1)}) custom-call(f32[4]{0:T(128)S(1)} %add_divide_fusion.gate_ref, bf16[1024,1024]{1,0:T(8,128)(2,1)S(1)} %bitcast.41, bf16[1024,1024]{1,0:T(8,128)(2,1)S(1)} %bitcast.42, bf16[1024,256]{1,0:T(8,128)(2,1)S(1)} %bitcast.45, ...), custom_call_target="tpu_custom_call" | custom-call | flops 2684354560 | bytes 6291456 | tf_op jit(solution)/shard_map/attention/pallas_call | solution.py:295
  131.8 1.2 copy-done.1
  133.0 0.8 copy-done.3
  133.8 1.4 copy-done.2
  135.2 1.0 copy-done.4
  136.2 0.8 copy-done.6
  137.1 0.6 finish.1
  137.6 45.5 %all_to_all.26 = bf16[8,128,768]{2,1,0:T(8,128)(2,1)S(1)} all-to-all(bf16[8,128,768]{2,1,0:T(8,128)(2,1)S(1)} %bitcast.43), channel_id=1, replica_groups=mesh['seq'=64,'tp'=8] {'tp'}, dimensions={0} | all-to-all | bytes 3145728 | tf_op jit(solution)/shard_map/all_to_all | solution.py:484
  183.1 0.1 slice_bitcast_fusion
  183.2 1.1 copy.21
  184.3 0.1 slice_bitcast_fusion.1
  184.4 0.8 copy.30
  185.2 0.8 copy.31
  (19 shorter events, 0.2 us)
Async XLA Ops:
  0.6 1.0 copy-start
  3.5 22.4 %all-to-all-start.1 = ((bf16[8,128,256]{2,1,0:T(8,128)(2,1)}), bf16[8,128,256]{2,1,0:T(8,128)(2,1)S(1)}, u32[]{:S(2)}, u32[]{:S(2)}) async-start(bf16[8,128,256]{2,1,0:T(8,128)(2,1)} %maximum_bitcast_fusion.1), calls=%async_computation.1 | async-start | bytes 1048576 | tf_op jit(solution)/shard_map/all_to_all | solution.py:478
  14.6 15.0 %copy-start.9 = (f32[2,4]{1,0:T(2,128)S(1)}, f32[2,4]{1,0:T(2,128)}, u32[]{:S(2)}) copy-start(f32[2,4]{1,0:T(2,128)} %param.10) | copy-start | bytes 100
  25.9 62.1 %all-to-all-start = ((bf16[8,128,1024]{2,1,0:T(8,128)(2,1)}), bf16[8,128,1024]{2,1,0:T(8,128)(2,1)S(1)}, u32[]{:S(2)}, u32[]{:S(2)}) async-start(bf16[8,128,1024]{2,1,0:T(8,128)(2,1)} %maximum_bitcast_fusion), calls=%async_computation | async-start | bytes 4194304 | tf_op jit(solution)/shard_map/all_to_all | solution.py:478
  29.5 57.5 %copy-start.10 = (f32[4]{0:T(128)S(1)}, f32[4]{0:T(128)}, u32[]{:S(2)}) copy-start(f32[4]{0:T(128)} %param.11) | copy-start | bytes 52
  30.1 6.6 %collective-permute-start = (f32[272,128]{1,0:T(8,128)S(1)}, f32[272,128]{1,0:T(8,128)S(1)}, u32[]{:S(2)}, u32[]{:S(2)}) collective-permute-start(f32[272,128]{1,0:T(8,128)S(1)} %moments.1.own_ref), channel_id=1, source_target_pairs={{0,8},{8,0},{16,24},{24,16},{32,40},{40,32},{48,56},{56,48},{64,72... | collective-permute-start | bytes 417800 | tf_op jit(solution)/shard_map/ppermute | solution.py:202
  36.8 5.4 %collective-permute-start.1 = (bf16[272,128]{1,0:T(8,128)(2,1)S(1)}, bf16[272,128]{1,0:T(8,128)(2,1)S(1)}, u32[]{:S(2)}, u32[]{:S(2)}) collective-permute-start(bf16[272,128]{1,0:T(8,128)(2,1)S(1)} %get-tuple-element.23), channel_id=1, source_target_pairs={{0,16},{8,24},{16,32},{24,40},{32,48},{40,56},{48,64},{56,72},{64,... | collective-permute-start | bytes 208904 | tf_op jit(solution)/shard_map/ppermute | solution.py:211
  42.2 7.2 %collective-permute-start.2 = (bf16[272,128]{1,0:T(8,128)(2,1)S(1)}, bf16[272,128]{1,0:T(8,128)(2,1)S(1)}, u32[]{:S(2)}, u32[]{:S(2)}) collective-permute-start(bf16[272,128]{1,0:T(8,128)(2,1)S(1)} %get-tuple-element.25), channel_id=1, source_target_pairs={{0,32},{8,40},{16,48},{24,56},{32,64},{40,72},{48,80},{56,88},{64,... | collective-permute-start | bytes 208904 | tf_op jit(solution)/shard_map/ppermute | solution.py:211
  49.4 14.4 %collective-permute-start.3 = (bf16[272,128]{1,0:T(8,128)(2,1)S(1)}, bf16[272,128]{1,0:T(8,128)(2,1)S(1)}, u32[]{:S(2)}, u32[]{:S(2)}) collective-permute-start(bf16[272,128]{1,0:T(8,128)(2,1)S(1)} %get-tuple-element.27), channel_id=1, source_target_pairs={{0,64},{8,72},{16,80},{24,88},{32,96},{40,104},{48,112},{56,120},{... | collective-permute-start | bytes 208904 | tf_op jit(solution)/shard_map/ppermute | solution.py:211
  63.9 9.0 %collective-permute-start.4 = (bf16[272,128]{1,0:T(8,128)(2,1)S(1)}, bf16[272,128]{1,0:T(8,128)(2,1)S(1)}, u32[]{:S(2)}, u32[]{:S(2)}) collective-permute-start(bf16[272,128]{1,0:T(8,128)(2,1)S(1)} %get-tuple-element.29), channel_id=1, source_target_pairs={{0,128},{8,136},{16,144},{24,152},{32,160},{40,168},{48,176},{56,1... | collective-permute-start | bytes 208904 | tf_op jit(solution)/shard_map/ppermute | solution.py:211
  72.9 7.6 %collective-permute-start.5 = (bf16[272,128]{1,0:T(8,128)(2,1)S(1)}, bf16[272,128]{1,0:T(8,128)(2,1)S(1)}, u32[]{:S(2)}, u32[]{:S(2)}) collective-permute-start(bf16[272,128]{1,0:T(8,128)(2,1)S(1)} %get-tuple-element.31), channel_id=1, source_target_pairs={{0,256},{8,264},{16,272},{24,280},{32,288},{40,296},{48,304},{56,3... | collective-permute-start | bytes 208904 | tf_op jit(solution)/shard_map/ppermute | solution.py:211
  81.2 6.8 %collective-permute-start.6 = (f32[272,128]{1,0:T(8,128)S(1)}, f32[272,128]{1,0:T(8,128)S(1)}, u32[]{:S(2)}, u32[]{:S(2)}) collective-permute-start(f32[272,128]{1,0:T(8,128)S(1)} %get-tuple-element.33.held_ref), channel_id=1, source_target_pairs={{0,8},{8,0},{16,24},{24,16},{32,40},{40,32},{48,56},{56,48},{64,72... | collective-permute-start | bytes 417800 | tf_op jit(solution)/shard_map/ppermute | solution.py:202
  90.9 1.3 copy-start.7
  92.2 20.2 %copy-start.5 = (f32[128,128]{1,0:T(8,128)}, f32[128,128]{1,0:T(8,128)S(1)}, u32[]{:S(2)}) copy-start(f32[128,128]{1,0:T(8,128)S(1)} %get-tuple-element.39.later_ref) | copy-start | bytes 196612
  112.5 21.3 %all-to-all-start.3 = ((f32[64,4,128]{2,1,0:T(4,128)}), f32[64,4,128]{2,1,0:T(4,128)S(1)}, u32[]{:S(2)}, u32[]{:S(2)}) async-start(f32[64,4,128]{2,1,0:T(4,128)} %get-tuple-element.37), calls=%async_computation.3 | async-start | bytes 262144 | tf_op jit(solution)/shard_map/all_to_all | solution.py:493
  118.5 1.6 copy-start.8
  131.8 1.2 copy-start.1
  133.0 0.8 copy-start.3
  133.8 1.4 copy-start.2
  135.2 1.0 copy-start.4
  136.2 0.8 copy-start.6

commit v3 on v2

--- a/solution.py
+++ b/solution.py
@@ -161,19 +161,27 @@
     )(core, own, other)
 
 
-def round_kernel(start, recv_ref, base_ref, *refs):
-    held_ref, out_ref, send_ref = (None,) * start + refs if start else refs
-    tail = recv_ref[pl.ds(2 * HD, 16), :].astype(F32)
+def round_kernel(start, count, *refs):
+    recv_refs, refs = refs[:count], refs[count:]
+    base_ref = refs[0]
+    held_ref = None if start else refs[1]
+    out_ref, send_ref = refs[-2:]
+    windows = [None, None] if start else [load_state(held_ref, i) for i in range(2)]
+    for recv_ref in recv_refs:
+        tail = recv_ref[pl.ds(2 * HD, 16), :].astype(F32)
+        for i in range(2):
+            state = recv_ref[pl.ds(i * HD, HD), :].astype(F32)
+            norm = tail[i : i + 1] + tail[2 + i : 3 + i]
+            decay = tail[4 + i : 5 + i] + tail[6 + i : 7 + i]
+            if windows[i] is not None:
+                state0, norm0, decay0 = windows[i]
+                state = state0 + decay0 * state
+                norm = norm0 + decay0 * norm
+                decay = decay0 * decay
+            windows[i] = (state, norm, decay)
     tails = []
     for i in range(2):
-        state = recv_ref[pl.ds(i * HD, HD), :].astype(F32)
-        norm = tail[i : i + 1] + tail[2 + i : 3 + i]
-        decay = tail[4 + i : 5 + i] + tail[6 + i : 7 + i]
-        if not start:
-            state0, norm0, decay0 = load_state(held_ref, i)
-            state = state0 + decay0 * state
-            norm = norm0 + decay0 * norm
-            decay = decay0 * decay
+        state, norm, decay = windows[i]
         store_state(out_ref, i, state, norm, decay)
         state1, norm1, decay1 = load_state(base_ref, i)
         tails.append(
@@ -184,10 +192,11 @@
 
 
 def round_call(recv, base, held):
-    start = held is None
-    operands = (recv, base) if start else (recv, base, held)
-    return pl.pallas_call(
-        functools.partial(round_kernel, start),
+    operands = [*recv, base]
+    if held is not None:
+        operands.append(held)
+    return pl.pallas_call(
+        functools.partial(round_kernel, held is None, len(recv)),
         out_shape=(
             jax.ShapeDtypeStruct((ROWS, HD), F32),
             jax.ShapeDtypeStruct((ROWS, HD), BF16),
@@ -207,9 +216,13 @@
     held = None
     hop = 2
     while hop < size:
-        moves = [(i, i + hop) if ahead else (i + hop, i) for i in range(size - hop)]
-        held, send = round_call(lax.ppermute(send, "seq", moves), base, held)
-        hop *= 2
+        radix = 2 if hop == 8 else 4
+        recv = []
+        for step in range(hop, min(radix * hop, size), hop):
+            moves = [(i, i + step) if ahead else (i + step, i) for i in range(size - step)]
+            recv.append(lax.ppermute(send, "seq", moves))
+        held, send = round_call(recv, base, held)
+        hop *= radix
     return held
 
 
@@ -240,8 +253,26 @@
     return a[h : h + 1, :] + a[4 + h : 5 + h, :]
 
 
-def attention_kernel(gate_ref, q_ref, d_ref, k_ref, v_ref, extra_ref, gq_ref, gk_ref, gv_ref):
-    h = pl.program_id(1)
+def retrieval_cots(gate, q, d, memory, norm):
+    sq, slope = features_of(q.astype(F32))
+    numer = mm(sq.astype(BF16), memory, NN)
+    inv = 1.0 / (jnp.sum(sq * norm, axis=1, keepdims=True) + 1.0)
+    num_cot = (gate * d.astype(F32)) * inv
+    den_cot = -jnp.sum(num_cot * numer, axis=1, keepdims=True) * inv
+    return sq, slope, num_cot, den_cot
+
+
+def attention_kernel(
+    gate_ref, q_ref, d_ref, k_ref, v_ref, memory_ref, norm_ref, *refs
+):
+    gq_ref, gk_ref, gv_ref, mark_ref = refs[-4:]
+    mark_ref[...] = jnp.zeros_like(mark_ref)
+    h = pl.program_id(0)
+    memory, norm = memory_ref[...].astype(BF16), norm_ref[0:1, :]
+    _, slope, num_cot, den_cot = retrieval_cots(
+        gate_ref[h], q_ref[...], d_ref[...], memory, norm
+    )
+    extra = (mm(num_cot.astype(BF16), memory, NT) + den_cot * norm) * slope
     rest = 1.0 - gate_ref[h]
     local_cot = (rest * d_ref[...].astype(F32)).astype(BF16)
     u_pos = lax.broadcasted_iota(jnp.int32, (BLK, BLK), 0)
@@ -275,7 +306,7 @@
             grad_k[u] = plus(grad_k[u], mm(gs[u], q, NN))
             grad_v[u] = plus(grad_v[u], mm(p[u].astype(BF16), lc, NN))
         rows = pl.ds(tb * BLK, BLK)
-        gq_ref[rows, :] = (gq_t.T + extra_ref[rows, :]).astype(BF16)
+        gq_ref[rows, :] = (gq_t.T + extra[tb * BLK : (tb + 1) * BLK]).astype(BF16)
 
     @pl.when(h == 0)
     def _():
@@ -290,38 +321,43 @@
             gv_ref[pl.ds(u * BLK, BLK), :] += grad_v[u]
 
 
-def attention_call(gates, qd, kv, extra):
-    head = pl.BlockSpec((SEG, HD), lambda s, h: (s, h))
+def attention_call(seg, gates, qd, kv, kept, earlier=()):
+    def head(first):
+        return pl.BlockSpec((SEG, HD), lambda h: (seg, first + h))
+
+    def shared(col):
+        return pl.BlockSpec((SEG, HD), lambda h: (seg, col))
+
     return pl.pallas_call(
         attention_kernel,
-        grid=(2, 4),
+        grid=(4,),
         in_specs=[
             pl.BlockSpec(memory_space=SMEM),
-            head,
-            pl.BlockSpec((SEG, HD), lambda s, h: (s, 4 + h)),
-            pl.BlockSpec((SEG, HD), lambda s, h: (s, 0)),
-            pl.BlockSpec((SEG, HD), lambda s, h: (s, 1)),
-            head,
-        ],
-        out_specs=[
-            head,
-            pl.BlockSpec((SEG, HD), lambda s, h: (s, 0)),
-            pl.BlockSpec((SEG, HD), lambda s, h: (s, 0)),
-        ],
+            head(0),
+            head(4),
+            shared(0),
+            shared(1),
+            pl.BlockSpec((HD, HD), lambda h: (4 * seg + h, 0)),
+            pl.BlockSpec((8, HD), lambda h: (9 * HD // 8 + 4 * seg + h, 0)),
+        ]
+        + [pl.BlockSpec(memory_space=pl.ANY)] * len(earlier),
+        out_specs=[head(0), shared(0), shared(0), pl.BlockSpec((8, HD), lambda h: (0, 0))],
         out_shape=(
             jax.ShapeDtypeStruct((2 * SEG, 6 * HD), BF16),
             jax.ShapeDtypeStruct((2 * SEG, HD), F32),
             jax.ShapeDtypeStruct((2 * SEG, HD), F32),
+            jax.ShapeDtypeStruct((8, HD), F32),
         ),
-        compiler_params=params(32),
-        cost_estimate=cost(8 * 5 * 2 * SEG * SEG * HD, 6 << 20, 8 * SEG * SEG),
+        input_output_aliases={7 + i: i for i in range(len(earlier))},
+        compiler_params=params(60),
+        cost_estimate=cost(4 * 5 * 2 * SEG * SEG * HD, 3 << 20, 4 * SEG * SEG),
         name="attention",
-    )(gates, qd, qd, kv, kv, extra)
+    )(gates, qd, qd, kv, kv, kept, kept, *earlier)
 
 
 def memory_kernel(
     core_ref, gate_ref, qd_ref, own_ref, other_ref, held_ref, held_other_ref,
-    extra_ref, send_ref, later_ref, later_norm_ref, rows_ref,
+    kept_ref, send_ref, rows_ref,
 ):
     later = None
     later_norm = None
@@ -349,18 +385,14 @@
                 memory = decay * memory + moment
                 norm = decay * norm + total
             rows = pl.ds(e * SEG, SEG)
-            sq, slope = features_of(qd_ref[rows, cols].astype(F32))
-            sq_low = sq.astype(BF16)
             memory_low = memory.astype(BF16)
-            numer = mm(sq_low, memory_low, NN)
-            denom = jnp.sum(sq * norm, axis=1, keepdims=True) + 1.0
-            inv = 1.0 / denom
-            num_cot = (gate * qd_ref[rows, dcols].astype(F32)) * inv
-            den_cot = -jnp.sum(num_cot * numer, axis=1, keepdims=True) * inv
-            num_low = num_cot.astype(BF16)
-            feat_cot = mm(num_low, memory_low, NT) + den_cot * norm
-            extra_ref[rows, cols] = feat_cot * slope
-            cots.append((mm(sq_low, num_low, TN), jnp.sum(sq * den_cot, axis=0, keepdims=True)))
+            kept_ref[pl.ds((4 * e + h) * HD, HD), :] = memory
+            kept_ref[pl.ds(9 * HD + (4 * e + h) * 8, 8), :] = jnp.broadcast_to(norm, (8, HD))
+            sq, _, num_cot, den_cot = retrieval_cots(
+                gate, qd_ref[rows, cols], qd_ref[rows, dcols], memory_low, norm
+            )
+            state_cot = mm(sq.astype(BF16), num_cot.astype(BF16), TN)
+            cots.append((state_cot, jnp.sum(sq * den_cot, axis=0, keepdims=True)))
         own = cots[0][0] + decay * cots[1][0]
         own_norm = cots[0][1] + decay * cots[1][1]
         rows_ref[:, 2 * h, :] = own[:HALF]
@@ -377,8 +409,8 @@
         upper, rest = split_rows(rest)
         rows_ref[:, 12 + part, :] = jnp.broadcast_to(upper, (HALF, HD))
     send_ref[...] = rows_ref[...].astype(BF16)
-    later_ref[...] = later
-    later_norm_ref[...] = jnp.broadcast_to(later_norm, (8, HD))
+    kept_ref[pl.ds(8 * HD, HD), :] = later
+    kept_ref[pl.ds(9 * HD + 64, 8), :] = jnp.broadcast_to(later_norm, (8, HD))
 
 
 def memory_call(core, gates, qd, own, other, held, held_other):
@@ -386,19 +418,18 @@
         memory_kernel,
         in_specs=[pl.BlockSpec(memory_space=SMEM)] * 2 + [pl.BlockSpec(memory_space=VMEM)] * 5,
         out_shape=(
-            jax.ShapeDtypeStruct((2 * SEG, 4 * HD), F32),
+            jax.ShapeDtypeStruct((9 * HD + 72, HD), F32),
             jax.ShapeDtypeStruct((HALF, 16, HD), BF16),
-            jax.ShapeDtypeStruct((HD, HD), F32),
-            jax.ShapeDtypeStruct((8, HD), F32),
         ),
         scratch_shapes=[pltpu.VMEM((HALF, 16, HD), F32)],
-        compiler_params=params(32),
-        cost_estimate=cost(8 * 3 * 2 * SEG * HD * HD, 6 << 20, 8 * SEG * HD),
+        compiler_params=params(24),
+        cost_estimate=cost(8 * 2 * 2 * SEG * HD * HD, 3 << 20, 8 * SEG * HD),
         name="memory",
     )(core, gates, qd, own, other, held, held_other)
 
 
-def backward_kernel(me_ref, in_ref, out_ref, norm_ref, rows_ref):
+def backward_kernel(me_ref, in_ref, earlier_ref, out_ref, norm_ref, rows_ref):
+    del earlier_ref
     rows_ref[...] = in_ref[...].astype(F32)
     rates = sum(rows_ref[:, 12 + part, :] for part in range(3))
     c = cumulative(rates)
@@ -422,10 +453,13 @@
         norm_ref[4 * e : 4 * e + 4, :] = jnp.broadcast_to(own, (4, HD))
 
 
-def backward_call(me, recv):
+def backward_call(me, recv, earlier):
     return pl.pallas_call(
         backward_kernel,
-        in_specs=[pl.BlockSpec(memory_space=SMEM)] + [pl.BlockSpec(memory_space=VMEM)],
+        in_specs=[pl.BlockSpec(memory_space=SMEM)] + [
+            pl.BlockSpec(memory_space=VMEM),
+            pl.BlockSpec(memory_space=pl.ANY),
+        ],
         out_shape=(
             jax.ShapeDtypeStruct((HALF, 4, HD), F32),
             jax.ShapeDtypeStruct((8, HD), F32),
@@ -434,59 +468,124 @@
         compiler_params=params(16),
         cost_estimate=cost(4 * 2 * 64 * 64 * 384 * 6, 1 << 20, 4 * 4096),
         name="backward_scan",
-    )(me, recv)
+    )(me, recv, earlier)
 
 
 def finish_kernel(
     grads_ref, kv_ref, cot_ref, norm_ref, later_ref, later_norm_ref, gk_ref, gv_ref, out_ref
 ):
     del grads_ref
-    for e in range(2):
-        rows = pl.ds(e * SEG, SEG)
-        moment_cot = jnp.concatenate([cot_ref[:, 2 * e, :], cot_ref[:, 2 * e + 1, :]], axis=0)
-        total_cot = norm_ref[4 * e : 4 * e + 1, :]
-        if e == 0:
-            moment_cot = moment_cot + later_ref[...]
-            total_cot = total_cot + later_norm_ref[0:1, :]
-        sk, slope = features_of(kv_ref[rows, :HD].astype(F32))
-        high, low = split(moment_cot)
-        values = kv_ref[rows, HD:]
-        feat_cot = mm(values, high, NT) + mm(values, low, NT) + total_cot
-        extra_v = mm3(sk, (high, low), NN)
-        out_ref[rows, :HD] = (gk_ref[rows, :] + feat_cot * slope).astype(BF16)
-        out_ref[rows, HD:] = (gv_ref[rows, :] + extra_v).astype(BF16)
-
-
-def finish_call(grads, kv, cot, norm, later, later_norm, gk, gv):
+    is_last = pl.program_id(0) == 1
+
+    def rows(low, high):
+        return jnp.where(is_last, high, low)
+
+    moment_cot = jnp.concatenate(
+        [
+            rows(cot_ref[:, 0, :], cot_ref[:, 2, :]),
+            rows(cot_ref[:, 1, :], cot_ref[:, 3, :]),
+        ],
+        axis=0,
+    )
+    moment_cot = moment_cot + rows(later_ref[...], 0.0)
+    total_cot = rows(norm_ref[0:1, :] + later_norm_ref[0:1, :], norm_ref[4:5, :])
+    sk, slope = features_of(kv_ref[:, :HD].astype(F32))
+    high, low = split(moment_cot)
+    values = kv_ref[:, HD:]
+    feat_cot = mm(values, high, NT) + mm(values, low, NT) + total_cot
+    extra_v = mm3(sk, (high, low), NN)
+    out_ref[:, :HD] = (gk_ref[...] + feat_cot * slope).astype(BF16)
+    out_ref[:, HD:] = (gv_ref[...] + extra_v).astype(BF16)
+
+
+def finish_call(grads, kv, cot, norm, kept, gk, gv):
+    part = pl.BlockSpec((SEG, HD), lambda e: (e, 0))
     return pl.pallas_call(
         finish_kernel,
-        grid=(1,),
-        in_specs=[pl.BlockSpec(memory_space=pl.ANY)] + [pl.BlockSpec(memory_space=VMEM)] * 7,
-        out_specs=pl.BlockSpec((2 * SEG, 2 * HD), lambda i: (0, 2)),
+        grid=(2,),
+        in_specs=[
+            pl.BlockSpec(memory_space=pl.ANY),
+            pl.BlockSpec((SEG, 2 * HD), lambda e: (e, 0)),
+            pl.BlockSpec((HALF, 4, HD), lambda e: (0, 0, 0)),
+            pl.BlockSpec((8, HD), lambda e: (0, 0)),
+            pl.BlockSpec((HD, HD), lambda e: (8, 0)),
+            pl.BlockSpec((8, HD), lambda e: (9 * HD // 8 + 8, 0)),
+            part,
+            part,
+        ],
+        out_specs=pl.BlockSpec((SEG, 2 * HD), lambda e: (e, 2)),
         out_shape=jax.ShapeDtypeStruct((2 * SEG, 6 * HD), BF16),
         input_output_aliases={0: 0},
-        compiler_params=params(16),
+        compiler_params=params(60),
         cost_estimate=cost(2 * 5 * 2 * SEG * HD * HD, 3 << 20, 2 * SEG * HD),
         name="finish",
-    )(grads, kv, cot, norm, later, later_norm, gk, gv)
-
-
-def to_heads(x, y):
+    )(grads, kv, cot, norm, kept, kept, gk, gv)
+
+
+def copies_kernel(moves, count, *refs):
+    refs, sems = refs[:count], refs[count]
+    copies = [
+        pltpu.make_async_copy(refs[a].at[src], refs[b].at[dst], sems.at[i])
+        for i, (a, src, b, dst) in enumerate(moves)
+    ]
+    for copy in copies:
+        copy.start()
+    for copy in copies:
+        copy.wait()
+
+
+def copies_call(moves, arrays, outs, mib, name):
+    return pl.pallas_call(
+        functools.partial(copies_kernel, moves, len(arrays) + len(outs)),
+        in_specs=[pl.BlockSpec(memory_space=VMEM)] * len(arrays),
+        out_specs=[pl.BlockSpec(memory_space=pl.ANY)] * len(outs),
+        out_shape=[jax.ShapeDtypeStruct(shape, BF16) for shape in outs],
+        scratch_shapes=[pltpu.SemaphoreType.DMA((len(moves),))],
+        compiler_params=params(mib),
+        cost_estimate=cost(0, 4 * sum(math.prod(shape) for shape in outs)),
+        name=name,
+    )(*arrays)
+
+
+def pack_pair(x, y):
+    tokens, width = x.shape[0], x.shape[1] // 8
+    every = slice(None)
+    moves = [
+        (a, (every, pl.ds(g * width, width)), 2, (g, every, pl.ds(a * width, width)))
+        for g in range(8)
+        for a in range(2)
+    ]
+    return copies_call(moves, (x, y), [(8, tokens, 2 * width)], 60, "pack_pair")[0]
+
+
+def unpack_grads(x):
+    tokens = x.shape[1]
+    every = slice(None)
+    widths = (4 * HD, HD, HD)
+    starts = (0, 4 * HD, 5 * HD)
+    moves = [
+        (0, (g, every, pl.ds(start, width)), 1 + i, (every, pl.ds(g * width, width)))
+        for g in range(8)
+        for i, (start, width) in enumerate(zip(starts, widths))
+    ]
+    outs = [(tokens, 8 * width) for width in widths]
+    return copies_call(moves, (x,), outs, 8, "unpack_grads")
+
+
+def side_by_side(x, y):
     tokens, width = x.shape[0], x.shape[1] // 8
     blocks = jnp.concatenate([a.reshape(tokens, 8, width) for a in (x, y)], axis=2)
-    blocks = jnp.transpose(blocks, (1, 0, 2))
+    return jnp.transpose(blocks, (1, 0, 2))
+
+
+def to_heads(blocks):
     moved = lax.all_to_all(blocks, "tp", split_axis=0, concat_axis=0, tiled=True)
-    return moved.reshape(8 * tokens, 2 * width)
+    return moved.reshape(-1, blocks.shape[2])
 
 
 def to_tokens(x):
     blocks = x.reshape(8, x.shape[0] // 8, x.shape[1])
     return lax.all_to_all(blocks, "tp", split_axis=0, concat_axis=0, tiled=True)
-
-
-def columns(x, start, width):
-    part = jnp.transpose(x[:, :, start : start + width], (1, 0, 2))
-    return part.reshape(x.shape[1], -1)
 
 
 def over_seq(x):
@@ -498,26 +597,21 @@
     core = me % 2
     gates = jax.nn.sigmoid(gate_logit)
     rate_rows = jnp.broadcast_to(rate.reshape(8, 1), (8, HD))
-    kv = to_heads(keys, values)
-    qd = to_heads(query, cotangent)
+    kv = to_heads(pack_pair(keys, values))
+    qd = to_heads(side_by_side(query, cotangent))
     own = moments_call(kv, rate_rows)
     other = swap_cores(own)
     base, send = chip_call(core, own, other)
     held = exclusive_scan(base, send, True)
     held_other = swap_cores(held)
-    extra, cots, later, later_norm = memory_call(core, gates, qd, own, other, held, held_other)
-    third = over_seq(cots)
-    grads, gk, gv = attention_call(gates, qd, kv, extra)
-    carried, carried_norm = backward_call(me, third)
+    kept, cots = memory_call(core, gates, qd, own, other, held, held_other)
+    arrived = over_seq(cots)
+    *part, mark = attention_call(0, gates, qd, kv, kept)
+    carried, carried_norm = backward_call(me, arrived, mark)
     cot = over_seq(carried)
-    grads = finish_call(grads, kv, cot, carried_norm, later, later_norm, gk, gv)
-    moved = to_tokens(grads)
-    width = 4 * HD
-    return (
-        columns(moved, 0, width),
-        columns(moved, width, HD),
-        columns(moved, width + HD, HD),
-    )
+    grads, gk, gv, _ = attention_call(1, gates, qd, kv, kept, part)
+    grads = finish_call(grads, kv, cot, carried_norm, kept, gk, gv)
+    return tuple(unpack_grads(to_tokens(grads)))
 
 
 def solution(mesh):

time: 188 us -> 179 us (0.952)
  blocking collectives: 64 us -> 44.4 us
  local copies, waits for them, and re-layouts: 15 us -> 4.69 us
  Pallas kernels: 18.1 us -> 27.5 us
  starting transfers between devices: 64.9 us -> 73.2 us
  waiting for transfers between devices: 20.6 us -> 26.2 us
    all_to_all x1 -> x0, blocking collectives: 18.6 us -> none  [over_seq(): return lax.all_to_all(x, 'seq', split_axis=0, concat_axis=0, tiled=True)]
    all_to_all x1 -> x2, starting transfers between devices: 6.02 us -> 15.5 us  [over_seq(): return lax.all_to_all(x, 'seq', split_axis=0, concat_axis=0, tiled=True)]
    pallas_call x7 -> x8, Pallas kernels: 13.1 us -> 21.8 us  [the longest x2 14.9 us: attention_call(): pl.pallas_call(attention_kernel, grid=(4,), in_specs=[pl.BlockSpec(memory...]
    all_to_all x1 -> x2, waiting for transfers between devices: 0.01 us -> 7.4 us  [over_seq(): return lax.all_to_all(x, 'seq', split_axis=0, concat_axis=0, tiled=True)]
    unnamed x24 -> x18, local copies, waits for them, and re-layouts: 9.34 us -> 2.78 us
    reshape x5 -> x1, local copies, waits for them, and re-layouts: 5.46 us -> 1.76 us  [side_by_side(): a.reshape(tokens, 8, width)]
    ppermute x5 -> x7, waiting for transfers between devices: 7.37 us -> 5.58 us  [exclusive_scan(): recv.append(lax.ppermute(send, 'seq', moves))]
    ppermute x5 -> x7, starting transfers between devices: 36.1 us -> 36.2 us  [exclusive_scan(): recv.append(lax.ppermute(send, 'seq', moves))]
  transfers between devices with their start and end apart: 10 -> 13, of which waited for: 8 -> 8; matrix products, arithmetic and copies ran while one was open for 2% -> 2% of each run, Pallas kernels for 7% -> 9%
where the time goes in v3:
time: 179 us
  starting transfers between devices  73.2 us (41%)
  blocking collectives  44.4 us (25%)
  Pallas kernels  27.5 us (15%)
  waiting for transfers between devices  26.2 us (15%)
  local copies, waits for them, and re-layouts  4.69 us (3%)
    all_to_all x1, blocking collectives, to_tokens(): return lax.all_to_all(blocks, 'tp', split_axis=0, concat_axis=0, tiled=True)  44.4 us
    ppermute x7, starting transfers between devices, exclusive_scan(): recv.append(lax.ppermute(send, 'seq', moves))  36.2 us
    all_to_all x2, starting transfers between devices, over_seq(): return lax.all_to_all(x, 'seq', split_axis=0, concat_axis=0, tiled=True)  15.5 us
    pallas_call x2, Pallas kernels, attention_call(): pl.pallas_call(attention_kernel, grid=(4,), in_specs=[pl.BlockSpec(memory...  14.9 us
    all_to_all x2, waiting for transfers between devices, to_heads(): lax.all_to_all(blocks, 'tp', split_axis=0, concat_axis=0, tiled=True)  11.3 us
    all_to_all x2, starting transfers between devices, to_heads(): lax.all_to_all(blocks, 'tp', split_axis=0, concat_axis=0, tiled=True)  11.3 us
    ppermute x2, starting transfers between devices, swap_cores(): lax.ppermute(x, 'seq', [(i, i ^ 1) for i in range(lax.axis_size('seq'))])  10.3 us
    all_to_all x2, waiting for transfers between devices, over_seq(): return lax.all_to_all(x, 'seq', split_axis=0, concat_axis=0, tiled=True)  7.4 us
  transfers between devices with their start and end apart: 13, of which 8 were waited for; matrix products, arithmetic and copies ran while one was open for 2% of the time, Pallas kernels for 9%

profile of v3, /device:TPU:1, one launch (start us, length us, event | category | flops | bytes accessed | tf_op | source)
XLA Modules:
  0.0 178.6 jit_solution(7384826187356423086)
XLA Ops:
  0.6 1.9 %pack_pair.1 = bf16[8,128,256]{2,1,0:T(8,128)(2,1)} custom-call(bf16[128,1024]{1,0:T(8,128)(2,1)} %refs_0_.1, bf16[128,1024]{1,0:T(8,128)(2,1)} %refs_1_.1), custom_call_target="tpu_custom_call" | custom-call | bytes 1048576 | tf_op jit(solution)/shard_map/pack_pair/pallas_call | solution.py:538
  2.6 7.7 %all-to-all-start.1 = ((bf16[8,128,256]{2,1,0:T(8,128)(2,1)}), bf16[8,128,256]{2,1,0:T(8,128)(2,1)S(1)}, u32[]{:S(2)}, u32[]{:S(2)}) async-start(bf16[8,128,256]{2,1,0:T(8,128)(2,1)} %pack_pair.1), calls=%async_computation.1 | async-start | bytes 1048576 | tf_op jit(solution)/shard_map/all_to_all | solution.py:582
  10.2 1.8 copy_bitcast_fusion
  12.0 1.6 maximum_bitcast_fusion
  13.7 11.3 %all-to-all-done.1 = bf16[8,128,256]{2,1,0:T(8,128)(2,1)S(1)} async-done(((bf16[8,128,256]{2,1,0:T(8,128)(2,1)}), bf16[8,128,256]{2,1,0:T(8,128)(2,1)S(1)}, u32[]{:S(2)}, u32[]{:S(2)}) %all-to-all-start.1) | async-done | bytes 524320 | tf_op jit(solution)/shard_map/all_to_all | solution.py:582
  25.0 3.6 %all-to-all-start = ((bf16[8,128,1024]{2,1,0:T(8,128)(2,1)}), bf16[8,128,1024]{2,1,0:T(8,128)(2,1)S(1)}, u32[]{:S(2)}, u32[]{:S(2)}) async-start(bf16[8,128,1024]{2,1,0:T(8,128)(2,1)} %maximum_bitcast_fusion), calls=%async_computation | async-start | bytes 4194304 | tf_op jit(solution)/shard_map/all_to_all | solution.py:582
  28.6 0.0 copy-start.8
  28.6 0.1 broadcast_in_dim.7
  28.7 0.1 broadcast_in_dim.8.rate_ref
  28.8 0.0 copy-done.1
  28.8 0.4 moments.1.own_ref
  29.2 5.6 %collective-permute-start = (f32[272,128]{1,0:T(8,128)S(1)}, f32[272,128]{1,0:T(8,128)S(1)}, u32[]{:S(2)}, u32[]{:S(2)}) collective-permute-start(f32[272,128]{1,0:T(8,128)S(1)} %moments.1.own_ref), channel_id=1, source_target_pairs={{0,8},{8,0},{16,24},{24,16},{32,40},{40,32},{48,56},{56,48},{64,72... | collective-permute-start | bytes 417800 | tf_op jit(solution)/shard_map/ppermute | solution.py:211
  34.8 1.0 collective-permute-done.other_ref
  35.8 0.1 chip_terms.1
  35.9 7.6 %collective-permute-start.3 = (bf16[272,128]{1,0:T(8,128)(2,1)S(1)}, bf16[272,128]{1,0:T(8,128)(2,1)S(1)}, u32[]{:S(2)}, u32[]{:S(2)}) collective-permute-start(bf16[272,128]{1,0:T(8,128)(2,1)S(1)} %get-tuple-element.21), channel_id=1, source_target_pairs={{0,48},{8,56},{16,64},{24,72},{32,80},{40,88},{48,96},{56,104},{64... | collective-permute-start | bytes 208904 | tf_op jit(solution)/shard_map/ppermute | solution.py:223
  43.5 6.1 %collective-permute-start.2 = (bf16[272,128]{1,0:T(8,128)(2,1)S(1)}, bf16[272,128]{1,0:T(8,128)(2,1)S(1)}, u32[]{:S(2)}, u32[]{:S(2)}) collective-permute-start(bf16[272,128]{1,0:T(8,128)(2,1)S(1)} %get-tuple-element.21), channel_id=1, source_target_pairs={{0,32},{8,40},{16,48},{24,56},{32,64},{40,72},{48,80},{56,88},{64,... | collective-permute-start | bytes 208904 | tf_op jit(solution)/shard_map/ppermute | solution.py:223
  49.6 3.1 %collective-permute-start.1 = (bf16[272,128]{1,0:T(8,128)(2,1)S(1)}, bf16[272,128]{1,0:T(8,128)(2,1)S(1)}, u32[]{:S(2)}, u32[]{:S(2)}) collective-permute-start(bf16[272,128]{1,0:T(8,128)(2,1)S(1)} %get-tuple-element.21), channel_id=1, source_target_pairs={{0,16},{8,24},{16,32},{24,40},{32,48},{40,56},{48,64},{56,72},{64,... | collective-permute-start | bytes 208904 | tf_op jit(solution)/shard_map/ppermute | solution.py:223
  52.7 0.0 collective-permute-done.3.refs_2_
  52.7 0.0 collective-permute-done.2.refs_1_
  52.8 2.4 %collective-permute-done.1.refs_0_ = bf16[272,128]{1,0:T(8,128)(2,1)S(1)} collective-permute-done((bf16[272,128]{1,0:T(8,128)(2,1)S(1)}, bf16[272,128]{1,0:T(8,128)(2,1)S(1)}, u32[]{:S(2)}, u32[]{:S(2)}) %collective-permute-start.1) | collective-permute-done | bytes 69664 | tf_op jit(solution)/shard_map/ppermute | solution.py:223
  55.2 0.1 round.3
  55.2 7.8 %collective-permute-start.4 = (bf16[272,128]{1,0:T(8,128)(2,1)S(1)}, bf16[272,128]{1,0:T(8,128)(2,1)S(1)}, u32[]{:S(2)}, u32[]{:S(2)}) collective-permute-start(bf16[272,128]{1,0:T(8,128)(2,1)S(1)} %get-tuple-element.23), channel_id=1, source_target_pairs={{0,64},{8,72},{16,80},{24,88},{32,96},{40,104},{48,112},{56,120},{... | collective-permute-start | bytes 208904 | tf_op jit(solution)/shard_map/ppermute | solution.py:223
  63.1 1.3 collective-permute-done.4.refs_0_
  64.5 7.7 %collective-permute-start.7 = (bf16[272,128]{1,0:T(8,128)(2,1)S(1)}, bf16[272,128]{1,0:T(8,128)(2,1)S(1)}, u32[]{:S(2)}, u32[]{:S(2)}) collective-permute-start(bf16[272,128]{1,0:T(8,128)(2,1)S(1)} %get-tuple-element.25), channel_id=1, source_target_pairs={{0,384},{8,392},{16,400},{24,408},{32,416},{40,424},{48,432},{56,4... | collective-permute-start | bytes 208904 | tf_op jit(solution)/shard_map/ppermute | solution.py:223
  72.2 1.5 collective-permute-start.6
  73.7 2.3 %collective-permute-start.5 = (bf16[272,128]{1,0:T(8,128)(2,1)S(1)}, bf16[272,128]{1,0:T(8,128)(2,1)S(1)}, u32[]{:S(2)}, u32[]{:S(2)}) collective-permute-start(bf16[272,128]{1,0:T(8,128)(2,1)S(1)} %get-tuple-element.25), channel_id=1, source_target_pairs={{0,128},{8,136},{16,144},{24,152},{32,160},{40,168},{48,176},{56,1... | collective-permute-start | bytes 208904 | tf_op jit(solution)/shard_map/ppermute | solution.py:223
  76.0 0.0 collective-permute-done.7.refs_2_
  76.0 0.0 collective-permute-done.6.refs_1_
  76.0 1.8 %collective-permute-done.5.refs_0_ = bf16[272,128]{1,0:T(8,128)(2,1)S(1)} collective-permute-done((bf16[272,128]{1,0:T(8,128)(2,1)S(1)}, bf16[272,128]{1,0:T(8,128)(2,1)S(1)}, u32[]{:S(2)}, u32[]{:S(2)}) %collective-permute-start.5) | collective-permute-done | bytes 69664 | tf_op jit(solution)/shard_map/ppermute | solution.py:223
  77.8 0.7 round.5
  78.5 4.7 %collective-permute-start.8 = (f32[272,128]{1,0:T(8,128)S(1)}, f32[272,128]{1,0:T(8,128)S(1)}, u32[]{:S(2)}, u32[]{:S(2)}) collective-permute-start(f32[272,128]{1,0:T(8,128)S(1)} %get-tuple-element.27.held_ref), channel_id=1, source_target_pairs={{0,8},{8,0},{16,24},{24,16},{32,40},{40,32},{48,56},{56,48},{64,72... | collective-permute-start | bytes 417800 | tf_op jit(solution)/shard_map/ppermute | solution.py:211
  83.3 0.9 collective-permute-done.8.held_other_ref
  84.2 0.0 all-to-all-done
  84.2 3.5 %memory.1 = (f32[1224,128]{1,0:T(8,128)S(1)}, bf16[64,16,128]{2,1,0:T(8,128)(2,1)}) custom-call(s32[1]{0:T(128)S(6)} %select_n.7.core_ref, f32[4]{0:T(128)S(1)} %add_divide_fusion.gate_ref, bf16[1024,1024]{1,0:T(8,128)(2,1)S(1)} %bitcast.12, f32[272,128]{1,0:T(8,128)S(1)} %moments.1.own_ref, f32[272,128]{1,0:T(8,128)S(1)} %collective-permute-done.other_ref, ...), custom_call_target="tpu_custom_call" | custom-call | flops 268435456 | bytes 3145728 | tf_op jit(solution)/shard_map/memory/pallas_call | solution.py:417
  87.8 0.8 copy-done.2
  88.6 9.4 %all-to-all-start.2 = ((bf16[64,16,128]{2,1,0:T(8,128)(2,1)}), bf16[64,16,128]{2,1,0:T(8,128)(2,1)S(1)}, u32[]{:S(2)}, u32[]{:S(2)}) async-start(bf16[64,16,128]{2,1,0:T(8,128)(2,1)} %get-tuple-element.33), calls=%async_computation.2 | async-start | bytes 524288 | tf_op jit(solution)/shard_map/all_to_all | solution.py:592
  98.0 7.5 %attention.2 = (bf16[1024,768]{1,0:T(8,128)(2,1)}, f32[1024,128]{1,0:T(8,128)}, f32[1024,128]{1,0:T(8,128)}, f32[8,128]{1,0:T(8,128)}) custom-call(f32[4]{0:T(128)} %copy-done.3, bf16[1024,1024]{1,0:T(8,128)(2,1)} %bitcast.13, bf16[1024,1024]{1,0:T(8,128)(2,1)} %bitcast.14, bf16[1024,256]{1,0:T(8,128)(2,1)} %bitcast.18, bf16[1024,256]{1,0:T(8,128)(2,1)} %bitcast.19, ...), custom_call_target="tpu_custom_call" | custom-call | flops 1342177280 | bytes 3145728 | tf_op jit(solution)/shard_map/attention/pallas_call | solution.py:331
  105.5 4.5 %all-to-all-done.2.in_ref = bf16[64,16,128]{2,1,0:T(8,128)(2,1)S(1)} async-done(((bf16[64,16,128]{2,1,0:T(8,128)(2,1)}), bf16[64,16,128]{2,1,0:T(8,128)(2,1)S(1)}, u32[]{:S(2)}, u32[]{:S(2)}) %all-to-all-start.2) | async-done | bytes 262176 | tf_op jit(solution)/shard_map/all_to_all | solution.py:592
  110.0 0.7 copy-done.5
  110.7 1.7 backward_scan.1
  112.4 0.6 copy-done.4
  113.0 6.0 %all-to-all-start.3 = ((f32[64,4,128]{2,1,0:T(4,128)}), f32[64,4,128]{2,1,0:T(4,128)S(1)}, u32[]{:S(2)}, u32[]{:S(2)}) async-start(f32[64,4,128]{2,1,0:T(4,128)} %get-tuple-element.35), calls=%async_computation.3 | async-start | bytes 262144 | tf_op jit(solution)/shard_map/all_to_all | solution.py:592
  119.0 7.5 %attention.3 = (bf16[1024,768]{1,0:T(8,128)(2,1)}, f32[1024,128]{1,0:T(8,128)}, f32[1024,128]{1,0:T(8,128)}, f32[8,128]{1,0:T(8,128)}) custom-call(f32[4]{0:T(128)} %copy-done.3, bf16[1024,1024]{1,0:T(8,128)(2,1)} %bitcast.15, bf16[1024,1024]{1,0:T(8,128)(2,1)} %bitcast.16, ...), custom_call_target="tpu_custom_call", output_to_operand_aliasing={{0}: (7, {}), {1}: (8, {}), {2}: (9, {})} | custom-call | flops 1342177280 | bytes 3145728 | tf_op jit(solution)/shard_map/attention/pallas_call | solution.py:331
  126.5 2.9 %all-to-all-done.3.cot_ref = f32[64,4,128]{2,1,0:T(4,128)S(1)} async-done(((f32[64,4,128]{2,1,0:T(4,128)}), f32[64,4,128]{2,1,0:T(4,128)S(1)}, u32[]{:S(2)}, u32[]{:S(2)}) %all-to-all-start.3) | async-done | bytes 131104 | tf_op jit(solution)/shard_map/all_to_all | solution.py:592
  129.4 0.7 copy-done.6
  130.0 2.8 %finish.1 = bf16[1024,768]{1,0:T(8,128)(2,1)} custom-call(bf16[1024,768]{1,0:T(8,128)(2,1)} %get-tuple-element.32.grads_ref, bf16[1024,256]{1,0:T(8,128)(2,1)} %bitcast.22, f32[64,4,128]{2,1,0:T(4,128)} %copy-done.6, f32[8,128]{1,0:T(8,128)} %copy-done.4, f32[1224,128]{1,0:T(8,128)} %copy-done.2, ...), custom_call_target="tpu_custom_call", output_to_operand_aliasing={{}: (0, {})} | custom-call | flops 167772160 | bytes 3145728 | tf_op jit(solution)/shard_map/finish/pallas_call | solution.py:503
  132.8 44.4 %all_to_all.25.refs_0_ = bf16[8,128,768]{2,1,0:T(8,128)(2,1)S(1)} all-to-all(bf16[8,128,768]{2,1,0:T(8,128)(2,1)} %bitcast.23), channel_id=1, replica_groups=mesh['seq'=64,'tp'=8] {'tp'}, dimensions={0} | all-to-all | bytes 3145728 | tf_op jit(solution)/shard_map/all_to_all | solution.py:588
  177.3 1.3 unpack_grads.1
  (14 shorter events, 0.1 us)
Async XLA Ops:
  2.6 22.4 %all-to-all-start.1 = ((bf16[8,128,256]{2,1,0:T(8,128)(2,1)}), bf16[8,128,256]{2,1,0:T(8,128)(2,1)S(1)}, u32[]{:S(2)}, u32[]{:S(2)}) async-start(bf16[8,128,256]{2,1,0:T(8,128)(2,1)} %pack_pair.1), calls=%async_computation.1 | async-start | bytes 1048576 | tf_op jit(solution)/shard_map/all_to_all | solution.py:582
  13.7 15.0 %copy-start.7 = (f32[2,4]{1,0:T(2,128)S(1)}, f32[2,4]{1,0:T(2,128)}, u32[]{:S(2)}) copy-start(f32[2,4]{1,0:T(2,128)} %param.10) | copy-start | bytes 100
  25.0 3.8 %copy-start.1 = (bf16[8,128,256]{2,1,0:T(8,128)(2,1)}, bf16[8,128,256]{2,1,0:T(8,128)(2,1)S(1)}, u32[]{:S(2)}) copy-start(bf16[8,128,256]{2,1,0:T(8,128)(2,1)S(1)} %all-to-all-done.1) | copy-start | bytes 1572868
  25.0 59.2 %all-to-all-start = ((bf16[8,128,1024]{2,1,0:T(8,128)(2,1)}), bf16[8,128,1024]{2,1,0:T(8,128)(2,1)S(1)}, u32[]{:S(2)}, u32[]{:S(2)}) async-start(bf16[8,128,1024]{2,1,0:T(8,128)(2,1)} %maximum_bitcast_fusion), calls=%async_computation | async-start | bytes 4194304 | tf_op jit(solution)/shard_map/all_to_all | solution.py:582
  28.6 54.6 %copy-start.8 = (f32[4]{0:T(128)S(1)}, f32[4]{0:T(128)}, u32[]{:S(2)}) copy-start(f32[4]{0:T(128)} %param.11) | copy-start | bytes 52
  29.2 6.6 %collective-permute-start = (f32[272,128]{1,0:T(8,128)S(1)}, f32[272,128]{1,0:T(8,128)S(1)}, u32[]{:S(2)}, u32[]{:S(2)}) collective-permute-start(f32[272,128]{1,0:T(8,128)S(1)} %moments.1.own_ref), channel_id=1, source_target_pairs={{0,8},{8,0},{16,24},{24,16},{32,40},{40,32},{48,56},{56,48},{64,72... | collective-permute-start | bytes 417800 | tf_op jit(solution)/shard_map/ppermute | solution.py:211
  35.9 16.9 %collective-permute-start.3 = (bf16[272,128]{1,0:T(8,128)(2,1)S(1)}, bf16[272,128]{1,0:T(8,128)(2,1)S(1)}, u32[]{:S(2)}, u32[]{:S(2)}) collective-permute-start(bf16[272,128]{1,0:T(8,128)(2,1)S(1)} %get-tuple-element.21), channel_id=1, source_target_pairs={{0,48},{8,56},{16,64},{24,72},{32,80},{40,88},{48,96},{56,104},{64... | collective-permute-start | bytes 208904 | tf_op jit(solution)/shard_map/ppermute | solution.py:223
  43.5 9.2 %collective-permute-start.2 = (bf16[272,128]{1,0:T(8,128)(2,1)S(1)}, bf16[272,128]{1,0:T(8,128)(2,1)S(1)}, u32[]{:S(2)}, u32[]{:S(2)}) collective-permute-start(bf16[272,128]{1,0:T(8,128)(2,1)S(1)} %get-tuple-element.21), channel_id=1, source_target_pairs={{0,32},{8,40},{16,48},{24,56},{32,64},{40,72},{48,80},{56,88},{64,... | collective-permute-start | bytes 208904 | tf_op jit(solution)/shard_map/ppermute | solution.py:223
  49.6 5.5 %collective-permute-start.1 = (bf16[272,128]{1,0:T(8,128)(2,1)S(1)}, bf16[272,128]{1,0:T(8,128)(2,1)S(1)}, u32[]{:S(2)}, u32[]{:S(2)}) collective-permute-start(bf16[272,128]{1,0:T(8,128)(2,1)S(1)} %get-tuple-element.21), channel_id=1, source_target_pairs={{0,16},{8,24},{16,32},{24,40},{32,48},{40,56},{48,64},{56,72},{64,... | collective-permute-start | bytes 208904 | tf_op jit(solution)/shard_map/ppermute | solution.py:223
  55.2 9.2 %collective-permute-start.4 = (bf16[272,128]{1,0:T(8,128)(2,1)S(1)}, bf16[272,128]{1,0:T(8,128)(2,1)S(1)}, u32[]{:S(2)}, u32[]{:S(2)}) collective-permute-start(bf16[272,128]{1,0:T(8,128)(2,1)S(1)} %get-tuple-element.23), channel_id=1, source_target_pairs={{0,64},{8,72},{16,80},{24,88},{32,96},{40,104},{48,112},{56,120},{... | collective-permute-start | bytes 208904 | tf_op jit(solution)/shard_map/ppermute | solution.py:223
  64.5 11.5 %collective-permute-start.7 = (bf16[272,128]{1,0:T(8,128)(2,1)S(1)}, bf16[272,128]{1,0:T(8,128)(2,1)S(1)}, u32[]{:S(2)}, u32[]{:S(2)}) collective-permute-start(bf16[272,128]{1,0:T(8,128)(2,1)S(1)} %get-tuple-element.25), channel_id=1, source_target_pairs={{0,384},{8,392},{16,400},{24,408},{32,416},{40,424},{48,432},{56,4... | collective-permute-start | bytes 208904 | tf_op jit(solution)/shard_map/ppermute | solution.py:223
  72.2 3.8 %collective-permute-start.6 = (bf16[272,128]{1,0:T(8,128)(2,1)S(1)}, bf16[272,128]{1,0:T(8,128)(2,1)S(1)}, u32[]{:S(2)}, u32[]{:S(2)}) collective-permute-start(bf16[272,128]{1,0:T(8,128)(2,1)S(1)} %get-tuple-element.25), channel_id=1, source_target_pairs={{0,256},{8,264},{16,272},{24,280},{32,288},{40,296},{48,304},{56,3... | collective-permute-start | bytes 208904 | tf_op jit(solution)/shard_map/ppermute | solution.py:223
  73.7 4.1 %collective-permute-start.5 = (bf16[272,128]{1,0:T(8,128)(2,1)S(1)}, bf16[272,128]{1,0:T(8,128)(2,1)S(1)}, u32[]{:S(2)}, u32[]{:S(2)}) collective-permute-start(bf16[272,128]{1,0:T(8,128)(2,1)S(1)} %get-tuple-element.25), channel_id=1, source_target_pairs={{0,128},{8,136},{16,144},{24,152},{32,160},{40,168},{48,176},{56,1... | collective-permute-start | bytes 208904 | tf_op jit(solution)/shard_map/ppermute | solution.py:223
  78.5 5.7 %collective-permute-start.8 = (f32[272,128]{1,0:T(8,128)S(1)}, f32[272,128]{1,0:T(8,128)S(1)}, u32[]{:S(2)}, u32[]{:S(2)}) collective-permute-start(f32[272,128]{1,0:T(8,128)S(1)} %get-tuple-element.27.held_ref), channel_id=1, source_target_pairs={{0,8},{8,0},{16,24},{24,16},{32,40},{40,32},{48,56},{56,48},{64,72... | collective-permute-start | bytes 417800 | tf_op jit(solution)/shard_map/ppermute | solution.py:211
  83.3 14.7 %copy-start.3 = (f32[4]{0:T(128)}, f32[4]{0:T(128)S(1)}, u32[]{:S(2)}) copy-start(f32[4]{0:T(128)S(1)} %add_divide_fusion.gate_ref) | copy-start | bytes 52
  84.2 13.8 %copy-start = (bf16[8,128,1024]{2,1,0:T(8,128)(2,1)}, bf16[8,128,1024]{2,1,0:T(8,128)(2,1)S(1)}, u32[]{:S(2)}) copy-start(bf16[8,128,1024]{2,1,0:T(8,128)(2,1)S(1)} %all-to-all-done) | copy-start | bytes 6291460
  87.8 0.8 copy-start.2
  88.6 21.4 %all-to-all-start.2 = ((bf16[64,16,128]{2,1,0:T(8,128)(2,1)}), bf16[64,16,128]{2,1,0:T(8,128)(2,1)S(1)}, u32[]{:S(2)}, u32[]{:S(2)}) async-start(bf16[64,16,128]{2,1,0:T(8,128)(2,1)} %get-tuple-element.33), calls=%async_computation.2 | async-start | bytes 524288 | tf_op jit(solution)/shard_map/all_to_all | solution.py:592
  110.0 0.7 copy-start.5
  112.4 0.6 copy-start.4
  113.0 16.4 %all-to-all-start.3 = ((f32[64,4,128]{2,1,0:T(4,128)}), f32[64,4,128]{2,1,0:T(4,128)S(1)}, u32[]{:S(2)}, u32[]{:S(2)}) async-start(f32[64,4,128]{2,1,0:T(4,128)} %get-tuple-element.35), calls=%async_computation.3 | async-start | bytes 262144 | tf_op jit(solution)/shard_map/all_to_all | solution.py:592
  129.4 0.7 copy-start.6

commit v4 on v3

--- a/solution.py
+++ b/solution.py
@@ -516,7 +516,7 @@
         out_specs=pl.BlockSpec((SEG, 2 * HD), lambda e: (e, 2)),
         out_shape=jax.ShapeDtypeStruct((2 * SEG, 6 * HD), BF16),
         input_output_aliases={0: 0},
-        compiler_params=params(60),
+        compiler_params=params(53),
         cost_estimate=cost(2 * 5 * 2 * SEG * HD * HD, 3 << 20, 2 * SEG * HD),
         name="finish",
     )(grads, kv, cot, norm, kept, kept, gk, gv)

time: 179 us -> 178 us (level)
  no operation moved by 1% of the time
where the time goes in v4:
time: 178 us; the launch traced here: 177 us
  starting transfers between devices  73.2 us (41%)
  blocking collectives  44.5 us (25%)
  Pallas kernels  27.3 us (15%)
  waiting for transfers between devices  26.2 us (15%)
  local copies, waits for them, and re-layouts  3.45 us (2%)
    all_to_all x1, blocking collectives, to_tokens(): return lax.all_to_all(blocks, 'tp', split_axis=0, concat_axis=0, tiled=True)  44.5 us
    ppermute x7, starting transfers between devices, exclusive_scan(): recv.append(lax.ppermute(send, 'seq', moves))  36.2 us
    all_to_all x2, starting transfers between devices, over_seq(): return lax.all_to_all(x, 'seq', split_axis=0, concat_axis=0, tiled=True)  15.5 us
    pallas_call x2, Pallas kernels, attention_call(): pl.pallas_call(attention_kernel, grid=(4,), in_specs=[pl.BlockSpec(memory...  14.9 us
    all_to_all x2, waiting for transfers between devices, to_heads(): lax.all_to_all(blocks, 'tp', split_axis=0, concat_axis=0, tiled=True)  11.3 us
    all_to_all x2, starting transfers between devices, to_heads(): lax.all_to_all(blocks, 'tp', split_axis=0, concat_axis=0, tiled=True)  11.3 us
    ppermute x2, starting transfers between devices, swap_cores(): lax.ppermute(x, 'seq', [(i, i ^ 1) for i in range(lax.axis_size('seq'))])  10.3 us
    all_to_all x2, waiting for transfers between devices, over_seq(): return lax.all_to_all(x, 'seq', split_axis=0, concat_axis=0, tiled=True)  7.37 us
  transfers between devices with their start and end apart: 13, of which 8 were waited for; matrix products, arithmetic and copies ran while one was open for 2% of the time, Pallas kernels for 9%

profile of v4, /device:TPU:1, one launch (start us, length us, event | category | flops | bytes accessed | tf_op | source)
XLA Modules:
  0.0 177.2 jit_solution(12415190943603566917)
XLA Ops:
  0.6 1.9 %pack_pair.1 = bf16[8,128,256]{2,1,0:T(8,128)(2,1)} custom-call(bf16[128,1024]{1,0:T(8,128)(2,1)} %refs_0_.1, bf16[128,1024]{1,0:T(8,128)(2,1)} %refs_1_.1), custom_call_target="tpu_custom_call" | custom-call | bytes 1048576 | tf_op jit(solution)/shard_map/pack_pair/pallas_call | solution.py:538
  2.6 7.7 %all-to-all-start.1 = ((bf16[8,128,256]{2,1,0:T(8,128)(2,1)}), bf16[8,128,256]{2,1,0:T(8,128)(2,1)S(1)}, u32[]{:S(2)}, u32[]{:S(2)}) async-start(bf16[8,128,256]{2,1,0:T(8,128)(2,1)} %pack_pair.1), calls=%async_computation.1 | async-start | bytes 1048576 | tf_op jit(solution)/shard_map/all_to_all | solution.py:582
  10.2 1.8 copy_bitcast_fusion
  12.0 1.6 maximum_bitcast_fusion
  13.7 11.3 %all-to-all-done.1 = bf16[8,128,256]{2,1,0:T(8,128)(2,1)S(1)} async-done(((bf16[8,128,256]{2,1,0:T(8,128)(2,1)}), bf16[8,128,256]{2,1,0:T(8,128)(2,1)S(1)}, u32[]{:S(2)}, u32[]{:S(2)}) %all-to-all-start.1) | async-done | bytes 524320 | tf_op jit(solution)/shard_map/all_to_all | solution.py:582
  25.0 3.6 %all-to-all-start = ((bf16[8,128,1024]{2,1,0:T(8,128)(2,1)}), bf16[8,128,1024]{2,1,0:T(8,128)(2,1)S(1)}, u32[]{:S(2)}, u32[]{:S(2)}) async-start(bf16[8,128,1024]{2,1,0:T(8,128)(2,1)} %maximum_bitcast_fusion), calls=%async_computation | async-start | bytes 4194304 | tf_op jit(solution)/shard_map/all_to_all | solution.py:582
  28.6 0.0 copy-start.7
  28.6 0.1 broadcast_in_dim.7
  28.7 0.1 broadcast_in_dim.8.rate_ref
  28.8 0.0 copy-done.1
  28.8 0.4 moments.1.own_ref
  29.2 5.6 %collective-permute-start = (f32[272,128]{1,0:T(8,128)S(1)}, f32[272,128]{1,0:T(8,128)S(1)}, u32[]{:S(2)}, u32[]{:S(2)}) collective-permute-start(f32[272,128]{1,0:T(8,128)S(1)} %moments.1.own_ref), channel_id=1, source_target_pairs={{0,8},{8,0},{16,24},{24,16},{32,40},{40,32},{48,56},{56,48},{64,72... | collective-permute-start | bytes 417800 | tf_op jit(solution)/shard_map/ppermute | solution.py:211
  34.8 1.0 collective-permute-done.other_ref
  35.8 0.1 chip_terms.1
  35.9 7.6 %collective-permute-start.3 = (bf16[272,128]{1,0:T(8,128)(2,1)S(1)}, bf16[272,128]{1,0:T(8,128)(2,1)S(1)}, u32[]{:S(2)}, u32[]{:S(2)}) collective-permute-start(bf16[272,128]{1,0:T(8,128)(2,1)S(1)} %get-tuple-element.21), channel_id=1, source_target_pairs={{0,48},{8,56},{16,64},{24,72},{32,80},{40,88},{48,96},{56,104},{64... | collective-permute-start | bytes 208904 | tf_op jit(solution)/shard_map/ppermute | solution.py:223
  43.5 6.1 %collective-permute-start.2 = (bf16[272,128]{1,0:T(8,128)(2,1)S(1)}, bf16[272,128]{1,0:T(8,128)(2,1)S(1)}, u32[]{:S(2)}, u32[]{:S(2)}) collective-permute-start(bf16[272,128]{1,0:T(8,128)(2,1)S(1)} %get-tuple-element.21), channel_id=1, source_target_pairs={{0,32},{8,40},{16,48},{24,56},{32,64},{40,72},{48,80},{56,88},{64,... | collective-permute-start | bytes 208904 | tf_op jit(solution)/shard_map/ppermute | solution.py:223
  49.6 3.1 %collective-permute-start.1 = (bf16[272,128]{1,0:T(8,128)(2,1)S(1)}, bf16[272,128]{1,0:T(8,128)(2,1)S(1)}, u32[]{:S(2)}, u32[]{:S(2)}) collective-permute-start(bf16[272,128]{1,0:T(8,128)(2,1)S(1)} %get-tuple-element.21), channel_id=1, source_target_pairs={{0,16},{8,24},{16,32},{24,40},{32,48},{40,56},{48,64},{56,72},{64,... | collective-permute-start | bytes 208904 | tf_op jit(solution)/shard_map/ppermute | solution.py:223
  52.7 0.0 collective-permute-done.3.refs_2_
  52.7 0.0 collective-permute-done.2.refs_1_
  52.8 2.4 %collective-permute-done.1.refs_0_ = bf16[272,128]{1,0:T(8,128)(2,1)S(1)} collective-permute-done((bf16[272,128]{1,0:T(8,128)(2,1)S(1)}, bf16[272,128]{1,0:T(8,128)(2,1)S(1)}, u32[]{:S(2)}, u32[]{:S(2)}) %collective-permute-start.1) | collective-permute-done | bytes 69664 | tf_op jit(solution)/shard_map/ppermute | solution.py:223
  55.2 0.1 round.3
  55.2 7.8 %collective-permute-start.4 = (bf16[272,128]{1,0:T(8,128)(2,1)S(1)}, bf16[272,128]{1,0:T(8,128)(2,1)S(1)}, u32[]{:S(2)}, u32[]{:S(2)}) collective-permute-start(bf16[272,128]{1,0:T(8,128)(2,1)S(1)} %get-tuple-element.23), channel_id=1, source_target_pairs={{0,64},{8,72},{16,80},{24,88},{32,96},{40,104},{48,112},{56,120},{... | collective-permute-start | bytes 208904 | tf_op jit(solution)/shard_map/ppermute | solution.py:223
  63.1 1.3 collective-permute-done.4.refs_0_
  64.5 7.7 %collective-permute-start.7 = (bf16[272,128]{1,0:T(8,128)(2,1)S(1)}, bf16[272,128]{1,0:T(8,128)(2,1)S(1)}, u32[]{:S(2)}, u32[]{:S(2)}) collective-permute-start(bf16[272,128]{1,0:T(8,128)(2,1)S(1)} %get-tuple-element.25), channel_id=1, source_target_pairs={{0,384},{8,392},{16,400},{24,408},{32,416},{40,424},{48,432},{56,4... | collective-permute-start | bytes 208904 | tf_op jit(solution)/shard_map/ppermute | solution.py:223
  72.2 1.5 collective-permute-start.6
  73.7 2.3 %collective-permute-start.5 = (bf16[272,128]{1,0:T(8,128)(2,1)S(1)}, bf16[272,128]{1,0:T(8,128)(2,1)S(1)}, u32[]{:S(2)}, u32[]{:S(2)}) collective-permute-start(bf16[272,128]{1,0:T(8,128)(2,1)S(1)} %get-tuple-element.25), channel_id=1, source_target_pairs={{0,128},{8,136},{16,144},{24,152},{32,160},{40,168},{48,176},{56,1... | collective-permute-start | bytes 208904 | tf_op jit(solution)/shard_map/ppermute | solution.py:223
  76.0 0.0 collective-permute-done.7.refs_2_
  76.0 0.0 collective-permute-done.6.refs_1_
  76.0 1.8 %collective-permute-done.5.refs_0_ = bf16[272,128]{1,0:T(8,128)(2,1)S(1)} collective-permute-done((bf16[272,128]{1,0:T(8,128)(2,1)S(1)}, bf16[272,128]{1,0:T(8,128)(2,1)S(1)}, u32[]{:S(2)}, u32[]{:S(2)}) %collective-permute-start.5) | collective-permute-done | bytes 69664 | tf_op jit(solution)/shard_map/ppermute | solution.py:223
  77.8 0.7 round.5
  78.5 4.7 %collective-permute-start.8 = (f32[272,128]{1,0:T(8,128)S(1)}, f32[272,128]{1,0:T(8,128)S(1)}, u32[]{:S(2)}, u32[]{:S(2)}) collective-permute-start(f32[272,128]{1,0:T(8,128)S(1)} %get-tuple-element.27.held_ref), channel_id=1, source_target_pairs={{0,8},{8,0},{16,24},{24,16},{32,40},{40,32},{48,56},{56,48},{64,72... | collective-permute-start | bytes 417800 | tf_op jit(solution)/shard_map/ppermute | solution.py:211
  83.3 0.9 collective-permute-done.8.held_other_ref
  84.2 0.0 all-to-all-done
  84.2 3.5 %memory.1 = (f32[1224,128]{1,0:T(8,128)S(1)}, bf16[64,16,128]{2,1,0:T(8,128)(2,1)}) custom-call(s32[1]{0:T(128)S(6)} %select_n.7.core_ref, f32[4]{0:T(128)S(1)} %add_divide_fusion.gate_ref, bf16[1024,1024]{1,0:T(8,128)(2,1)S(1)} %bitcast.12, f32[272,128]{1,0:T(8,128)S(1)} %moments.1.own_ref, f32[272,128]{1,0:T(8,128)S(1)} %collective-permute-done.other_ref, ...), custom_call_target="tpu_custom_call" | custom-call | flops 268435456 | bytes 3145728 | tf_op jit(solution)/shard_map/memory/pallas_call | solution.py:417
  87.8 0.8 copy-done.3
  88.6 9.4 %all-to-all-start.2 = ((bf16[64,16,128]{2,1,0:T(8,128)(2,1)}), bf16[64,16,128]{2,1,0:T(8,128)(2,1)S(1)}, u32[]{:S(2)}, u32[]{:S(2)}) async-start(bf16[64,16,128]{2,1,0:T(8,128)(2,1)} %get-tuple-element.33), calls=%async_computation.2 | async-start | bytes 524288 | tf_op jit(solution)/shard_map/all_to_all | solution.py:592
  98.0 7.4 %attention.2 = (bf16[1024,768]{1,0:T(8,128)(2,1)}, f32[1024,128]{1,0:T(8,128)}, f32[1024,128]{1,0:T(8,128)}, f32[8,128]{1,0:T(8,128)}) custom-call(f32[4]{0:T(128)} %copy-done.4, bf16[1024,1024]{1,0:T(8,128)(2,1)} %bitcast.13, bf16[1024,1024]{1,0:T(8,128)(2,1)} %bitcast.14, bf16[1024,256]{1,0:T(8,128)(2,1)} %bitcast.18, bf16[1024,256]{1,0:T(8,128)(2,1)} %bitcast.19, ...), custom_call_target="tpu_custom_call" | custom-call | flops 1342177280 | bytes 3145728 | tf_op jit(solution)/shard_map/attention/pallas_call | solution.py:331
  105.5 4.5 %all-to-all-done.2.in_ref = bf16[64,16,128]{2,1,0:T(8,128)(2,1)S(1)} async-done(((bf16[64,16,128]{2,1,0:T(8,128)(2,1)}), bf16[64,16,128]{2,1,0:T(8,128)(2,1)S(1)}, u32[]{:S(2)}, u32[]{:S(2)}) %all-to-all-start.2) | async-done | bytes 262176 | tf_op jit(solution)/shard_map/all_to_all | solution.py:592
  110.0 0.7 copy-done.5
  110.7 1.7 backward_scan.1
  112.4 6.0 %all-to-all-start.3 = ((f32[64,4,128]{2,1,0:T(4,128)}), f32[64,4,128]{2,1,0:T(4,128)S(1)}, u32[]{:S(2)}, u32[]{:S(2)}) async-start(f32[64,4,128]{2,1,0:T(4,128)} %get-tuple-element.35), calls=%async_computation.3 | async-start | bytes 262144 | tf_op jit(solution)/shard_map/all_to_all | solution.py:592
  118.4 0.0 copy-start.2
  118.4 7.5 %attention.3 = (bf16[1024,768]{1,0:T(8,128)(2,1)}, f32[1024,128]{1,0:T(8,128)}, f32[1024,128]{1,0:T(8,128)}, f32[8,128]{1,0:T(8,128)}) custom-call(f32[4]{0:T(128)} %copy-done.4, bf16[1024,1024]{1,0:T(8,128)(2,1)} %bitcast.15, bf16[1024,1024]{1,0:T(8,128)(2,1)} %bitcast.16, ...), custom_call_target="tpu_custom_call", output_to_operand_aliasing={{0}: (7, {}), {1}: (8, {}), {2}: (9, {})} | custom-call | flops 1342177280 | bytes 3145728 | tf_op jit(solution)/shard_map/attention/pallas_call | solution.py:331
  125.9 2.8 %all-to-all-done.3.cot_ref = f32[64,4,128]{2,1,0:T(4,128)S(1)} async-done(((f32[64,4,128]{2,1,0:T(4,128)}), f32[64,4,128]{2,1,0:T(4,128)S(1)}, u32[]{:S(2)}, u32[]{:S(2)}) %all-to-all-start.3) | async-done | bytes 131104 | tf_op jit(solution)/shard_map/all_to_all | solution.py:592
  128.8 0.0 copy-done.2
  128.8 2.6 %finish.1 = bf16[1024,768]{1,0:T(8,128)(2,1)} custom-call(bf16[1024,768]{1,0:T(8,128)(2,1)} %get-tuple-element.32.grads_ref, bf16[1024,256]{1,0:T(8,128)(2,1)S(1)} %bitcast.22, f32[64,4,128]{2,1,0:T(4,128)S(1)} %all-to-all-done.3.cot_ref, f32[8,128]{1,0:T(8,128)S(1)} %get-tuple-element.36.norm_ref, ...), custom_call_target="tpu_custom_call", output_to_operand_aliasing={{}: (0, {})} | custom-call | flops 167772160 | bytes 3145728 | tf_op jit(solution)/shard_map/finish/pallas_call | solution.py:503
  131.4 44.5 %all_to_all.25.refs_0_ = bf16[8,128,768]{2,1,0:T(8,128)(2,1)S(1)} all-to-all(bf16[8,128,768]{2,1,0:T(8,128)(2,1)} %bitcast.23), channel_id=1, replica_groups=mesh['seq'=64,'tp'=8] {'tp'}, dimensions={0} | all-to-all | bytes 3145728 | tf_op jit(solution)/shard_map/all_to_all | solution.py:588
  175.9 1.3 unpack_grads.1
  (12 shorter events, 0.1 us)
Async XLA Ops:
  2.6 22.4 %all-to-all-start.1 = ((bf16[8,128,256]{2,1,0:T(8,128)(2,1)}), bf16[8,128,256]{2,1,0:T(8,128)(2,1)S(1)}, u32[]{:S(2)}, u32[]{:S(2)}) async-start(bf16[8,128,256]{2,1,0:T(8,128)(2,1)} %pack_pair.1), calls=%async_computation.1 | async-start | bytes 1048576 | tf_op jit(solution)/shard_map/all_to_all | solution.py:582
  13.7 15.0 %copy-start.6 = (f32[2,4]{1,0:T(2,128)S(1)}, f32[2,4]{1,0:T(2,128)}, u32[]{:S(2)}) copy-start(f32[2,4]{1,0:T(2,128)} %param.10) | copy-start | bytes 100
  25.0 3.8 %copy-start.1 = (bf16[8,128,256]{2,1,0:T(8,128)(2,1)}, bf16[8,128,256]{2,1,0:T(8,128)(2,1)S(1)}, u32[]{:S(2)}) copy-start(bf16[8,128,256]{2,1,0:T(8,128)(2,1)S(1)} %all-to-all-done.1) | copy-start | bytes 1572868
  25.0 59.2 %all-to-all-start = ((bf16[8,128,1024]{2,1,0:T(8,128)(2,1)}), bf16[8,128,1024]{2,1,0:T(8,128)(2,1)S(1)}, u32[]{:S(2)}, u32[]{:S(2)}) async-start(bf16[8,128,1024]{2,1,0:T(8,128)(2,1)} %maximum_bitcast_fusion), calls=%async_computation | async-start | bytes 4194304 | tf_op jit(solution)/shard_map/all_to_all | solution.py:582
  28.6 54.6 %copy-start.7 = (f32[4]{0:T(128)S(1)}, f32[4]{0:T(128)}, u32[]{:S(2)}) copy-start(f32[4]{0:T(128)} %param.11) | copy-start | bytes 52
  29.2 6.6 %collective-permute-start = (f32[272,128]{1,0:T(8,128)S(1)}, f32[272,128]{1,0:T(8,128)S(1)}, u32[]{:S(2)}, u32[]{:S(2)}) collective-permute-start(f32[272,128]{1,0:T(8,128)S(1)} %moments.1.own_ref), channel_id=1, source_target_pairs={{0,8},{8,0},{16,24},{24,16},{32,40},{40,32},{48,56},{56,48},{64,72... | collective-permute-start | bytes 417800 | tf_op jit(solution)/shard_map/ppermute | solution.py:211
  35.9 16.9 %collective-permute-start.3 = (bf16[272,128]{1,0:T(8,128)(2,1)S(1)}, bf16[272,128]{1,0:T(8,128)(2,1)S(1)}, u32[]{:S(2)}, u32[]{:S(2)}) collective-permute-start(bf16[272,128]{1,0:T(8,128)(2,1)S(1)} %get-tuple-element.21), channel_id=1, source_target_pairs={{0,48},{8,56},{16,64},{24,72},{32,80},{40,88},{48,96},{56,104},{64... | collective-permute-start | bytes 208904 | tf_op jit(solution)/shard_map/ppermute | solution.py:223
  43.5 9.2 %collective-permute-start.2 = (bf16[272,128]{1,0:T(8,128)(2,1)S(1)}, bf16[272,128]{1,0:T(8,128)(2,1)S(1)}, u32[]{:S(2)}, u32[]{:S(2)}) collective-permute-start(bf16[272,128]{1,0:T(8,128)(2,1)S(1)} %get-tuple-element.21), channel_id=1, source_target_pairs={{0,32},{8,40},{16,48},{24,56},{32,64},{40,72},{48,80},{56,88},{64,... | collective-permute-start | bytes 208904 | tf_op jit(solution)/shard_map/ppermute | solution.py:223
  49.6 5.5 %collective-permute-start.1 = (bf16[272,128]{1,0:T(8,128)(2,1)S(1)}, bf16[272,128]{1,0:T(8,128)(2,1)S(1)}, u32[]{:S(2)}, u32[]{:S(2)}) collective-permute-start(bf16[272,128]{1,0:T(8,128)(2,1)S(1)} %get-tuple-element.21), channel_id=1, source_target_pairs={{0,16},{8,24},{16,32},{24,40},{32,48},{40,56},{48,64},{56,72},{64,... | collective-permute-start | bytes 208904 | tf_op jit(solution)/shard_map/ppermute | solution.py:223
  55.2 9.2 %collective-permute-start.4 = (bf16[272,128]{1,0:T(8,128)(2,1)S(1)}, bf16[272,128]{1,0:T(8,128)(2,1)S(1)}, u32[]{:S(2)}, u32[]{:S(2)}) collective-permute-start(bf16[272,128]{1,0:T(8,128)(2,1)S(1)} %get-tuple-element.23), channel_id=1, source_target_pairs={{0,64},{8,72},{16,80},{24,88},{32,96},{40,104},{48,112},{56,120},{... | collective-permute-start | bytes 208904 | tf_op jit(solution)/shard_map/ppermute | solution.py:223
  64.5 11.5 %collective-permute-start.7 = (bf16[272,128]{1,0:T(8,128)(2,1)S(1)}, bf16[272,128]{1,0:T(8,128)(2,1)S(1)}, u32[]{:S(2)}, u32[]{:S(2)}) collective-permute-start(bf16[272,128]{1,0:T(8,128)(2,1)S(1)} %get-tuple-element.25), channel_id=1, source_target_pairs={{0,384},{8,392},{16,400},{24,408},{32,416},{40,424},{48,432},{56,4... | collective-permute-start | bytes 208904 | tf_op jit(solution)/shard_map/ppermute | solution.py:223
  72.2 3.8 %collective-permute-start.6 = (bf16[272,128]{1,0:T(8,128)(2,1)S(1)}, bf16[272,128]{1,0:T(8,128)(2,1)S(1)}, u32[]{:S(2)}, u32[]{:S(2)}) collective-permute-start(bf16[272,128]{1,0:T(8,128)(2,1)S(1)} %get-tuple-element.25), channel_id=1, source_target_pairs={{0,256},{8,264},{16,272},{24,280},{32,288},{40,296},{48,304},{56,3... | collective-permute-start | bytes 208904 | tf_op jit(solution)/shard_map/ppermute | solution.py:223
  73.7 4.1 %collective-permute-start.5 = (bf16[272,128]{1,0:T(8,128)(2,1)S(1)}, bf16[272,128]{1,0:T(8,128)(2,1)S(1)}, u32[]{:S(2)}, u32[]{:S(2)}) collective-permute-start(bf16[272,128]{1,0:T(8,128)(2,1)S(1)} %get-tuple-element.25), channel_id=1, source_target_pairs={{0,128},{8,136},{16,144},{24,152},{32,160},{40,168},{48,176},{56,1... | collective-permute-start | bytes 208904 | tf_op jit(solution)/shard_map/ppermute | solution.py:223
  78.5 5.7 %collective-permute-start.8 = (f32[272,128]{1,0:T(8,128)S(1)}, f32[272,128]{1,0:T(8,128)S(1)}, u32[]{:S(2)}, u32[]{:S(2)}) collective-permute-start(f32[272,128]{1,0:T(8,128)S(1)} %get-tuple-element.27.held_ref), channel_id=1, source_target_pairs={{0,8},{8,0},{16,24},{24,16},{32,40},{40,32},{48,56},{56,48},{64,72... | collective-permute-start | bytes 417800 | tf_op jit(solution)/shard_map/ppermute | solution.py:211
  83.3 14.7 %copy-start.4 = (f32[4]{0:T(128)}, f32[4]{0:T(128)S(1)}, u32[]{:S(2)}) copy-start(f32[4]{0:T(128)S(1)} %add_divide_fusion.gate_ref) | copy-start | bytes 52
  84.2 13.8 %copy-start = (bf16[8,128,1024]{2,1,0:T(8,128)(2,1)}, bf16[8,128,1024]{2,1,0:T(8,128)(2,1)S(1)}, u32[]{:S(2)}) copy-start(bf16[8,128,1024]{2,1,0:T(8,128)(2,1)S(1)} %all-to-all-done) | copy-start | bytes 6291460
  87.8 0.8 copy-start.3
  88.6 21.4 %all-to-all-start.2 = ((bf16[64,16,128]{2,1,0:T(8,128)(2,1)}), bf16[64,16,128]{2,1,0:T(8,128)(2,1)S(1)}, u32[]{:S(2)}, u32[]{:S(2)}) async-start(bf16[64,16,128]{2,1,0:T(8,128)(2,1)} %get-tuple-element.33), calls=%async_computation.2 | async-start | bytes 524288 | tf_op jit(solution)/shard_map/all_to_all | solution.py:592
  110.0 0.7 copy-start.5
  112.4 16.4 %all-to-all-start.3 = ((f32[64,4,128]{2,1,0:T(4,128)}), f32[64,4,128]{2,1,0:T(4,128)S(1)}, u32[]{:S(2)}, u32[]{:S(2)}) async-start(f32[64,4,128]{2,1,0:T(4,128)} %get-tuple-element.35), calls=%async_computation.3 | async-start | bytes 262144 | tf_op jit(solution)/shard_map/all_to_all | solution.py:592
  118.4 10.4 %copy-start.2 = (bf16[8,128,256]{2,1,0:T(8,128)(2,1)S(1)}, bf16[8,128,256]{2,1,0:T(8,128)(2,1)}, u32[]{:S(2)}) copy-start(bf16[8,128,256]{2,1,0:T(8,128)(2,1)} %copy-done.1) | copy-start | bytes 1572868

commit v5 on v4

--- a/solution.py
+++ b/solution.py
@@ -349,7 +349,7 @@
             jax.ShapeDtypeStruct((8, HD), F32),
         ),
         input_output_aliases={7 + i: i for i in range(len(earlier))},
-        compiler_params=params(60),
+        compiler_params=params(53),
         cost_estimate=cost(4 * 5 * 2 * SEG * SEG * HD, 3 << 20, 4 * SEG * SEG),
         name="attention",
     )(gates, qd, qd, kv, kv, kept, kept, *earlier)

time: 178 us -> 177 us (level)
  no operation moved by 1% of the time
where the time goes in v5:
time: 177 us; the launch traced here: 176 us
  starting transfers between devices  73.2 us (41%)
  blocking collectives  44.4 us (25%)
  Pallas kernels  27.1 us (15%)
  waiting for transfers between devices  25.6 us (14%)
  local copies, waits for them, and re-layouts  3.56 us (2%)
    all_to_all x1, blocking collectives, to_tokens(): return lax.all_to_all(blocks, 'tp', split_axis=0, concat_axis=0, tiled=True)  44.4 us
    ppermute x7, starting transfers between devices, exclusive_scan(): recv.append(lax.ppermute(send, 'seq', moves))  36.2 us
    all_to_all x2, starting transfers between devices, over_seq(): return lax.all_to_all(x, 'seq', split_axis=0, concat_axis=0, tiled=True)  15.5 us
    pallas_call x2, Pallas kernels, attention_call(): pl.pallas_call(attention_kernel, grid=(4,), in_specs=[pl.BlockSpec(memory...  14.8 us
    all_to_all x2, waiting for transfers between devices, to_heads(): lax.all_to_all(blocks, 'tp', split_axis=0, concat_axis=0, tiled=True)  11.3 us
    all_to_all x2, starting transfers between devices, to_heads(): lax.all_to_all(blocks, 'tp', split_axis=0, concat_axis=0, tiled=True)  11.3 us
    ppermute x2, starting transfers between devices, swap_cores(): lax.ppermute(x, 'seq', [(i, i ^ 1) for i in range(lax.axis_size('seq'))])  10.3 us
    all_to_all x2, waiting for transfers between devices, over_seq(): return lax.all_to_all(x, 'seq', split_axis=0, concat_axis=0, tiled=True)  6.77 us
  transfers between devices with their start and end apart: 13, of which 8 were waited for; matrix products, arithmetic and copies ran while one was open for 2% of the time, Pallas kernels for 9%

profile of v5, /device:TPU:1, one launch (start us, length us, event | category | flops | bytes accessed | tf_op | source)
XLA Modules:
  0.0 176.4 jit_solution(5363017635937948030)
XLA Ops:
  0.6 1.9 %pack_pair.1 = bf16[8,128,256]{2,1,0:T(8,128)(2,1)} custom-call(bf16[128,1024]{1,0:T(8,128)(2,1)} %refs_0_.1, bf16[128,1024]{1,0:T(8,128)(2,1)} %refs_1_.1), custom_call_target="tpu_custom_call" | custom-call | bytes 1048576 | tf_op jit(solution)/shard_map/pack_pair/pallas_call | solution.py:538
  2.6 7.7 %all-to-all-start.1 = ((bf16[8,128,256]{2,1,0:T(8,128)(2,1)}), bf16[8,128,256]{2,1,0:T(8,128)(2,1)S(1)}, u32[]{:S(2)}, u32[]{:S(2)}) async-start(bf16[8,128,256]{2,1,0:T(8,128)(2,1)} %pack_pair.1), calls=%async_computation.1 | async-start | bytes 1048576 | tf_op jit(solution)/shard_map/all_to_all | solution.py:582
  10.2 1.8 copy_bitcast_fusion
  12.0 1.6 maximum_bitcast_fusion
  13.7 11.3 %all-to-all-done.1 = bf16[8,128,256]{2,1,0:T(8,128)(2,1)S(1)} async-done(((bf16[8,128,256]{2,1,0:T(8,128)(2,1)}), bf16[8,128,256]{2,1,0:T(8,128)(2,1)S(1)}, u32[]{:S(2)}, u32[]{:S(2)}) %all-to-all-start.1) | async-done | bytes 524320 | tf_op jit(solution)/shard_map/all_to_all | solution.py:582
  25.0 3.6 %all-to-all-start = ((bf16[8,128,1024]{2,1,0:T(8,128)(2,1)}), bf16[8,128,1024]{2,1,0:T(8,128)(2,1)S(1)}, u32[]{:S(2)}, u32[]{:S(2)}) async-start(bf16[8,128,1024]{2,1,0:T(8,128)(2,1)} %maximum_bitcast_fusion), calls=%async_computation | async-start | bytes 4194304 | tf_op jit(solution)/shard_map/all_to_all | solution.py:582
  28.6 0.0 copy-done.5
  28.6 0.0 copy-start.6
  28.6 0.1 broadcast_in_dim.7
  28.7 0.1 broadcast_in_dim.8.rate_ref
  28.8 0.0 copy-done.1
  28.8 0.4 moments.1.own_ref
  29.2 5.6 %collective-permute-start = (f32[272,128]{1,0:T(8,128)S(1)}, f32[272,128]{1,0:T(8,128)S(1)}, u32[]{:S(2)}, u32[]{:S(2)}) collective-permute-start(f32[272,128]{1,0:T(8,128)S(1)} %moments.1.own_ref), channel_id=1, source_target_pairs={{0,8},{8,0},{16,24},{24,16},{32,40},{40,32},{48,56},{56,48},{64,72... | collective-permute-start | bytes 417800 | tf_op jit(solution)/shard_map/ppermute | solution.py:211
  34.8 1.0 collective-permute-done.other_ref
  35.8 0.1 chip_terms.1
  35.9 7.6 %collective-permute-start.3 = (bf16[272,128]{1,0:T(8,128)(2,1)S(1)}, bf16[272,128]{1,0:T(8,128)(2,1)S(1)}, u32[]{:S(2)}, u32[]{:S(2)}) collective-permute-start(bf16[272,128]{1,0:T(8,128)(2,1)S(1)} %get-tuple-element.21), channel_id=1, source_target_pairs={{0,48},{8,56},{16,64},{24,72},{32,80},{40,88},{48,96},{56,104},{64... | collective-permute-start | bytes 208904 | tf_op jit(solution)/shard_map/ppermute | solution.py:223
  43.5 6.1 %collective-permute-start.2 = (bf16[272,128]{1,0:T(8,128)(2,1)S(1)}, bf16[272,128]{1,0:T(8,128)(2,1)S(1)}, u32[]{:S(2)}, u32[]{:S(2)}) collective-permute-start(bf16[272,128]{1,0:T(8,128)(2,1)S(1)} %get-tuple-element.21), channel_id=1, source_target_pairs={{0,32},{8,40},{16,48},{24,56},{32,64},{40,72},{48,80},{56,88},{64,... | collective-permute-start | bytes 208904 | tf_op jit(solution)/shard_map/ppermute | solution.py:223
  49.6 3.1 %collective-permute-start.1 = (bf16[272,128]{1,0:T(8,128)(2,1)S(1)}, bf16[272,128]{1,0:T(8,128)(2,1)S(1)}, u32[]{:S(2)}, u32[]{:S(2)}) collective-permute-start(bf16[272,128]{1,0:T(8,128)(2,1)S(1)} %get-tuple-element.21), channel_id=1, source_target_pairs={{0,16},{8,24},{16,32},{24,40},{32,48},{40,56},{48,64},{56,72},{64,... | collective-permute-start | bytes 208904 | tf_op jit(solution)/shard_map/ppermute | solution.py:223
  52.7 0.0 collective-permute-done.3.refs_2_
  52.7 0.0 collective-permute-done.2.refs_1_
  52.8 2.4 %collective-permute-done.1.refs_0_ = bf16[272,128]{1,0:T(8,128)(2,1)S(1)} collective-permute-done((bf16[272,128]{1,0:T(8,128)(2,1)S(1)}, bf16[272,128]{1,0:T(8,128)(2,1)S(1)}, u32[]{:S(2)}, u32[]{:S(2)}) %collective-permute-start.1) | collective-permute-done | bytes 69664 | tf_op jit(solution)/shard_map/ppermute | solution.py:223
  55.2 0.1 round.3
  55.2 7.8 %collective-permute-start.4 = (bf16[272,128]{1,0:T(8,128)(2,1)S(1)}, bf16[272,128]{1,0:T(8,128)(2,1)S(1)}, u32[]{:S(2)}, u32[]{:S(2)}) collective-permute-start(bf16[272,128]{1,0:T(8,128)(2,1)S(1)} %get-tuple-element.23), channel_id=1, source_target_pairs={{0,64},{8,72},{16,80},{24,88},{32,96},{40,104},{48,112},{56,120},{... | collective-permute-start | bytes 208904 | tf_op jit(solution)/shard_map/ppermute | solution.py:223
  63.1 1.3 collective-permute-done.4.refs_0_
  64.5 7.7 %collective-permute-start.7 = (bf16[272,128]{1,0:T(8,128)(2,1)S(1)}, bf16[272,128]{1,0:T(8,128)(2,1)S(1)}, u32[]{:S(2)}, u32[]{:S(2)}) collective-permute-start(bf16[272,128]{1,0:T(8,128)(2,1)S(1)} %get-tuple-element.25), channel_id=1, source_target_pairs={{0,384},{8,392},{16,400},{24,408},{32,416},{40,424},{48,432},{56,4... | collective-permute-start | bytes 208904 | tf_op jit(solution)/shard_map/ppermute | solution.py:223
  72.2 1.5 collective-permute-start.6
  73.7 2.3 %collective-permute-start.5 = (bf16[272,128]{1,0:T(8,128)(2,1)S(1)}, bf16[272,128]{1,0:T(8,128)(2,1)S(1)}, u32[]{:S(2)}, u32[]{:S(2)}) collective-permute-start(bf16[272,128]{1,0:T(8,128)(2,1)S(1)} %get-tuple-element.25), channel_id=1, source_target_pairs={{0,128},{8,136},{16,144},{24,152},{32,160},{40,168},{48,176},{56,1... | collective-permute-start | bytes 208904 | tf_op jit(solution)/shard_map/ppermute | solution.py:223
  76.0 0.0 collective-permute-done.7.refs_2_
  76.0 0.0 collective-permute-done.6.refs_1_
  76.0 1.8 %collective-permute-done.5.refs_0_ = bf16[272,128]{1,0:T(8,128)(2,1)S(1)} collective-permute-done((bf16[272,128]{1,0:T(8,128)(2,1)S(1)}, bf16[272,128]{1,0:T(8,128)(2,1)S(1)}, u32[]{:S(2)}, u32[]{:S(2)}) %collective-permute-start.5) | collective-permute-done | bytes 69664 | tf_op jit(solution)/shard_map/ppermute | solution.py:223
  77.8 0.7 round.5
  78.5 4.7 %collective-permute-start.8 = (f32[272,128]{1,0:T(8,128)S(1)}, f32[272,128]{1,0:T(8,128)S(1)}, u32[]{:S(2)}, u32[]{:S(2)}) collective-permute-start(f32[272,128]{1,0:T(8,128)S(1)} %get-tuple-element.27.held_ref), channel_id=1, source_target_pairs={{0,8},{8,0},{16,24},{24,16},{32,40},{40,32},{48,56},{56,48},{64,72... | collective-permute-start | bytes 417800 | tf_op jit(solution)/shard_map/ppermute | solution.py:211
  83.3 1.0 collective-permute-done.8.held_other_ref
  84.2 0.0 all-to-all-done
  84.2 3.5 %memory.1 = (f32[1224,128]{1,0:T(8,128)S(1)}, bf16[64,16,128]{2,1,0:T(8,128)(2,1)}) custom-call(s32[1]{0:T(128)S(6)} %select_n.7.core_ref, f32[4]{0:T(128)S(1)} %add_divide_fusion.gate_ref, bf16[1024,1024]{1,0:T(8,128)(2,1)S(1)} %bitcast.12, f32[272,128]{1,0:T(8,128)S(1)} %moments.1.own_ref, f32[272,128]{1,0:T(8,128)S(1)} %collective-permute-done.other_ref, ...), custom_call_target="tpu_custom_call" | custom-call | flops 268435456 | bytes 3145728 | tf_op jit(solution)/shard_map/memory/pallas_call | solution.py:417
  87.8 0.8 copy-done.3
  88.6 9.4 %all-to-all-start.2 = ((bf16[64,16,128]{2,1,0:T(8,128)(2,1)}), bf16[64,16,128]{2,1,0:T(8,128)(2,1)S(1)}, u32[]{:S(2)}, u32[]{:S(2)}) async-start(bf16[64,16,128]{2,1,0:T(8,128)(2,1)} %get-tuple-element.33), calls=%async_computation.2 | async-start | bytes 524288 | tf_op jit(solution)/shard_map/all_to_all | solution.py:592
  98.0 7.4 %attention.2 = (bf16[1024,768]{1,0:T(8,128)(2,1)}, f32[1024,128]{1,0:T(8,128)S(1)}, f32[1024,128]{1,0:T(8,128)}, f32[8,128]{1,0:T(8,128)S(1)}) custom-call(f32[4]{0:T(128)S(1)} %add_divide_fusion.gate_ref, bf16[1024,1024]{1,0:T(8,128)(2,1)} %bitcast.13, bf16[1024,1024]{1,0:T(8,128)(2,1)} %bitcast.14, bf16[1024,256]{1,0:T(8,128)(2,1)} %bitcast.18, ...), custom_call_target="tpu_custom_call" | custom-call | flops 1342177280 | bytes 3145728 | tf_op jit(solution)/shard_map/attention/pallas_call | solution.py:331
  105.4 4.6 %all-to-all-done.2.in_ref = bf16[64,16,128]{2,1,0:T(8,128)(2,1)S(1)} async-done(((bf16[64,16,128]{2,1,0:T(8,128)(2,1)}), bf16[64,16,128]{2,1,0:T(8,128)(2,1)S(1)}, u32[]{:S(2)}, u32[]{:S(2)}) %all-to-all-start.2) | async-done | bytes 262176 | tf_op jit(solution)/shard_map/all_to_all | solution.py:592
  110.0 1.7 backward_scan.1
  111.7 6.0 %all-to-all-start.3 = ((f32[64,4,128]{2,1,0:T(4,128)}), f32[64,4,128]{2,1,0:T(4,128)S(1)}, u32[]{:S(2)}, u32[]{:S(2)}) async-start(f32[64,4,128]{2,1,0:T(4,128)} %get-tuple-element.35), calls=%async_computation.3 | async-start | bytes 262144 | tf_op jit(solution)/shard_map/all_to_all | solution.py:592
  117.7 7.4 %attention.3 = (bf16[1024,768]{1,0:T(8,128)(2,1)}, f32[1024,128]{1,0:T(8,128)S(1)}, f32[1024,128]{1,0:T(8,128)}, f32[8,128]{1,0:T(8,128)}) custom-call(f32[4]{0:T(128)S(1)} %add_divide_fusion.gate_ref, bf16[1024,1024]{1,0:T(8,128)(2,1)} %bitcast.15, bf16[1024,1024]{1,0:T(8,128)(2,1)} %bitcast.16, ...), custom_call_target="tpu_custom_call", output_to_operand_aliasing={{0}: (7, {}), {1}: (8, {}), {2}: (9, {})} | custom-call | flops 1342177280 | bytes 3145728 | tf_op jit(solution)/shard_map/attention/pallas_call | solution.py:331
  125.1 0.0 copy-start.4
  125.1 0.8 copy-done.4
  125.9 2.1 %all-to-all-done.3.cot_ref = f32[64,4,128]{2,1,0:T(4,128)S(1)} async-done(((f32[64,4,128]{2,1,0:T(4,128)}), f32[64,4,128]{2,1,0:T(4,128)S(1)}, u32[]{:S(2)}, u32[]{:S(2)}) %all-to-all-start.3) | async-done | bytes 131104 | tf_op jit(solution)/shard_map/all_to_all | solution.py:592
  128.1 2.6 %finish.1 = bf16[1024,768]{1,0:T(8,128)(2,1)} custom-call(bf16[1024,768]{1,0:T(8,128)(2,1)} %get-tuple-element.32.grads_ref, bf16[1024,256]{1,0:T(8,128)(2,1)S(1)} %bitcast.22, f32[64,4,128]{2,1,0:T(4,128)S(1)} %all-to-all-done.3.cot_ref, f32[8,128]{1,0:T(8,128)S(1)} %get-tuple-element.36.norm_ref, ...), custom_call_target="tpu_custom_call", output_to_operand_aliasing={{}: (0, {})} | custom-call | flops 167772160 | bytes 3145728 | tf_op jit(solution)/shard_map/finish/pallas_call | solution.py:503
  130.7 44.4 %all_to_all.25.refs_0_ = bf16[8,128,768]{2,1,0:T(8,128)(2,1)S(1)} all-to-all(bf16[8,128,768]{2,1,0:T(8,128)(2,1)} %bitcast.23), channel_id=1, replica_groups=mesh['seq'=64,'tp'=8] {'tp'}, dimensions={0} | all-to-all | bytes 3145728 | tf_op jit(solution)/shard_map/all_to_all | solution.py:588
  175.1 1.3 unpack_grads.1
  (10 shorter events, 0.1 us)
Async XLA Ops:
  2.6 22.4 %all-to-all-start.1 = ((bf16[8,128,256]{2,1,0:T(8,128)(2,1)}), bf16[8,128,256]{2,1,0:T(8,128)(2,1)S(1)}, u32[]{:S(2)}, u32[]{:S(2)}) async-start(bf16[8,128,256]{2,1,0:T(8,128)(2,1)} %pack_pair.1), calls=%async_computation.1 | async-start | bytes 1048576 | tf_op jit(solution)/shard_map/all_to_all | solution.py:582
  13.7 14.9 %copy-start.5 = (f32[2,4]{1,0:T(2,128)S(1)}, f32[2,4]{1,0:T(2,128)}, u32[]{:S(2)}) copy-start(f32[2,4]{1,0:T(2,128)} %param.10) | copy-start | bytes 100
  25.0 3.8 %copy-start.1 = (bf16[8,128,256]{2,1,0:T(8,128)(2,1)}, bf16[8,128,256]{2,1,0:T(8,128)(2,1)S(1)}, u32[]{:S(2)}) copy-start(bf16[8,128,256]{2,1,0:T(8,128)(2,1)S(1)} %all-to-all-done.1) | copy-start | bytes 1572868
  25.0 59.2 %all-to-all-start = ((bf16[8,128,1024]{2,1,0:T(8,128)(2,1)}), bf16[8,128,1024]{2,1,0:T(8,128)(2,1)S(1)}, u32[]{:S(2)}, u32[]{:S(2)}) async-start(bf16[8,128,1024]{2,1,0:T(8,128)(2,1)} %maximum_bitcast_fusion), calls=%async_computation | async-start | bytes 4194304 | tf_op jit(solution)/shard_map/all_to_all | solution.py:582
  28.6 54.6 %copy-start.6 = (f32[4]{0:T(128)S(1)}, f32[4]{0:T(128)}, u32[]{:S(2)}) copy-start(f32[4]{0:T(128)} %param.11) | copy-start | bytes 52
  29.2 6.6 %collective-permute-start = (f32[272,128]{1,0:T(8,128)S(1)}, f32[272,128]{1,0:T(8,128)S(1)}, u32[]{:S(2)}, u32[]{:S(2)}) collective-permute-start(f32[272,128]{1,0:T(8,128)S(1)} %moments.1.own_ref), channel_id=1, source_target_pairs={{0,8},{8,0},{16,24},{24,16},{32,40},{40,32},{48,56},{56,48},{64,72... | collective-permute-start | bytes 417800 | tf_op jit(solution)/shard_map/ppermute | solution.py:211
  35.9 16.9 %collective-permute-start.3 = (bf16[272,128]{1,0:T(8,128)(2,1)S(1)}, bf16[272,128]{1,0:T(8,128)(2,1)S(1)}, u32[]{:S(2)}, u32[]{:S(2)}) collective-permute-start(bf16[272,128]{1,0:T(8,128)(2,1)S(1)} %get-tuple-element.21), channel_id=1, source_target_pairs={{0,48},{8,56},{16,64},{24,72},{32,80},{40,88},{48,96},{56,104},{64... | collective-permute-start | bytes 208904 | tf_op jit(solution)/shard_map/ppermute | solution.py:223
  43.5 9.2 %collective-permute-start.2 = (bf16[272,128]{1,0:T(8,128)(2,1)S(1)}, bf16[272,128]{1,0:T(8,128)(2,1)S(1)}, u32[]{:S(2)}, u32[]{:S(2)}) collective-permute-start(bf16[272,128]{1,0:T(8,128)(2,1)S(1)} %get-tuple-element.21), channel_id=1, source_target_pairs={{0,32},{8,40},{16,48},{24,56},{32,64},{40,72},{48,80},{56,88},{64,... | collective-permute-start | bytes 208904 | tf_op jit(solution)/shard_map/ppermute | solution.py:223
  49.6 5.5 %collective-permute-start.1 = (bf16[272,128]{1,0:T(8,128)(2,1)S(1)}, bf16[272,128]{1,0:T(8,128)(2,1)S(1)}, u32[]{:S(2)}, u32[]{:S(2)}) collective-permute-start(bf16[272,128]{1,0:T(8,128)(2,1)S(1)} %get-tuple-element.21), channel_id=1, source_target_pairs={{0,16},{8,24},{16,32},{24,40},{32,48},{40,56},{48,64},{56,72},{64,... | collective-permute-start | bytes 208904 | tf_op jit(solution)/shard_map/ppermute | solution.py:223
  55.2 9.2 %collective-permute-start.4 = (bf16[272,128]{1,0:T(8,128)(2,1)S(1)}, bf16[272,128]{1,0:T(8,128)(2,1)S(1)}, u32[]{:S(2)}, u32[]{:S(2)}) collective-permute-start(bf16[272,128]{1,0:T(8,128)(2,1)S(1)} %get-tuple-element.23), channel_id=1, source_target_pairs={{0,64},{8,72},{16,80},{24,88},{32,96},{40,104},{48,112},{56,120},{... | collective-permute-start | bytes 208904 | tf_op jit(solution)/shard_map/ppermute | solution.py:223
  64.5 11.5 %collective-permute-start.7 = (bf16[272,128]{1,0:T(8,128)(2,1)S(1)}, bf16[272,128]{1,0:T(8,128)(2,1)S(1)}, u32[]{:S(2)}, u32[]{:S(2)}) collective-permute-start(bf16[272,128]{1,0:T(8,128)(2,1)S(1)} %get-tuple-element.25), channel_id=1, source_target_pairs={{0,384},{8,392},{16,400},{24,408},{32,416},{40,424},{48,432},{56,4... | collective-permute-start | bytes 208904 | tf_op jit(solution)/shard_map/ppermute | solution.py:223
  72.2 3.8 %collective-permute-start.6 = (bf16[272,128]{1,0:T(8,128)(2,1)S(1)}, bf16[272,128]{1,0:T(8,128)(2,1)S(1)}, u32[]{:S(2)}, u32[]{:S(2)}) collective-permute-start(bf16[272,128]{1,0:T(8,128)(2,1)S(1)} %get-tuple-element.25), channel_id=1, source_target_pairs={{0,256},{8,264},{16,272},{24,280},{32,288},{40,296},{48,304},{56,3... | collective-permute-start | bytes 208904 | tf_op jit(solution)/shard_map/ppermute | solution.py:223
  73.7 4.1 %collective-permute-start.5 = (bf16[272,128]{1,0:T(8,128)(2,1)S(1)}, bf16[272,128]{1,0:T(8,128)(2,1)S(1)}, u32[]{:S(2)}, u32[]{:S(2)}) collective-permute-start(bf16[272,128]{1,0:T(8,128)(2,1)S(1)} %get-tuple-element.25), channel_id=1, source_target_pairs={{0,128},{8,136},{16,144},{24,152},{32,160},{40,168},{48,176},{56,1... | collective-permute-start | bytes 208904 | tf_op jit(solution)/shard_map/ppermute | solution.py:223
  78.5 5.7 %collective-permute-start.8 = (f32[272,128]{1,0:T(8,128)S(1)}, f32[272,128]{1,0:T(8,128)S(1)}, u32[]{:S(2)}, u32[]{:S(2)}) collective-permute-start(f32[272,128]{1,0:T(8,128)S(1)} %get-tuple-element.27.held_ref), channel_id=1, source_target_pairs={{0,8},{8,0},{16,24},{24,16},{32,40},{40,32},{48,56},{56,48},{64,72... | collective-permute-start | bytes 417800 | tf_op jit(solution)/shard_map/ppermute | solution.py:211
  84.2 13.8 %copy-start = (bf16[8,128,1024]{2,1,0:T(8,128)(2,1)}, bf16[8,128,1024]{2,1,0:T(8,128)(2,1)S(1)}, u32[]{:S(2)}) copy-start(bf16[8,128,1024]{2,1,0:T(8,128)(2,1)S(1)} %all-to-all-done) | copy-start | bytes 6291460
  87.8 0.8 copy-start.3
  88.6 21.4 %all-to-all-start.2 = ((bf16[64,16,128]{2,1,0:T(8,128)(2,1)}), bf16[64,16,128]{2,1,0:T(8,128)(2,1)S(1)}, u32[]{:S(2)}, u32[]{:S(2)}) async-start(bf16[64,16,128]{2,1,0:T(8,128)(2,1)} %get-tuple-element.33), calls=%async_computation.2 | async-start | bytes 524288 | tf_op jit(solution)/shard_map/all_to_all | solution.py:592
  111.7 16.4 %all-to-all-start.3 = ((f32[64,4,128]{2,1,0:T(4,128)}), f32[64,4,128]{2,1,0:T(4,128)S(1)}, u32[]{:S(2)}, u32[]{:S(2)}) async-start(f32[64,4,128]{2,1,0:T(4,128)} %get-tuple-element.35), calls=%async_computation.3 | async-start | bytes 262144 | tf_op jit(solution)/shard_map/all_to_all | solution.py:592
  117.7 10.4 %copy-start.2 = (bf16[8,128,256]{2,1,0:T(8,128)(2,1)S(1)}, bf16[8,128,256]{2,1,0:T(8,128)(2,1)}, u32[]{:S(2)}) copy-start(bf16[8,128,256]{2,1,0:T(8,128)(2,1)} %copy-done.1) | copy-start | bytes 1572868
  125.1 0.8 copy-start.4
